TPU v7x, 32 devices: a whole 2x2x4 slice. The times are simulated.
32 devices in a mesh: section: 4 (over y, x), dp: 8 (over z, core).
Axes of the slice: x: 2, y: 2, z: 4, core: 2. Of those that a mesh axis runs over, the one named last changes fastest.
Arguments:
- tokens: bfloat16 [4096, 768], P('dp'), may hold values from -6 to 6
- cotangent: bfloat16 [4, 4096, 768], P('section', 'dp'), may hold values from -6 to 6
- positions: float32 [32, 3, 128], P('dp'), may hold values from -6 to 6
- conformer_group: int32 [32], P('dp'), may hold values from 0 to 1, as said below
- atom_counts: int32 [16], P('dp'), may hold values from 32 to 128, as said below
- path_dist: int32 [16, 128, 128], P('dp'), may hold values from 0 to 63
- edge_kind: int32 [16, 128, 128], P('dp'), may hold values from 0 to 31
- attn_in: bfloat16 [4, 768, 2304], P('section'), may hold values from -0.21875 to 0.21875
- attn_out: bfloat16 [4, 768, 768], P('section'), may hold values from -0.625 to 0.625
- ffn_up: bfloat16 [4, 768, 768], P('section'), may hold values from -0.21875 to 0.21875
- ffn_down: bfloat16 [4, 768, 768], P('section'), may hold values from -0.21875 to 0.21875
- norm_gain: bfloat16 [4, 768, 2], P('section'), may hold values from 0.25 to 1.75
- norm_shift: bfloat16 [4, 768, 2], P('section'), may hold values from -2 to 2
- kernel_proj: bfloat16 [128, 32], replicated, may hold values from -1.5 to 1.5
- path_table: bfloat16 [64, 32], replicated, may hold values from -3 to 3
- edge_table: bfloat16 [32, 32], replicated, may hold values from -3 to 3
Outputs:
- hidden: bfloat16 [4, 4096, 768], P('section', 'dp')
- input_grads: bfloat16 [4, 4096, 768], P('section', 'dp')
- grad_attn_in: float32 [4, 768, 2304], P('section', 'dp')
- grad_attn_out: float32 [4, 768, 768], P('section', 'dp')
- grad_ffn_up: float32 [4, 768, 768], P('section', 'dp')
- grad_ffn_down: float32 [4, 768, 768], P('section', 'dp')
- grad_norm_gain: float32 [4, 768, 2], P('section', 'dp')
- grad_norm_shift: float32 [4, 768, 2], P('section', 'dp')
- grad_kernel_proj: float32 [128, 32], P('section')
- grad_path_table: float32 [64, 32], P('section')
- grad_edge_table: float32 [32, 32], P('section')
Inputs may be any that keep to these rules, and one draw needn't show every extreme that they name: `conformer_group`: values index the molecules of the same index of dp: each of its 2 molecules has exactly 2 conformers there. `atom_counts`: every index of dp holds a molecule with 128 atoms.
All inputs are finite; a program needn't handle non-finite values.
Results may differ from a plain program's by a relative error of at most 0.02.
Values may be sent and summed in bfloat16 or wider, within the bound.
A program may use at most 256 MiB of HBM per device.

v0:
```python
import math

import jax
import jax.numpy as jnp
from jax import lax
from jax.sharding import PartitionSpec as P

MICRO = 2
SEQ_MB = 2


EPS = 1e-05
NEG_BIG = -1e30
KERN_SPAN = 8.0
KERN_WIDTH = 0.4
HIGH = lax.Precision.HIGHEST


def shifted(value, axis, steps):
    count = lax.axis_size(axis)
    first, last = (max(0, -steps), min(count, count - steps))
    return lax.ppermute(value, axis, [(source, source + steps) for source in range(first, last)])


def gelu_tanh(values):
    return (
        0.5
        * values
        * (1.0 + jnp.tanh(0.7978845608028654 * (values + 0.044715 * values * values * values)))
    )


def kernels(positions, kernel_count):
    diffs = positions[:, :, :, None] - positions[:, :, None, :]
    dist = jnp.sqrt(jnp.sum(diffs * diffs, axis=1))
    centers = jnp.arange(kernel_count, dtype=jnp.float32) * (KERN_SPAN / kernel_count)
    scaled = (dist[:, None, :, :] - centers[None, :, None, None]) / KERN_WIDTH
    return jnp.exp(-0.5 * scaled * scaled)


def norm_fwd(values, gain, shift):
    center = values - jnp.mean(values, axis=-1, keepdims=True)
    inv_std = lax.rsqrt(jnp.mean(center * center, axis=-1, keepdims=True) + EPS)
    normal_x = center * inv_std
    return (normal_x * gain + shift, normal_x, inv_std)


def norm_back(grad_out, normal_x, inv_std, gain):
    scaled = grad_out * gain
    grad_in = inv_std * (
        scaled
        - jnp.mean(scaled, axis=-1, keepdims=True)
        - normal_x * jnp.mean(scaled * normal_x, axis=-1, keepdims=True)
    )
    return (grad_in, jnp.sum(grad_out * normal_x, axis=0), jnp.sum(grad_out, axis=0))


def left_dot(first, second):
    return lax.dot_general(
        first, second, (((0,), (0,)), ((), ())), preferred_element_type=jnp.float32
    )


def right_dot(first, second):
    return lax.dot_general(
        first, second, (((1,), (1,)), ((), ())), preferred_element_type=jnp.float32
    )


def make_bias(micro_data, tables):
    positions, path_blk, edge_blk, count_blk = micro_data
    kernel_proj, path_table, edge_table = tables
    feats_low = kernels(positions, kernel_proj.shape[0]).astype(jnp.bfloat16)
    bias = jnp.einsum("kh,skij->shij", kernel_proj, feats_low, preferred_element_type=jnp.float32)
    looked = jnp.take(path_table.astype(jnp.float32), path_blk, axis=0) + jnp.take(
        edge_table.astype(jnp.float32), edge_blk, axis=0
    )
    bias = bias + jnp.transpose(looked, (0, 3, 1, 2))
    return bias.astype(jnp.bfloat16)


def table_grads(grad_bias, micro_data, tables):
    positions, path_blk, edge_blk, count_blk = micro_data
    kernel_proj, path_table, edge_table = tables
    heads = kernel_proj.shape[1]
    feats_wide = kernels(positions, kernel_proj.shape[0]).astype(jnp.bfloat16).astype(jnp.float32)
    grad_kernel = jnp.einsum("shij,skij->kh", grad_bias, feats_wide, precision=HIGH)
    pair_rows = jnp.transpose(grad_bias, (0, 2, 3, 1)).reshape(-1, heads)
    grad_path = jax.ops.segment_sum(
        pair_rows, path_blk.reshape(-1), num_segments=path_table.shape[0]
    )
    grad_edge = jax.ops.segment_sum(
        pair_rows, edge_blk.reshape(-1), num_segments=edge_table.shape[0]
    )
    return (grad_kernel, grad_path, grad_edge)


def layer_forward(layer_in, params, bias_low, count_blk):
    attn_in, attn_out, ffn_up, ffn_down, norm_gain, norm_shift = params
    seq_count, heads, atom_slots = (bias_low.shape[0], bias_low.shape[1], bias_low.shape[2])
    width = attn_out.shape[0]
    head_dim = width // heads
    scale = 1.0 / math.sqrt(head_dim)
    shape_four = (seq_count, atom_slots, heads, head_dim)
    gains = norm_gain.astype(jnp.float32)
    shifts = norm_shift.astype(jnp.float32)
    in_wide = layer_in.astype(jnp.float32)
    normed, normal_one, inv_one = norm_fwd(in_wide, gains[:, 0], shifts[:, 0])
    normed_low = normed.astype(jnp.bfloat16)
    qkv_low = jnp.dot(normed_low, attn_in, preferred_element_type=jnp.float32).astype(jnp.bfloat16)
    queries = qkv_low[:, :width].reshape(shape_four)
    keys_all = qkv_low[:, width : 2 * width].reshape(shape_four)
    values_all = qkv_low[:, 2 * width :].reshape(shape_four)
    scores = (
        jnp.einsum("sihe,sjhe->shij", queries, keys_all, preferred_element_type=jnp.float32) * scale
    )
    scores = scores + bias_low.astype(jnp.float32)
    key_live = jnp.arange(atom_slots, dtype=jnp.int32)[None, :] < count_blk[:, None]
    scores = jnp.where(key_live[:, None, None, :], scores, NEG_BIG)
    probs = jax.nn.softmax(scores, axis=-1)
    probs_low = probs.astype(jnp.bfloat16)
    attended = jnp.einsum(
        "shij,sjhe->sihe", probs_low, values_all, preferred_element_type=jnp.float32
    )
    attended_low = attended.reshape(seq_count * atom_slots, width).astype(jnp.bfloat16)
    middle = in_wide + jnp.dot(attended_low, attn_out, preferred_element_type=jnp.float32)
    normed_two, normal_two, inv_two = norm_fwd(middle, gains[:, 1], shifts[:, 1])
    normed_two_low = normed_two.astype(jnp.bfloat16)
    upper = jnp.dot(normed_two_low, ffn_up, preferred_element_type=jnp.float32)
    act_low = gelu_tanh(upper).astype(jnp.bfloat16)
    layer_out = middle + jnp.dot(act_low, ffn_down, preferred_element_type=jnp.float32)
    saved = (
        normed_low,
        normal_one,
        inv_one,
        queries,
        keys_all,
        values_all,
        probs,
        probs_low,
        attended_low,
        normal_two,
        inv_two,
        normed_two_low,
        upper,
        act_low,
    )
    return (layer_out.astype(jnp.bfloat16), saved)


def ffn_back(grad_out, saved, params):
    attn_in, attn_out, ffn_up, ffn_down, norm_gain, norm_shift = params
    (
        normed_low,
        normal_one,
        inv_one,
        queries,
        keys_all,
        values_all,
        probs,
        probs_low,
        attended_low,
        normal_two,
        inv_two,
        normed_two_low,
        upper,
        act_low,
    ) = saved
    gains = norm_gain.astype(jnp.float32)
    grad_low = grad_out.astype(jnp.bfloat16)
    grad_down = left_dot(act_low, grad_low)
    grad_act = right_dot(grad_low, ffn_down)
    grad_upper = jax.vjp(gelu_tanh, upper)[1](grad_act)[0].astype(jnp.bfloat16)
    grad_up = left_dot(normed_two_low, grad_upper)
    grad_normed_two = right_dot(grad_upper, ffn_up)
    back_two, gain_two, shift_two = norm_back(grad_normed_two, normal_two, inv_two, gains[:, 1])
    return (grad_out + back_two, grad_up, grad_down, gain_two, shift_two)


def attn_back(grad_middle, saved, params):
    attn_in, attn_out, ffn_up, ffn_down, norm_gain, norm_shift = params
    (
        normed_low,
        normal_one,
        inv_one,
        queries,
        keys_all,
        values_all,
        probs,
        probs_low,
        attended_low,
        normal_two,
        inv_two,
        normed_two_low,
        upper,
        act_low,
    ) = saved
    seq_count, atom_slots, heads, head_dim = queries.shape
    width = heads * head_dim
    all_rows = seq_count * atom_slots
    scale = 1.0 / math.sqrt(head_dim)
    gains = norm_gain.astype(jnp.float32)
    middle_low = grad_middle.astype(jnp.bfloat16)
    grad_out_proj = left_dot(attended_low, middle_low)
    grad_attended = right_dot(middle_low, attn_out).astype(jnp.bfloat16).reshape(queries.shape)
    grad_probs = jnp.einsum(
        "sihe,sjhe->shij", grad_attended, values_all, preferred_element_type=jnp.float32
    )
    grad_values = jnp.einsum(
        "shij,sihe->sjhe", probs_low, grad_attended, preferred_element_type=jnp.float32
    )
    grad_scores = probs * (grad_probs - jnp.sum(probs * grad_probs, axis=-1, keepdims=True))
    scores_low = grad_scores.astype(jnp.bfloat16)
    grad_queries = (
        jnp.einsum("shij,sjhe->sihe", scores_low, keys_all, preferred_element_type=jnp.float32)
        * scale
    )
    grad_keys = (
        jnp.einsum("shij,sihe->sjhe", scores_low, queries, preferred_element_type=jnp.float32)
        * scale
    )
    grad_qkv = jnp.concatenate(
        [
            grad_queries.reshape(all_rows, width),
            grad_keys.reshape(all_rows, width),
            grad_values.reshape(all_rows, width),
        ],
        axis=1,
    ).astype(jnp.bfloat16)
    grad_in_proj = left_dot(normed_low, grad_qkv)
    grad_normed = right_dot(grad_qkv, attn_in)
    back_one, gain_one, shift_one = norm_back(grad_normed, normal_one, inv_one, gains[:, 0])
    grad_layer_in = (grad_middle + back_one).astype(jnp.bfloat16)
    return (grad_layer_in, grad_in_proj, grad_out_proj, gain_one, shift_one, scores_low)


def pick_micro(stored, micro_idx):
    return lax.dynamic_index_in_dim(stored, micro_idx, 0, keepdims=False)


def keep_micro(stored, value, micro_idx, live):
    kept = jnp.where(live, value, pick_micro(stored, micro_idx))
    return lax.dynamic_update_index_in_dim(stored, kept, micro_idx, 0)


def on_device(
    tokens,
    cotangent,
    positions,
    conformer_group,
    atom_counts,
    path_dist,
    edge_kind,
    attn_in,
    attn_out,
    ffn_up,
    ffn_down,
    norm_gain,
    norm_shift,
    kernel_proj,
    path_table,
    edge_table,
):
    sections = lax.axis_size("section")
    section_num = lax.axis_index("section")
    params = (attn_in[0], attn_out[0], ffn_up[0], ffn_down[0], norm_gain[0], norm_shift[0])
    tables = (kernel_proj, path_table, edge_table)
    atom_slots = positions.shape[2]
    width = attn_out.shape[1]
    heads = kernel_proj.shape[1]
    micro_rows = SEQ_MB * atom_slots
    ticks = MICRO + sections - 1
    path_seq = jnp.take(path_dist, conformer_group, axis=0)
    edge_seq = jnp.take(edge_kind, conformer_group, axis=0)
    count_seq = jnp.take(atom_counts, conformer_group, axis=0)
    cot_micro = cotangent[0].reshape(MICRO, micro_rows, width)
    bias_shape = (SEQ_MB, heads, atom_slots, atom_slots)

    def micro_slice(micro_idx):
        seq_start = micro_idx * SEQ_MB
        return tuple(
            (
                lax.dynamic_slice_in_dim(arr, seq_start, SEQ_MB, 0)
                for arr in (positions, path_seq, edge_seq, count_seq)
            )
        )

    incoming = jnp.zeros((micro_rows, width), jnp.bfloat16)
    bias_incoming = jnp.zeros(bias_shape, jnp.bfloat16)
    bias_store = jnp.zeros((MICRO,) + bias_shape, jnp.bfloat16)
    input_store = jnp.zeros((MICRO, micro_rows, width), jnp.bfloat16)
    output_store = jnp.zeros((MICRO, micro_rows, width), jnp.bfloat16)
    for tick_num in range(ticks):
        micro_num = tick_num - section_num
        live = (micro_num >= 0) & (micro_num < MICRO)
        micro_idx = jnp.clip(micro_num, 0, MICRO - 1)
        if tick_num < MICRO:
            first_in = tokens[tick_num * micro_rows : (tick_num + 1) * micro_rows]
        else:
            first_in = jnp.zeros((micro_rows, width), jnp.bfloat16)
        layer_in = jnp.where(section_num == 0, first_in, incoming)
        micro_data = micro_slice(micro_idx)
        bias_used = lax.cond(
            section_num == 0, lambda: make_bias(micro_data, tables), lambda: bias_incoming
        )
        layer_out = lax.cond(
            live,
            lambda: layer_forward(layer_in, params, bias_used, micro_data[3])[0],
            lambda: jnp.zeros((micro_rows, width), jnp.bfloat16),
        )
        bias_store = keep_micro(bias_store, bias_used, micro_idx, live)
        if tick_num < ticks - 1:
            incoming, bias_incoming = shifted((layer_out, bias_used), "section", 1)
        input_store = keep_micro(input_store, layer_in, micro_idx, live)
        output_store = keep_micro(output_store, layer_out, micro_idx, live)
    grad_incoming = jnp.zeros((micro_rows, width), jnp.bfloat16)
    bias_grad_in = jnp.zeros(bias_shape, jnp.float32)
    grad_store = jnp.zeros((MICRO, micro_rows, width), jnp.bfloat16)
    totals = tuple((jnp.zeros(arr.shape, jnp.float32) for arr in params[:4])) + tuple(
        (jnp.zeros((width,), jnp.float32) for unused in range(4))
    )
    table_tot = tuple((jnp.zeros(arr.shape, jnp.float32) for arr in tables))
    for tick_num in range(ticks):
        micro_num = tick_num - (sections - 1 - section_num)
        live = (micro_num >= 0) & (micro_num < MICRO)
        micro_idx = jnp.clip(micro_num, 0, MICRO - 1)
        grad_total = pick_micro(cot_micro, micro_idx).astype(jnp.float32) + grad_incoming.astype(
            jnp.float32
        )
        layer_in = pick_micro(input_store, micro_idx)
        micro_data = micro_slice(micro_idx)
        kept_bias = pick_micro(bias_store, micro_idx)
        grad_from_later = bias_grad_in

        def ffn_section():
            saved = layer_forward(layer_in, params, kept_bias, micro_data[3])[1]
            return (saved, ffn_back(grad_total, saved, params))

        def add_ffn(tot, ffn_part):
            grad_middle, grad_up, grad_down, gain_two, shift_two = ffn_part
            return (
                tot[0],
                tot[1],
                tot[2] + grad_up,
                tot[3] + grad_down,
                tot[4],
                tot[5] + gain_two,
                tot[6],
                tot[7] + shift_two,
            )

        def attn_step(tot, tabs, saved, grad_middle):
            grad_in, grad_in_proj, grad_out_proj, gain_one, shift_one, scores_low = attn_back(
                grad_middle, saved, params
            )
            tot = (
                tot[0] + grad_in_proj,
                tot[1] + grad_out_proj,
                tot[2],
                tot[3],
                tot[4] + gain_one,
                tot[5],
                tot[6] + shift_one,
                tot[7],
            )
            bias_send = scores_low.astype(jnp.float32) + grad_from_later

            def table_add(old_tabs):
                parts = table_grads(bias_send, micro_data, tables)
                return tuple((old + new for old, new in zip(old_tabs, parts)))

            tabs = lax.cond(section_num == 0, table_add, lambda old_tabs: old_tabs, tabs)
            return (tot, tabs, grad_in, bias_send)

        def spare_step(tot, tabs):
            return (
                tot,
                tabs,
                jnp.zeros((micro_rows, width), jnp.bfloat16),
                jnp.zeros(bias_shape, jnp.float32),
            )

        def full_step(tot, tabs):
            saved, ffn_part = ffn_section()
            return attn_step(add_ffn(tot, ffn_part), tabs, saved, ffn_part[0])

        totals, table_tot, grad_in, bias_send = lax.cond(
            live, full_step, spare_step, totals, table_tot
        )
        grad_store = keep_micro(grad_store, grad_in, micro_idx, live)
        if tick_num < ticks - 1:
            grad_incoming, bias_grad_in = (
                shifted(grad_in, "section", -1),
                shifted(bias_send.astype(jnp.bfloat16), "section", -1).astype(bias_send.dtype),
            )
    total_in, total_out, total_up, total_down, gain_one_t, gain_two_t, shift_one_t, shift_two_t = (
        totals
    )
    gain_tot = jnp.stack([gain_one_t, gain_two_t], axis=1)
    shift_tot = jnp.stack([shift_one_t, shift_two_t], axis=1)
    sums_all = (
        lax.psum_scatter(total_in, "dp", scatter_dimension=0, tiled=True),
        lax.psum_scatter(total_out, "dp", scatter_dimension=0, tiled=True),
        lax.psum_scatter(total_up, "dp", scatter_dimension=0, tiled=True),
        lax.psum_scatter(total_down, "dp", scatter_dimension=0, tiled=True),
        lax.psum_scatter(gain_tot, "dp", scatter_dimension=0, tiled=True),
        lax.psum_scatter(shift_tot, "dp", scatter_dimension=0, tiled=True),
    )
    sum_in, sum_out, sum_up, sum_down, sum_gain, sum_shift = sums_all
    molecule_sums = lax.psum((table_tot[0], table_tot[1], table_tot[2]), "dp")
    table_sums = (
        lax.psum_scatter(molecule_sums[0], "section", scatter_dimension=0, tiled=True),
        lax.psum_scatter(molecule_sums[1], "section", scatter_dimension=0, tiled=True),
        lax.psum_scatter(molecule_sums[2], "section", scatter_dimension=0, tiled=True),
    )
    hidden = output_store.reshape(1, MICRO * micro_rows, width)
    input_grads = grad_store.reshape(1, MICRO * micro_rows, width)
    return (
        hidden,
        input_grads,
        sum_in[None],
        sum_out[None],
        sum_up[None],
        sum_down[None],
        sum_gain[None],
        sum_shift[None],
        table_sums[0],
        table_sums[1],
        table_sums[2],
    )


def solution(mesh):
    in_specs = (
        P("dp", None),
        P("section", "dp", None),
        P("dp", None, None),
        P("dp"),
        P("dp"),
        P("dp", None, None),
        P("dp", None, None),
        P("section", None, None),
        P("section", None, None),
        P("section", None, None),
        P("section", None, None),
        P("section", None, None),
        P("section", None, None),
        P(),
        P(),
        P(),
    )
    out_specs = (
        P("section", "dp", None),
        P("section", "dp", None),
        P("section", "dp", None),
        P("section", "dp", None),
        P("section", "dp", None),
        P("section", "dp", None),
        P("section", "dp", None),
        P("section", "dp", None),
        P("section", None),
        P("section", None),
        P("section", None),
    )
    return jax.shard_map(
        on_device, mesh=mesh, in_specs=in_specs, out_specs=out_specs, check_vma=False
    )
```

profile of v0, /device:TPU:0, one launch (start us, length us, event | category | flops | bytes accessed | tf_op | source)
XLA Modules:
  0.0 3120.1 jit_solution(12482083648939707846)
XLA Ops:
  12.6 248.8 %conditional.20 = (bf16[2,32,128,128]{3,1,2,0:T(8,128)(2,1)}) conditional(s32[]{:T(128)} %convert_element_type.1089, () %tuple.230, (f32[4,3,128]{2,0,1:T(4,128)}, s32[]{:T(128)}, bf16[128,32]{0,1:T(8,128)(2,1)}, bf16[64,32]{0,1:T(8,128)(2,1)}, s32[4,128,128]{2,1,0:T(8,128)S(1)}, /*index=5*/bf16[32,32]{1,0:T(8,128)(2,1)}, ...), branch_computations={%region_0.0_spmd, %region_1.6_spmd} | conditional | flops 295373952 | bytes 46137444 | solution.py:303
  13.5 108.2 %gather_fusion.1 = f32[32768,32]{1,0:T(8,128)} fusion(f32[32,32]{1,0:T(8,128)S(1)} %convert_element_type.854, s32[32768]{0:T(1024)S(1)} %broadcast_clamp_fusion), kind=kCustom, calls=%fused_computation.2.clone | custom fusion | bytes 8519680 | tf_op jit(solution)/shard_map/cond/branch_1_fun/jit(_take)/gather | solution.py:75
  121.7 11.4 copy.696
  133.2 108.2 %gather_fusion = f32[32768,32]{1,0:T(8,128)} fusion(f32[64,32]{1,0:T(8,128)S(1)} %convert_element_type.853, s32[32768]{0:T(1024)S(1)} %broadcast_clamp_fusion.1), kind=kCustom, calls=%fused_computation.1.clone | custom fusion | bytes 8519680 | tf_op jit(solution)/shard_map/cond/branch_1_fun/jit(_take)/gather | solution.py:75
  241.4 11.4 copy.694
  253.0 8.3 fusion.80
  264.0 44.8 %collective-permute-done.1 = bf16[2,32,128,128]{3,1,2,0:T(8,128)(2,1)} collective-permute-done((bf16[2,32,128,128]{3,1,2,0:T(8,128)(2,1)}, bf16[2,32,128,128]{3,1,2,0:T(8,128)(2,1)}, u32[]{:S(2)}, u32[]{:S(2)}) %collective-permute-start.1) | collective-permute-done | bytes 2097184 | tf_op jit(solution)/shard_map/ppermute | solution.py:22
  308.8 248.8 %conditional.22 = (bf16[2,32,128,128]{3,1,2,0:T(8,128)(2,1)}) conditional(s32[]{:T(128)} %convert_element_type.1089, bf16[2,32,128,128]{3,1,2,0:T(8,128)(2,1)} %collective-permute-done.1, (f32[4,3,128]{2,0,1:T(4,128)}, s32[]{:T(128)}, bf16[128,32]{0,1:T(8,128)(2,1)}, bf16[64,32]{0,1:T(8,128)(2,1)}, s32[4,128,128]{2,1,0:T(8,128)S(1)}, ...), branch_computations={%region_11.15_spmd, %region_12.17_spmd} | conditional | flops 295373952 | bytes 46137444 | solution.py:303
  309.6 108.2 %gather_fusion.3 = f32[32768,32]{1,0:T(8,128)} fusion(f32[32,32]{1,0:T(8,128)S(1)} %convert_element_type.872, s32[32768]{0:T(1024)S(1)} %broadcast_clamp_fusion.2), kind=kCustom, calls=%fused_computation.8.clone | custom fusion | bytes 8519680 | tf_op jit(solution)/shard_map/cond/branch_1_fun/jit(_take)/gather | solution.py:75
  417.8 11.4 copy.700
  429.3 108.2 %gather_fusion.2 = f32[32768,32]{1,0:T(8,128)} fusion(f32[64,32]{1,0:T(8,128)S(1)} %convert_element_type.871, s32[32768]{0:T(1024)S(1)} %broadcast_clamp_fusion.3), kind=kCustom, calls=%fused_computation.4.clone | custom fusion | bytes 8519680 | tf_op jit(solution)/shard_map/cond/branch_1_fun/jit(_take)/gather | solution.py:75
  537.5 11.4 copy.698
  549.2 8.4 fusion.95
  562.1 37.3 %conditional.21 = (bf16[256,768]{1,0:T(8,128)(2,1)}) conditional(s32[]{:T(128)} %convert_element_type.1088, () %tuple.229, (bf16[256,768]{1,0:T(8,128)(2,1)}, bf16[768,2]{0,1:T(2,128)(2,1)S(1)}, bf16[768,2]{0,1:T(2,128)(2,1)S(1)}, bf16[768,2304]{1,0:T(8,128)(2,1)}, s32[4]{0:T(128)S(1)}, /*index=5*/s32[]{:T(128)}, ...), branch_computations={%region_3.7_spmd, %region_4.14_spmd} | conditional | flops 1928466304 | bytes 41951836 | solution.py:306
  609.7 272.8 %conditional.24 = (bf16[2,32,128,128]{3,1,2,0:T(8,128)(2,1)}) conditional(s32[]{:T(128)} %convert_element_type.1089, bf16[2,32,128,128]{3,1,2,0:T(8,128)(2,1)} %collective-permute-done.3, (f32[4,3,128]{2,0,1:T(4,128)S(1)}, s32[]{:T(128)}, bf16[128,32]{0,1:T(8,128)(2,1)S(1)}, bf16[64,32]{0,1:T(8,128)(2,1)S(1)}, s32[4,128,128]{2,1,0:T(8,128)}, ...), branch_computations={%region_22.26_spmd, %region_23.28_spmd} | conditional | flops 295373952 | bytes 46194732 | solution.py:303
  612.1 118.7 %gather_fusion.5 = f32[32768,32]{1,0:T(8,128)} fusion(f32[32,32]{1,0:T(8,128)S(1)} %convert_element_type.890, s32[32768]{0:T(1024)} %broadcast_clamp_fusion.4), kind=kCustom, calls=%fused_computation.9.clone | custom fusion | bytes 8519680 | tf_op jit(solution)/shard_map/cond/branch_1_fun/jit(_take)/gather | solution.py:75
  730.8 11.4 copy.704
  743.8 118.7 %gather_fusion.4 = f32[32768,32]{1,0:T(8,128)} fusion(f32[64,32]{1,0:T(8,128)S(1)} %convert_element_type.889, s32[32768]{0:T(1024)} %broadcast_clamp_fusion.5), kind=kCustom, calls=%fused_computation.5.clone | custom fusion | bytes 8519680 | tf_op jit(solution)/shard_map/cond/branch_1_fun/jit(_take)/gather | solution.py:75
  862.5 11.4 copy.702
  874.2 8.4 fusion.110
  895.6 37.1 %conditional.23 = (bf16[256,768]{1,0:T(8,128)(2,1)}) conditional(s32[]{:T(128)} %convert_element_type.1090, () %tuple.233, (bf16[256,768]{1,0:T(8,128)(2,1)}, bf16[768,2]{0,1:T(2,128)(2,1)S(1)}, bf16[768,2]{0,1:T(2,128)(2,1)S(1)}, bf16[768,2304]{1,0:T(8,128)(2,1)}, s32[4]{0:T(128)S(1)}, /*index=5*/s32[]{:T(128)}, ...), branch_computations={%region_14.18_spmd, %region_15.25_spmd} | conditional | flops 1928466304 | bytes 41951836 | solution.py:306
  950.2 41.4 %collective-permute-start.4 = (bf16[256,768]{1,0:T(8,128)(2,1)}, bf16[256,768]{1,0:T(8,128)(2,1)}, u32[]{:S(2)}, u32[]{:S(2)}) collective-permute-start(bf16[256,768]{1,0:T(8,128)(2,1)} %get-tuple-element.4033), channel_id=1, source_target_pairs={{0,8},{8,16},{16,24},{1,9},{9,17},{17,25},{2,10},{10,18},{18,26},{... | collective-permute-start | bytes 1179656 | tf_op jit(solution)/shard_map/ppermute | solution.py:22
  991.6 272.7 %conditional.26 = (bf16[2,32,128,128]{3,1,2,0:T(8,128)(2,1)}) conditional(s32[]{:T(128)} %convert_element_type.1089, bf16[2,32,128,128]{3,1,2,0:T(8,128)(2,1)} %collective-permute-done.5, (f32[4,3,128]{2,0,1:T(4,128)S(1)}, s32[]{:T(128)}, bf16[128,32]{0,1:T(8,128)(2,1)S(1)}, bf16[64,32]{0,1:T(8,128)(2,1)S(1)}, s32[4,128,128]{2,1,0:T(8,128)}, ...), branch_computations={%region_33.37_spmd, %region_34.39_spmd} | conditional | flops 295373952 | bytes 46194732 | solution.py:303
  993.9 118.7 %gather_fusion.7 = f32[32768,32]{1,0:T(8,128)} fusion(f32[32,32]{1,0:T(8,128)S(1)} %convert_element_type.908, s32[32768]{0:T(1024)} %broadcast_clamp_fusion.6), kind=kCustom, calls=%fused_computation.10.clone | custom fusion | bytes 8519680 | tf_op jit(solution)/shard_map/cond/branch_1_fun/jit(_take)/gather | solution.py:75
  1112.6 11.4 copy.708
  1125.7 118.7 %gather_fusion.6 = f32[32768,32]{1,0:T(8,128)} fusion(f32[64,32]{1,0:T(8,128)S(1)} %convert_element_type.907, s32[32768]{0:T(1024)} %broadcast_clamp_fusion.7), kind=kCustom, calls=%fused_computation.6.clone | custom fusion | bytes 8519680 | tf_op jit(solution)/shard_map/cond/branch_1_fun/jit(_take)/gather | solution.py:75
  1244.4 11.4 copy.706
  1256.0 8.3 fusion.125
  1291.3 27.6 collective-permute-done.6
  1319.8 248.4 %conditional.28 = (bf16[2,32,128,128]{3,1,2,0:T(8,128)(2,1)}) conditional(s32[]{:T(128)} %convert_element_type.1089, bf16[2,32,128,128]{3,1,2,0:T(8,128)(2,1)} %collective-permute-done.7, (f32[4,3,128]{2,0,1:T(4,128)S(1)}, s32[]{:T(128)}, bf16[128,32]{0,1:T(8,128)(2,1)S(1)}, bf16[64,32]{0,1:T(8,128)(2,1)S(1)}, s32[4,128,128]{2,1,0:T(8,128)S(1)}, ...), branch_computations={%region_44.48_spmd, %region_45.50_spmd} | conditional | flops 295373952 | bytes 46063632 | solution.py:303
  1320.4 108.2 %gather_fusion.9 = f32[32768,32]{1,0:T(8,128)} fusion(f32[32,32]{1,0:T(8,128)S(1)} %convert_element_type.926, s32[32768]{0:T(1024)S(1)} %broadcast_clamp_fusion.8), kind=kCustom, calls=%fused_computation.11.clone | custom fusion | bytes 8519680 | tf_op jit(solution)/shard_map/cond/branch_1_fun/jit(_take)/gather | solution.py:75
  1428.6 11.4 copy.712
  1440.1 108.2 %gather_fusion.8 = f32[32768,32]{1,0:T(8,128)} fusion(f32[64,32]{1,0:T(8,128)S(1)} %convert_element_type.925, s32[32768]{0:T(1024)S(1)} %broadcast_clamp_fusion.9), kind=kCustom, calls=%fused_computation.7.clone | custom fusion | bytes 8519680 | tf_op jit(solution)/shard_map/cond/branch_1_fun/jit(_take)/gather | solution.py:75
  1548.3 11.4 copy.710
  1559.9 8.3 fusion.140
  1576.9 25.1 conditional.30
  1608.8 54.0 %collective-permute-done.8 = bf16[256,768]{1,0:T(8,128)(2,1)} collective-permute-done((bf16[256,768]{1,0:T(8,128)(2,1)}, bf16[256,768]{1,0:T(8,128)(2,1)}, u32[]{:S(2)}, u32[]{:S(2)}) %collective-permute-start.8) | collective-permute-done | bytes 393248 | tf_op jit(solution)/shard_map/ppermute | solution.py:22
  1668.0 12.6 conditional.31
  1687.3 53.0 %collective-permute-done.10 = bf16[256,768]{1,0:T(8,128)(2,1)} collective-permute-done((bf16[256,768]{1,0:T(8,128)(2,1)}, bf16[256,768]{1,0:T(8,128)(2,1)}, u32[]{:S(2)}, u32[]{:S(2)}) %collective-permute-start.10) | collective-permute-done | bytes 393248 | tf_op jit(solution)/shard_map/ppermute | solution.py:22
  1745.6 12.9 conditional.32
  1765.2 151.5 %collective-permute-done.12 = bf16[256,768]{1,0:T(8,128)(2,1)} collective-permute-done((bf16[256,768]{1,0:T(8,128)(2,1)}, bf16[256,768]{1,0:T(8,128)(2,1)}, u32[]{:S(2)}, u32[]{:S(2)}) %collective-permute-start.12) | collective-permute-done | bytes 393248 | tf_op jit(solution)/shard_map/ppermute | solution.py:22
  1921.9 427.4 %conditional.33 = (f32[768,2304]{1,0:T(8,128)}, f32[768,768]{1,0:T(8,128)}, f32[768,768]{1,0:T(8,128)}, f32[768,768]{1,0:T(8,128)}, f32[768]{0:T(1024)}, /*index...) conditional(s32[]{:T(128)} %convert_element_type.1103, ...), branch_computations={%region_121.125_spmd, %region_122.146_spmd} | conditional | flops 7117012992 | bytes 281617248 | solution.py:387
  1969.9 7.3 convolution_add_fusion.21
  1996.7 348.9 %conditional.3 = ((f32[128,32]{0,1:T(8,128)}, f32[64,32]{1,0:T(8,128)}, f32[32,32]{1,0:T(8,128)})) conditional(s32[]{:T(128)} %convert_element_type.1037, (f32[128,32]{0,1:T(8,128)}, f32[64,32]{1,0:T(8,128)}, f32[32,32]{1,0:T(8,128)}) %tuple.193, (f32[4,3,128]{2,0,1:T(4,128)S(1)}, s32[]{:T(128)}, f32[2,32,128,128]{2,3,1,0:T(8,128)}, ...), branch_computations={%region_136.139_spmd, %region_137.143_spmd} | conditional | flops 1633947776 | bytes 49862752 | solution.py:372
  2002.7 12.2 fusion.48
  2015.6 14.5 copy.648
  2030.1 157.8 %scatter_fusion.6 = f32[64,32]{1,0:T(8,128)} fusion(f32[64,32]{1,0:T(8,128)} %get-tuple-element.2359, s32[32768]{0:T(1024)} %bitcast.990, f32[32768,32]{1,0:T(8,128)} %bitcast.912), kind=kCustom, calls=%fused_computation.19 | custom fusion | flops 1048576 | bytes 12713984 | tf_op jit(solution)/shard_map/cond/branch_1_fun/cond/branch_1_fun/scatter-add | solution.py:89
  2187.9 157.8 %scatter_fusion.7 = f32[32,32]{1,0:T(8,128)} fusion(f32[32,32]{1,0:T(8,128)} %get-tuple-element.2361, s32[32768]{0:T(1024)} %bitcast.987, f32[32768,32]{1,0:T(8,128)} %bitcast.913), kind=kCustom, calls=%fused_computation.20 | custom fusion | flops 1048576 | bytes 12713984 | tf_op jit(solution)/shard_map/cond/branch_1_fun/cond/branch_1_fun/scatter-add | solution.py:92
  2357.2 51.5 %collective-permute-done.14 = bf16[256,768]{1,0:T(8,128)(2,1)} collective-permute-done((bf16[256,768]{1,0:T(8,128)(2,1)}, bf16[256,768]{1,0:T(8,128)(2,1)}, u32[]{:S(2)}, u32[]{:S(2)}) %collective-permute-start.14) | collective-permute-done | bytes 393248 | tf_op jit(solution)/shard_map/ppermute | solution.py:22
  2414.0 418.2 %conditional.34 = (f32[768,2304]{1,0:T(8,128)}, f32[768,768]{1,0:T(8,128)}, f32[768,768]{1,0:T(8,128)}, f32[768,768]{1,0:T(8,128)}, f32[768]{0:T(1024)}, /*index...) conditional(s32[]{:T(128)} %convert_element_type.1107, ...), branch_computations={%region_143.147_spmd, %region_144.168_spmd} | conditional | flops 7118061568 | bytes 315724800 | solution.py:387
  2453.1 7.3 convolution_add_fusion.26
  2479.9 348.7 %conditional.4 = ((f32[128,32]{0,1:T(8,128)}, f32[64,32]{1,0:T(8,128)}, f32[32,32]{1,0:T(8,128)})) conditional(s32[]{:T(128)} %convert_element_type.1062, (f32[128,32]{0,1:T(8,128)}, f32[64,32]{1,0:T(8,128)}, f32[32,32]{1,0:T(8,128)}) %tuple.198, (f32[4,3,128]{2,0,1:T(4,128)S(1)}, s32[]{:T(128)}, f32[2,32,128,128]{2,3,1,0:T(8,128)}, ...), branch_computations={%region_158.161_spmd, %region_159.165_spmd} | conditional | flops 1636044928 | bytes 98097248 | solution.py:372
  2485.9 13.7 fusion.64
  2502.6 10.3 copy.671
  2512.9 157.9 %scatter_fusion = f32[64,32]{1,0:T(8,128)} fusion(f32[64,32]{1,0:T(8,128)} %get-tuple-element.2410, s32[32768]{0:T(1024)S(1)} %bitcast.984, f32[32768,32]{1,0:T(8,128)} %bitcast.906), kind=kCustom, calls=%fused_computation.21 | custom fusion | flops 1048576 | bytes 12713984 | tf_op jit(solution)/shard_map/cond/branch_1_fun/cond/branch_1_fun/scatter-add | solution.py:89
  2670.8 157.8 %scatter_fusion.1 = f32[32,32]{1,0:T(8,128)} fusion(f32[32,32]{1,0:T(8,128)} %get-tuple-element.2412, s32[32768]{0:T(1024)S(1)} %bitcast.983, f32[32768,32]{1,0:T(8,128)} %bitcast.907), kind=kCustom, calls=%fused_computation.22 | custom fusion | flops 1048576 | bytes 12713984 | tf_op jit(solution)/shard_map/cond/branch_1_fun/cond/branch_1_fun/scatter-add | solution.py:92
  2846.9 14.9 all-reduce.3
  2864.4 28.4 reduce-scatter.24.cloned.1.call-done
  2894.3 23.2 reduce-scatter.20.cloned.1.call-done
  2917.5 29.1 all-reduce.2
  2946.6 10.2 reduce-scatter.14.cloned.1.call-done
  2956.8 38.5 %reduce-scatter.16.cloned.1.call-done = f32[96,768]{1,0:T(8,128)} async-done(((f32[768,768]{1,0:T(8,128)}), f32[96,768]{1,0:T(8,128)}) %reduce-scatter.16.cloned.1.call-update) | async-done | bytes 294928 | tf_op jit(solution)/shard_map/reduce_scatter | solution.py:404
  2995.3 38.5 %reduce-scatter.18.cloned.1.call-done = f32[96,768]{1,0:T(8,128)} async-done(((f32[768,768]{1,0:T(8,128)}), f32[96,768]{1,0:T(8,128)}) %reduce-scatter.18.cloned.1.call-update) | async-done | bytes 294928 | tf_op jit(solution)/shard_map/reduce_scatter | solution.py:405
  3033.8 79.2 %reduce-scatter.12.cloned.1.call-done = f32[96,2304]{1,0:T(8,128)} async-done(((f32[768,2304]{1,0:T(8,128)}), f32[96,2304]{1,0:T(8,128)}) %reduce-scatter.12.cloned.1.call-update) | async-done | bytes 884752 | tf_op jit(solution)/shard_map/reduce_scatter | solution.py:402
  (684 shorter events, 412.4 us)
Async XLA Ops:
  7.2 2855.7 %reduce-scatter.22.cloned.1.call-start = ((), (), s32[]{:S(2)}) async-start(), calls=%async_computation.12 | async-start | bytes 442368
  12.6 296.2 %copy-start.45 = (s32[4,128,128]{2,1,0:T(8,128)}, s32[4,128,128]{2,1,0:T(8,128)S(1)}, u32[]{:S(2)}) copy-start(s32[4,128,128]{2,1,0:T(8,128)S(1)} %get-tuple-element.3863) | copy-start | bytes 786436
  12.6 1564.3 %copy-start.38 = (s32[4,128,128]{2,1,0:T(8,128)}, s32[4,128,128]{2,1,0:T(8,128)S(1)}, u32[]{:S(2)}) copy-start(s32[4,128,128]{2,1,0:T(8,128)S(1)} %get-tuple-element.3862) | copy-start | bytes 786436
  261.4 47.4 %collective-permute-start.1 = (bf16[2,32,128,128]{3,1,2,0:T(8,128)(2,1)}, bf16[2,32,128,128]{3,1,2,0:T(8,128)(2,1)}, u32[]{:S(2)}, u32[]{:S(2)}) collective-permute-start(bf16[2,32,128,128]{3,1,2,0:T(8,128)(2,1)} %get-tuple-element.4028), channel_id=1, source_target_pairs={{0,8},{8,16},{16,24},{1,9},{9,17},{17,25},{2,10},{10,18},{18,26},{... | collective-permute-start | bytes 6291464 | tf_op jit(solution)/shard_map/ppermute | solution.py:22
  264.0 298.1 %copy-start.2 = (bf16[1,768,768]{2,1,0:T(8,128)(2,1)S(1)}, bf16[1,768,768]{2,1,0:T(8,128)(2,1)}, u32[]{:S(2)}) copy-start(bf16[1,768,768]{2,1,0:T(8,128)(2,1)} %param.70) | copy-start | bytes 3538948
  264.0 298.1 %copy-start.7 = (bf16[1,768,768]{2,1,0:T(8,128)(2,1)S(1)}, bf16[1,768,768]{2,1,0:T(8,128)(2,1)}, u32[]{:S(2)}) copy-start(bf16[1,768,768]{2,1,0:T(8,128)(2,1)} %param.72) | copy-start | bytes 3538948
  264.0 298.1 %copy-start.169 = (bf16[1,768,2]{1,2,0:T(2,128)(2,1)S(1)}, bf16[1,768,2]{1,2,0:T(2,128)(2,1)}, u32[]{:S(2)}) copy-start(bf16[1,768,2]{1,2,0:T(2,128)(2,1)} %param.73) | copy-start | bytes 9220
  264.0 298.1 %copy-start.174 = (bf16[1,768,2]{1,2,0:T(2,128)(2,1)S(1)}, bf16[1,768,2]{1,2,0:T(2,128)(2,1)}, u32[]{:S(2)}) copy-start(bf16[1,768,2]{1,2,0:T(2,128)(2,1)} %param.74) | copy-start | bytes 9220
  264.0 298.1 %copy-start.262 = (s32[4]{0:T(128)S(1)}, s32[4]{0:T(128)}, u32[]{:S(2)}) copy-start(s32[4]{0:T(128)} %get-tuple-element.3714) | copy-start | bytes 52
  557.5 52.2 %collective-permute-start.3 = (bf16[2,32,128,128]{3,1,2,0:T(8,128)(2,1)}, bf16[2,32,128,128]{3,1,2,0:T(8,128)(2,1)}, u32[]{:S(2)}, u32[]{:S(2)}) collective-permute-start(bf16[2,32,128,128]{3,1,2,0:T(8,128)(2,1)} %get-tuple-element.4030), channel_id=1, source_target_pairs={{0,8},{8,16},{16,24},{1,9},{9,17},{17,25},{2,10},{10,18},{18,26},{... | collective-permute-start | bytes 6291464 | tf_op jit(solution)/shard_map/ppermute | solution.py:22
  599.4 289.7 %collective-permute-start = (bf16[256,768]{1,0:T(8,128)(2,1)}, bf16[256,768]{1,0:T(8,128)(2,1)}, u32[]{:S(2)}, u32[]{:S(2)}) collective-permute-start(bf16[256,768]{1,0:T(8,128)(2,1)} %get-tuple-element.4029), channel_id=1, source_target_pairs={{0,8},{8,16},{16,24},{1,9},{9,17},{17,25},{2,10},{10,18},{18,26},{... | collective-permute-start | bytes 1179656 | tf_op jit(solution)/shard_map/ppermute | solution.py:22
  882.5 109.1 %collective-permute-start.5 = (bf16[2,32,128,128]{3,1,2,0:T(8,128)(2,1)}, bf16[2,32,128,128]{3,1,2,0:T(8,128)(2,1)}, u32[]{:S(2)}, u32[]{:S(2)}) collective-permute-start(bf16[2,32,128,128]{3,1,2,0:T(8,128)(2,1)} %get-tuple-element.4032), channel_id=1, source_target_pairs={{0,8},{8,16},{16,24},{1,9},{9,17},{17,25},{2,10},{10,18},{18,26},{... | collective-permute-start | bytes 6291464 | tf_op jit(solution)/shard_map/ppermute | solution.py:22
  932.7 10.4 collective-permute-start.2
  950.2 325.2 %collective-permute-start.4 = (bf16[256,768]{1,0:T(8,128)(2,1)}, bf16[256,768]{1,0:T(8,128)(2,1)}, u32[]{:S(2)}, u32[]{:S(2)}) collective-permute-start(bf16[256,768]{1,0:T(8,128)(2,1)} %get-tuple-element.4033), channel_id=1, source_target_pairs={{0,8},{8,16},{16,24},{1,9},{9,17},{17,25},{2,10},{10,18},{18,26},{... | collective-permute-start | bytes 1179656 | tf_op jit(solution)/shard_map/ppermute | solution.py:22
  1264.4 55.5 %collective-permute-start.7 = (bf16[2,32,128,128]{3,1,2,0:T(8,128)(2,1)}, bf16[2,32,128,128]{3,1,2,0:T(8,128)(2,1)}, u32[]{:S(2)}, u32[]{:S(2)}) collective-permute-start(bf16[2,32,128,128]{3,1,2,0:T(8,128)(2,1)} %get-tuple-element.4034), channel_id=1, source_target_pairs={{0,8},{8,16},{16,24},{1,9},{9,17},{17,25},{2,10},{10,18},{18,26},{... | collective-permute-start | bytes 6291464 | tf_op jit(solution)/shard_map/ppermute | solution.py:22
  1281.7 37.2 %collective-permute-start.6 = (bf16[256,768]{1,0:T(8,128)(2,1)}, bf16[256,768]{1,0:T(8,128)(2,1)S(1)}, u32[]{:S(2)}, u32[]{:S(2)}) collective-permute-start(bf16[256,768]{1,0:T(8,128)(2,1)} %get-tuple-element.4035), channel_id=1, source_target_pairs={{0,8},{8,16},{16,24},{1,9},{9,17},{17,25},{2,10},{10,18},{18,26},{... | collective-permute-start | bytes 1179656 | tf_op jit(solution)/shard_map/ppermute | solution.py:22
  1287.2 32.7 %copy-start.46 = (s32[4,128,128]{2,1,0:T(8,128)S(1)}, s32[4,128,128]{2,1,0:T(8,128)}, u32[]{:S(2)}) copy-start(s32[4,128,128]{2,1,0:T(8,128)} %copy-done.45) | copy-start | bytes 786436
  1287.3 32.5 %copy-start.68 = (bf16[2,256,768]{2,1,0:T(8,128)(2,1)}, bf16[2,256,768]{2,1,0:T(8,128)(2,1)S(1)}, u32[]{:S(2)}) copy-start(bf16[2,256,768]{2,1,0:T(8,128)(2,1)S(1)} %bitcast_dynamic-update-slice_fusion.31) | copy-start | bytes 2359300
  1606.0 61.9 %copy-start.170 = (bf16[1,768,2]{1,2,0:T(2,128)(2,1)S(1)}, bf16[1,768,2]{1,2,0:T(2,128)(2,1)}, u32[]{:S(2)}) copy-start(bf16[1,768,2]{1,2,0:T(2,128)(2,1)} %param.73) | copy-start | bytes 9220
  1606.0 61.9 %copy-start.175 = (bf16[1,768,2]{1,2,0:T(2,128)(2,1)S(1)}, bf16[1,768,2]{1,2,0:T(2,128)(2,1)}, u32[]{:S(2)}) copy-start(bf16[1,768,2]{1,2,0:T(2,128)(2,1)} %param.74) | copy-start | bytes 9220
  1606.0 61.9 %copy-start.264 = (s32[4]{0:T(128)S(1)}, s32[4]{0:T(128)}, u32[]{:S(2)}) copy-start(s32[4]{0:T(128)} %get-tuple-element.3714) | copy-start | bytes 52
  1606.0 57.8 %collective-permute-start.9 = (bf16[2,32,128,128]{2,3,1,0:T(8,128)(2,1)}, bf16[2,32,128,128]{2,3,1,0:T(8,128)(2,1)}, u32[]{:S(2)}, u32[]{:S(2)}) collective-permute-start(bf16[2,32,128,128]{2,3,1,0:T(8,128)(2,1)} %convert_element_type.1097), channel_id=1, source_target_pairs={{8,0},{16,8},{24,16},{9,1},{17,9},{25,17},{10,2},{18,10},{26,18},{... | collective-permute-start | bytes 6291464 | tf_op jit(solution)/shard_map/ppermute | solution.py:22
  1607.5 55.3 %collective-permute-start.8 = (bf16[256,768]{1,0:T(8,128)(2,1)}, bf16[256,768]{1,0:T(8,128)(2,1)}, u32[]{:S(2)}, u32[]{:S(2)}) collective-permute-start(bf16[256,768]{1,0:T(8,128)(2,1)} %get-tuple-element.2520), channel_id=1, source_target_pairs={{8,0},{16,8},{24,16},{9,1},{17,9},{25,17},{10,2},{18,10},{26,18},{... | collective-permute-start | bytes 1179656 | tf_op jit(solution)/shard_map/ppermute | solution.py:22
  1684.5 61.0 %copy-start.171 = (bf16[1,768,2]{1,2,0:T(2,128)(2,1)S(1)}, bf16[1,768,2]{1,2,0:T(2,128)(2,1)}, u32[]{:S(2)}) copy-start(bf16[1,768,2]{1,2,0:T(2,128)(2,1)} %param.73) | copy-start | bytes 9220
  1684.5 61.0 %copy-start.176 = (bf16[1,768,2]{1,2,0:T(2,128)(2,1)S(1)}, bf16[1,768,2]{1,2,0:T(2,128)(2,1)}, u32[]{:S(2)}) copy-start(bf16[1,768,2]{1,2,0:T(2,128)(2,1)} %param.74) | copy-start | bytes 9220
  1684.6 61.0 %copy-start.265 = (s32[4]{0:T(128)S(1)}, s32[4]{0:T(128)}, u32[]{:S(2)}) copy-start(s32[4]{0:T(128)} %get-tuple-element.3714) | copy-start | bytes 52
  1684.6 56.8 %collective-permute-start.11 = (bf16[2,32,128,128]{2,3,1,0:T(8,128)(2,1)}, bf16[2,32,128,128]{2,3,1,0:T(8,128)(2,1)}, u32[]{:S(2)}, u32[]{:S(2)}) collective-permute-start(bf16[2,32,128,128]{2,3,1,0:T(8,128)(2,1)} %convert_element_type.1101), channel_id=1, source_target_pairs={{8,0},{16,8},{24,16},{9,1},{17,9},{25,17},{10,2},{18,10},{26,18},{... | collective-permute-start | bytes 6291464 | tf_op jit(solution)/shard_map/ppermute | solution.py:22
  1686.0 54.4 %collective-permute-start.10 = (bf16[256,768]{1,0:T(8,128)(2,1)}, bf16[256,768]{1,0:T(8,128)(2,1)}, u32[]{:S(2)}, u32[]{:S(2)}) collective-permute-start(bf16[256,768]{1,0:T(8,128)(2,1)} %get-tuple-element.2533), channel_id=1, source_target_pairs={{8,0},{16,8},{24,16},{9,1},{17,9},{25,17},{10,2},{18,10},{26,18},{... | collective-permute-start | bytes 1179656 | tf_op jit(solution)/shard_map/ppermute | solution.py:22
  1762.4 159.5 %copy-start.172 = (bf16[1,768,2]{1,2,0:T(2,128)(2,1)S(1)}, bf16[1,768,2]{1,2,0:T(2,128)(2,1)}, u32[]{:S(2)}) copy-start(bf16[1,768,2]{1,2,0:T(2,128)(2,1)} %param.73) | copy-start | bytes 9220
  1762.4 159.5 %copy-start.177 = (bf16[1,768,2]{1,2,0:T(2,128)(2,1)S(1)}, bf16[1,768,2]{1,2,0:T(2,128)(2,1)}, u32[]{:S(2)}) copy-start(bf16[1,768,2]{1,2,0:T(2,128)(2,1)} %param.74) | copy-start | bytes 9220
  1762.4 159.5 %copy-start.266 = (s32[4]{0:T(128)S(1)}, s32[4]{0:T(128)}, u32[]{:S(2)}) copy-start(s32[4]{0:T(128)} %get-tuple-element.3714) | copy-start | bytes 52
  1762.4 155.3 %collective-permute-start.13 = (bf16[2,32,128,128]{2,3,1,0:T(8,128)(2,1)}, bf16[2,32,128,128]{2,3,1,0:T(8,128)(2,1)}, u32[]{:S(2)}, u32[]{:S(2)}) collective-permute-start(bf16[2,32,128,128]{2,3,1,0:T(8,128)(2,1)} %convert_element_type.1105), channel_id=1, source_target_pairs={{8,0},{16,8},{24,16},{9,1},{17,9},{25,17},{10,2},{18,10},{26,18},{... | collective-permute-start | bytes 6291464 | tf_op jit(solution)/shard_map/ppermute | solution.py:22
  1763.8 152.8 %collective-permute-start.12 = (bf16[256,768]{1,0:T(8,128)(2,1)}, bf16[256,768]{1,0:T(8,128)(2,1)}, u32[]{:S(2)}, u32[]{:S(2)}) collective-permute-start(bf16[256,768]{1,0:T(8,128)(2,1)} %get-tuple-element.2546), channel_id=1, source_target_pairs={{8,0},{16,8},{24,16},{9,1},{17,9},{25,17},{10,2},{18,10},{26,18},{... | collective-permute-start | bytes 1179656 | tf_op jit(solution)/shard_map/ppermute | solution.py:22
  1923.4 65.5 %copy-start.191 = (f32[768]{0:T(1024)}, f32[768]{0:T(1024)S(1)}, u32[]{:S(2)}) copy-start(f32[768]{0:T(1024)S(1)} %get-tuple-element.3843) | copy-start | bytes 9220 | tf_op jit(solution)/shard_map/cond
  1923.5 65.3 %copy-start.214 = (f32[256]{0:T(256)}, f32[256]{0:T(256)S(1)}, u32[]{:S(2)}) copy-start(f32[256]{0:T(256)S(1)} %broadcast_multiply_fusion.33) | copy-start | bytes 3076 | tf_op jit(solution)/shard_map/cond
  1947.8 29.4 copy-start.28
  1996.7 350.3 %copy-start.29 = (f32[256,768]{1,0:T(8,128)S(1)}, f32[256,768]{1,0:T(8,128)}, u32[]{:S(2)}) copy-start(f32[256,768]{1,0:T(8,128)} %copy-done.28) | copy-start | bytes 2359300 | tf_op jit(solution)/shard_map/cond
  1996.7 350.3 %copy-start.192 = (f32[768]{0:T(1024)S(1)}, f32[768]{0:T(1024)}, u32[]{:S(2)}) copy-start(f32[768]{0:T(1024)} %copy-done.191) | copy-start | bytes 9220 | tf_op jit(solution)/shard_map/cond
  1996.7 350.3 %copy-start.215 = (f32[256]{0:T(256)S(1)}, f32[256]{0:T(256)}, u32[]{:S(2)}) copy-start(f32[256]{0:T(256)} %copy-done.214) | copy-start | bytes 3076 | tf_op jit(solution)/shard_map/cond
  2002.6 12.2 copy-start.43
  2002.7 12.2 copy-start.50
  2354.5 59.5 %copy-start.173 = (bf16[1,768,2]{1,2,0:T(2,128)(2,1)S(1)}, bf16[1,768,2]{1,2,0:T(2,128)(2,1)}, u32[]{:S(2)}) copy-start(bf16[1,768,2]{1,2,0:T(2,128)(2,1)} %param.73) | copy-start | bytes 9220
  2354.5 59.5 %copy-start.178 = (bf16[1,768,2]{1,2,0:T(2,128)(2,1)S(1)}, bf16[1,768,2]{1,2,0:T(2,128)(2,1)}, u32[]{:S(2)}) copy-start(bf16[1,768,2]{1,2,0:T(2,128)(2,1)} %param.74) | copy-start | bytes 9220
  2354.5 59.5 %copy-start.267 = (s32[4]{0:T(128)S(1)}, s32[4]{0:T(128)}, u32[]{:S(2)}) copy-start(s32[4]{0:T(128)} %get-tuple-element.3714) | copy-start | bytes 52
  2354.5 55.3 %collective-permute-start.15 = (bf16[2,32,128,128]{3,1,0,2:T(8,128)(2,1)}, bf16[2,32,128,128]{3,1,0,2:T(8,128)(2,1)}, u32[]{:S(2)}, u32[]{:S(2)}) collective-permute-start(bf16[2,32,128,128]{3,1,0,2:T(8,128)(2,1)} %copy.737), channel_id=1, source_target_pairs={{8,0},{16,8},{24,16},{9,1},{17,9},{25,17},{10,2},{18,10},{26,18},{... | collective-permute-start | bytes 6291464 | tf_op jit(solution)/shard_map/ppermute | solution.py:22
  2355.9 52.8 %collective-permute-start.14 = (bf16[256,768]{1,0:T(8,128)(2,1)}, bf16[256,768]{1,0:T(8,128)(2,1)}, u32[]{:S(2)}, u32[]{:S(2)}) collective-permute-start(bf16[256,768]{1,0:T(8,128)(2,1)} %get-tuple-element.2559), channel_id=1, source_target_pairs={{8,0},{16,8},{24,16},{9,1},{17,9},{25,17},{10,2},{18,10},{26,18},{... | collective-permute-start | bytes 1179656 | tf_op jit(solution)/shard_map/ppermute | solution.py:22
  2414.1 57.9 %copy-start.3 = (bf16[2,256,768]{2,1,0:T(8,128)(2,1)}, bf16[2,256,768]{2,1,0:T(8,128)(2,1)S(1)}, u32[]{:S(2)}) copy-start(bf16[2,256,768]{2,1,0:T(8,128)(2,1)S(1)} %get-tuple-element.2415) | copy-start | bytes 2359300 | tf_op jit(solution)/shard_map/cond
  2415.5 56.5 %copy-start.185 = (f32[768]{0:T(1024)}, f32[768]{0:T(1024)S(1)}, u32[]{:S(2)}) copy-start(f32[768]{0:T(1024)S(1)} %get-tuple-element.3860) | copy-start | bytes 9220 | tf_op jit(solution)/shard_map/cond
  2440.0 20.4 copy-start.22
  2479.9 350.1 %copy-start.4 = (bf16[2,256,768]{2,1,0:T(8,128)(2,1)S(1)}, bf16[2,256,768]{2,1,0:T(8,128)(2,1)}, u32[]{:S(2)}) copy-start(bf16[2,256,768]{2,1,0:T(8,128)(2,1)} %copy-done.3) | copy-start | bytes 2359300 | tf_op jit(solution)/shard_map/cond
  2479.9 350.1 %copy-start.23 = (f32[256,768]{1,0:T(8,128)S(1)}, f32[256,768]{1,0:T(8,128)}, u32[]{:S(2)}) copy-start(f32[256,768]{1,0:T(8,128)} %copy-done.22) | copy-start | bytes 2359300 | tf_op jit(solution)/shard_map/cond
  2479.9 350.1 %copy-start.186 = (f32[768]{0:T(1024)S(1)}, f32[768]{0:T(1024)}, u32[]{:S(2)}) copy-start(f32[768]{0:T(1024)} %copy-done.185) | copy-start | bytes 9220 | tf_op jit(solution)/shard_map/cond
  2479.9 350.0 %copy-start.209 = (f32[256]{0:T(256)S(1)}, f32[256]{0:T(256)}, u32[]{:S(2)}) copy-start(f32[256]{0:T(256)} %copy-done.207) | copy-start | bytes 3076 | tf_op jit(solution)/shard_map/cond
  2485.9 13.8 copy-start.14
  2485.9 13.8 copy-start.15
  2834.7 58.2 %reduce-scatter.24.cloned.1.call-start = ((), (), s32[]{:S(2)}) async-start(), calls=%async_computation.13 | async-start | bytes 442368
  2837.1 80.5 %reduce-scatter.20.cloned.1.call-start = ((), (), s32[]{:S(2)}) async-start(), calls=%async_computation.11 | async-start | bytes 81920 | tf_op jit(solution)/shard_map/reduce_scatter | solution.py:412
  2838.6 118.2 %reduce-scatter.14.cloned.1.call-start = ((), (), s32[]{:S(2)}) async-start(), calls=%async_computation.8 | async-start | bytes 2654208 | tf_op jit(solution)/shard_map/reduce_scatter | solution.py:403
  2839.1 156.2 %reduce-scatter.16.cloned.1.call-start = ((), (), s32[]{:S(2)}) async-start(), calls=%async_computation.9 | async-start | bytes 2654208 | tf_op jit(solution)/shard_map/reduce_scatter | solution.py:404
  2839.7 194.1 %reduce-scatter.18.cloned.1.call-start = ((), (), s32[]{:S(2)}) async-start(), calls=%async_computation.10 | async-start | bytes 2654208 | tf_op jit(solution)/shard_map/reduce_scatter | solution.py:405
  2840.3 272.7 %reduce-scatter.12.cloned.1.call-start = ((), (), s32[]{:S(2)}) async-start(), calls=%async_computation.7 | async-start | bytes 7962624 | tf_op jit(solution)/shard_map/reduce_scatter | solution.py:402
  2844.0 269.1 %copy-start.1 = (s32[2,128,128]{2,1,0:T(8,128)S(1)}, s32[2,128,128]{2,1,0:T(8,128)}, u32[]{:S(2)}) copy-start(s32[2,128,128]{2,1,0:T(8,128)} %param.68) | copy-start | bytes 393220
  2845.4 267.7 %copy-start.70 = (bf16[2,256,768]{2,1,0:T(8,128)(2,1)}, bf16[2,256,768]{2,1,0:T(8,128)(2,1)S(1)}, u32[]{:S(2)}) copy-start(bf16[2,256,768]{2,1,0:T(8,128)(2,1)S(1)} %bitcast_dynamic-update-slice_fusion.30) | copy-start | bytes 2359300
  2862.9 250.1 %copy-start.61 = (bf16[2,256,768]{2,1,0:T(8,128)(2,1)}, bf16[2,256,768]{2,1,0:T(8,128)(2,1)S(1)}, u32[]{:S(2)}) copy-start(bf16[2,256,768]{2,1,0:T(8,128)(2,1)S(1)} %bitcast_dynamic-update-slice_fusion.20) | copy-start | bytes 2359300
  (114 other events, 535.6 us)
Sparse Core Ops, SparseCore 0:
  2834.8 26.7 reduce-scatter.21
  2863.9 28.8 reduce-scatter.23
  2895.6 21.8 reduce-scatter.19
  2920.4 36.3 reduce-scatter.13
  2959.6 35.6 reduce-scatter.15
  2998.1 35.6 reduce-scatter.17
  3036.8 76.1 reduce-scatter.11
where the time goes:
time: 3140 us; the launch traced here: 3120 us
  local copies, waits for them, and re-layouts  1420 us (45%)
  other arithmetic  745 us (24%)
  waiting for transfers between devices  603 us (19%)
  matrix products  193 us (6%)
  starting transfers between devices  68.9 us (2%)
  blocking collectives  43.9 us (1%)
    gather x10, local copies, waits for them, and re-layouts, make_bias(): jnp.take(path_table.astype(jnp.float32), path_blk, axis=0)  619 us
    gather x10, local copies, waits for them, and re-layouts, make_bias(): jnp.take(edge_table.astype(jnp.float32), edge_blk, axis=0)  619 us
    ppermute x16, waiting for transfers between devices, shifted(): lax.ppermute(value, axis, [(source, source + steps) for source in range(f...  383 us
    scatter-add x2, other arithmetic, table_grads(): jax.ops.segment_sum(pair_rows, path_blk.reshape(-1), num_segments=path_ta...  316 us
    scatter-add x2, other arithmetic, table_grads(): jax.ops.segment_sum(pair_rows, edge_blk.reshape(-1), num_segments=edge_ta...  316 us
    reduce_scatter x1, waiting for transfers between devices, on_device(): lax.psum_scatter(total_in, 'dp', scatter_dimension=0, tiled=True)  79.2 us
    ppermute x16, starting transfers between devices, shifted(): lax.ppermute(value, axis, [(source, source + steps) for source in range(f...  68.6 us
  transfers between devices with their start and end apart: 23, of which 13 were waited for; matrix products, arithmetic and copies ran while one was open for 22% of the time, Pallas kernels for 0%

commit v1 on v0

--- a/solution.py
+++ b/solution.py
@@ -20,6 +20,14 @@
     count = lax.axis_size(axis)
     first, last = (max(0, -steps), min(count, count - steps))
     return lax.ppermute(value, axis, [(source, source + steps) for source in range(first, last)])
+
+
+def of_molecule(per_mol, group):
+    picked = jnp.broadcast_to(per_mol[:1], group.shape + per_mol.shape[1:])
+    for mol in range(1, per_mol.shape[0]):
+        hit = (group == mol).reshape((-1,) + (1,) * (per_mol.ndim - 1))
+        picked = jnp.where(hit, per_mol[mol : mol + 1], picked)
+    return picked
 
 
 def gelu_tanh(values):
@@ -270,9 +278,9 @@
     heads = kernel_proj.shape[1]
     micro_rows = SEQ_MB * atom_slots
     ticks = MICRO + sections - 1
-    path_seq = jnp.take(path_dist, conformer_group, axis=0)
-    edge_seq = jnp.take(edge_kind, conformer_group, axis=0)
-    count_seq = jnp.take(atom_counts, conformer_group, axis=0)
+    path_seq = of_molecule(path_dist, conformer_group)
+    edge_seq = of_molecule(edge_kind, conformer_group)
+    count_seq = of_molecule(atom_counts, conformer_group)
     cot_micro = cotangent[0].reshape(MICRO, micro_rows, width)
     bias_shape = (SEQ_MB, heads, atom_slots, atom_slots)
 

time: 3140 us -> 3130 us (level)
  waiting for transfers between devices: 603 us -> 650 us
  starting transfers between devices: 68.9 us -> 36.4 us
    ppermute x16, waiting for transfers between devices: 383 us -> 430 us  [shifted(): lax.ppermute(value, axis, [(source, source + steps) for source in range(f...]
    ppermute x16, starting transfers between devices: 68.6 us -> 36.1 us  [shifted(): lax.ppermute(value, axis, [(source, source + steps) for source in range(f...]
  transfers between devices with their start and end apart: 23 -> 23, of which waited for: 13 -> 14; matrix products, arithmetic and copies ran while one was open for 22% -> 13% of each run, Pallas kernels for 0% -> 0%
where the time goes in v1:
time: 3130 us; the launch traced here: 3110 us
  local copies, waits for them, and re-layouts  1390 us (44%)
  other arithmetic  745 us (24%)
  waiting for transfers between devices  650 us (21%)
  matrix products  192 us (6%)
  blocking collectives  43.9 us (1%)
  starting transfers between devices  36.4 us (1%)
  loops' own time  31.3 us (1%)
    gather x10, local copies, waits for them, and re-layouts, make_bias(): jnp.take(path_table.astype(jnp.float32), path_blk, axis=0)  608 us
    gather x10, local copies, waits for them, and re-layouts, make_bias(): jnp.take(edge_table.astype(jnp.float32), edge_blk, axis=0)  608 us
    ppermute x16, waiting for transfers between devices, shifted(): lax.ppermute(value, axis, [(source, source + steps) for source in range(f...  430 us
    scatter-add x2, other arithmetic, table_grads(): jax.ops.segment_sum(pair_rows, path_blk.reshape(-1), num_segments=path_ta...  316 us
    scatter-add x2, other arithmetic, table_grads(): jax.ops.segment_sum(pair_rows, edge_blk.reshape(-1), num_segments=edge_ta...  316 us
    reduce_scatter x1, waiting for transfers between devices, on_device(): lax.psum_scatter(total_in, 'dp', scatter_dimension=0, tiled=True)  79.5 us
  transfers between devices with their start and end apart: 23, of which 14 were waited for; matrix products, arithmetic and copies ran while one was open for 13% of the time, Pallas kernels for 0%

profile of v1, /device:TPU:0, one launch (start us, length us, event | category | flops | bytes accessed | tf_op | source)
XLA Modules:
  0.0 3108.3 jit_solution(7370787127975191222)
XLA Ops:
  9.0 247.9 %conditional.20 = (bf16[2,32,128,128]{3,1,2,0:T(8,128)(2,1)S(1)}) conditional(s32[]{:T(128)} %convert_element_type.1089, () %tuple.229, (f32[4,3,128]{2,0,1:T(4,128)}, s32[]{:T(128)}, bf16[128,32]{0,1:T(8,128)(2,1)}, bf16[64,32]{0,1:T(8,128)(2,1)}, s32[4,128,128]{2,1,0:T(8,128)S(1)}, /*index=5*/bf16[32,32]{1,0:T(8,128)(2,1)}, ...), branch_computations={%region_0.1_spmd, %region_1.5_spmd} | conditional | flops 295373952 | bytes 46137444 | solution.py:311
  9.9 108.2 %gather_fusion.1 = f32[32768,32]{1,0:T(8,128)} fusion(f32[32,32]{1,0:T(8,128)S(1)} %convert_element_type.854, s32[32768]{0:T(1024)S(1)} %broadcast_clamp_fusion), kind=kCustom, calls=%fused_computation.1.clone | custom fusion | bytes 8519680 | tf_op jit(solution)/shard_map/cond/branch_1_fun/jit(_take)/gather | solution.py:83
  118.1 11.4 copy.696
  129.6 108.2 %gather_fusion = f32[32768,32]{1,0:T(8,128)} fusion(f32[64,32]{1,0:T(8,128)S(1)} %convert_element_type.853, s32[32768]{0:T(1024)S(1)} %broadcast_clamp_fusion.1), kind=kCustom, calls=%fused_computation.clone | custom fusion | bytes 8519680 | tf_op jit(solution)/shard_map/cond/branch_1_fun/jit(_take)/gather | solution.py:83
  237.8 11.4 copy.694
  249.5 7.4 fusion.80
  259.5 44.4 %collective-permute-done.1 = bf16[2,32,128,128]{3,1,2,0:T(8,128)(2,1)} collective-permute-done((bf16[2,32,128,128]{3,1,2,0:T(8,128)(2,1)S(1)}, bf16[2,32,128,128]{3,1,2,0:T(8,128)(2,1)}, u32[]{:S(2)}, u32[]{:S(2)}) %collective-permute-start.1) | collective-permute-done | bytes 2097184 | tf_op jit(solution)/shard_map/ppermute | solution.py:22
  303.9 248.8 %conditional.22 = (bf16[2,32,128,128]{3,1,2,0:T(8,128)(2,1)}) conditional(s32[]{:T(128)} %convert_element_type.1089, bf16[2,32,128,128]{3,1,2,0:T(8,128)(2,1)} %collective-permute-done.1, (f32[4,3,128]{2,0,1:T(4,128)}, s32[]{:T(128)}, bf16[128,32]{0,1:T(8,128)(2,1)}, bf16[64,32]{0,1:T(8,128)(2,1)}, s32[4,128,128]{2,1,0:T(8,128)S(1)}, ...), branch_computations={%region_11.14_spmd, %region_12.16_spmd} | conditional | flops 295373952 | bytes 46137444 | solution.py:311
  304.7 108.2 %gather_fusion.3 = f32[32768,32]{1,0:T(8,128)} fusion(f32[32,32]{1,0:T(8,128)S(1)} %convert_element_type.872, s32[32768]{0:T(1024)S(1)} %broadcast_clamp_fusion.2), kind=kCustom, calls=%fused_computation.6.clone | custom fusion | bytes 8519680 | tf_op jit(solution)/shard_map/cond/branch_1_fun/jit(_take)/gather | solution.py:83
  413.0 11.4 copy.700
  424.5 108.2 %gather_fusion.2 = f32[32768,32]{1,0:T(8,128)} fusion(f32[64,32]{1,0:T(8,128)S(1)} %convert_element_type.871, s32[32768]{0:T(1024)S(1)} %broadcast_clamp_fusion.3), kind=kCustom, calls=%fused_computation.2.clone | custom fusion | bytes 8519680 | tf_op jit(solution)/shard_map/cond/branch_1_fun/jit(_take)/gather | solution.py:83
  532.7 11.4 copy.698
  544.3 8.4 fusion.95
  555.3 44.2 %collective-permute-done.3 = bf16[2,32,128,128]{3,1,2,0:T(8,128)(2,1)} collective-permute-done((bf16[2,32,128,128]{3,1,2,0:T(8,128)(2,1)}, bf16[2,32,128,128]{3,1,2,0:T(8,128)(2,1)}, u32[]{:S(2)}, u32[]{:S(2)}) %collective-permute-start.3) | collective-permute-done | bytes 2097184 | tf_op jit(solution)/shard_map/ppermute | solution.py:22
  599.5 249.9 %conditional.24 = (bf16[2,32,128,128]{3,1,2,0:T(8,128)(2,1)}) conditional(s32[]{:T(128)} %convert_element_type.1089, bf16[2,32,128,128]{3,1,2,0:T(8,128)(2,1)} %collective-permute-done.3, (f32[4,3,128]{2,0,1:T(4,128)}, s32[]{:T(128)}, bf16[128,32]{0,1:T(8,128)(2,1)}, bf16[64,32]{0,1:T(8,128)(2,1)}, s32[4,128,128]{2,1,0:T(8,128)}, ...), branch_computations={%region_22.25_spmd, %region_23.27_spmd} | conditional | flops 295373952 | bytes 46137444 | solution.py:311
  601.4 108.2 %gather_fusion.5 = f32[32768,32]{1,0:T(8,128)} fusion(f32[32,32]{1,0:T(8,128)S(1)} %convert_element_type.890, s32[32768]{0:T(1024)S(1)} %broadcast_clamp_fusion.4), kind=kCustom, calls=%fused_computation.7.clone | custom fusion | bytes 8519680 | tf_op jit(solution)/shard_map/cond/branch_1_fun/jit(_take)/gather | solution.py:83
  709.6 11.4 copy.704
  721.1 108.2 %gather_fusion.4 = f32[32768,32]{1,0:T(8,128)} fusion(f32[64,32]{1,0:T(8,128)S(1)} %convert_element_type.889, s32[32768]{0:T(1024)S(1)} %broadcast_clamp_fusion.5), kind=kCustom, calls=%fused_computation.3.clone | custom fusion | bytes 8519680 | tf_op jit(solution)/shard_map/cond/branch_1_fun/jit(_take)/gather | solution.py:83
  829.3 11.4 copy.702
  841.0 8.4 fusion.110
  855.9 37.1 %conditional.21 = (bf16[256,768]{1,0:T(8,128)(2,1)}) conditional(s32[]{:T(128)} %convert_element_type.1088, () %tuple.228, (bf16[256,768]{1,0:T(8,128)(2,1)}, bf16[768,2]{0,1:T(2,128)(2,1)S(1)}, bf16[768,2]{0,1:T(2,128)(2,1)S(1)}, bf16[768,2304]{1,0:T(8,128)(2,1)}, s32[4]{0:T(128)S(1)}, /*index=5*/s32[]{:T(128)}, ...), branch_computations={%region_3.6_spmd, %region_4.13_spmd} | conditional | flops 1928466304 | bytes 41951836 | solution.py:314
  910.3 37.1 %conditional.23 = (bf16[256,768]{1,0:T(8,128)(2,1)}) conditional(s32[]{:T(128)} %convert_element_type.1090, () %tuple.232, (bf16[256,768]{1,0:T(8,128)(2,1)}, bf16[768,2]{0,1:T(2,128)(2,1)S(1)}, bf16[768,2]{0,1:T(2,128)(2,1)S(1)}, bf16[768,2304]{1,0:T(8,128)(2,1)}, s32[4]{0:T(128)S(1)}, /*index=5*/s32[]{:T(128)}, ...), branch_computations={%region_14.17_spmd, %region_15.24_spmd} | conditional | flops 1928466304 | bytes 41951836 | solution.py:314
  961.5 272.9 %conditional.26 = (bf16[2,32,128,128]{3,1,2,0:T(8,128)(2,1)}) conditional(s32[]{:T(128)} %convert_element_type.1089, bf16[2,32,128,128]{3,1,2,0:T(8,128)(2,1)} %collective-permute-done.5, (f32[4,3,128]{2,0,1:T(4,128)S(1)}, s32[]{:T(128)}, bf16[128,32]{0,1:T(8,128)(2,1)S(1)}, bf16[64,32]{0,1:T(8,128)(2,1)S(1)}, s32[4,128,128]{2,1,0:T(8,128)}, ...), branch_computations={%region_33.36_spmd, %region_34.38_spmd} | conditional | flops 295373952 | bytes 46063632 | solution.py:311
  964.0 118.7 %gather_fusion.7 = f32[32768,32]{1,0:T(8,128)} fusion(f32[32,32]{1,0:T(8,128)S(1)} %convert_element_type.908, s32[32768]{0:T(1024)} %broadcast_clamp_fusion.6), kind=kCustom, calls=%fused_computation.8.clone | custom fusion | bytes 8519680 | tf_op jit(solution)/shard_map/cond/branch_1_fun/jit(_take)/gather | solution.py:83
  1082.7 11.4 copy.708
  1095.7 118.7 %gather_fusion.6 = f32[32768,32]{1,0:T(8,128)} fusion(f32[64,32]{1,0:T(8,128)S(1)} %convert_element_type.907, s32[32768]{0:T(1024)} %broadcast_clamp_fusion.7), kind=kCustom, calls=%fused_computation.4.clone | custom fusion | bytes 8519680 | tf_op jit(solution)/shard_map/cond/branch_1_fun/jit(_take)/gather | solution.py:83
  1214.4 11.4 copy.706
  1226.0 8.4 fusion.125
  1253.9 34.4 %collective-permute-done.4 = bf16[256,768]{1,0:T(8,128)(2,1)S(1)} collective-permute-done((bf16[256,768]{1,0:T(8,128)(2,1)}, bf16[256,768]{1,0:T(8,128)(2,1)S(1)}, u32[]{:S(2)}, u32[]{:S(2)}) %collective-permute-start.4) | collective-permute-done | bytes 393248 | tf_op jit(solution)/shard_map/ppermute | solution.py:22
  1307.8 249.0 %conditional.28 = (bf16[2,32,128,128]{3,1,2,0:T(8,128)(2,1)}) conditional(s32[]{:T(128)} %convert_element_type.1089, bf16[2,32,128,128]{3,1,2,0:T(8,128)(2,1)} %collective-permute-done.7, (f32[4,3,128]{2,0,1:T(4,128)S(1)}, s32[]{:T(128)}, bf16[128,32]{0,1:T(8,128)(2,1)S(1)}, bf16[64,32]{0,1:T(8,128)(2,1)S(1)}, s32[4,128,128]{2,1,0:T(8,128)S(1)}, ...), branch_computations={%region_44.47_spmd, %region_45.49_spmd} | conditional | flops 295373952 | bytes 46129224 | solution.py:311
  1308.9 108.2 %gather_fusion.9 = f32[32768,32]{1,0:T(8,128)} fusion(f32[32,32]{1,0:T(8,128)S(1)} %convert_element_type.926, s32[32768]{0:T(1024)S(1)} %broadcast_clamp_fusion.8), kind=kCustom, calls=%fused_computation.9.clone | custom fusion | bytes 8519680 | tf_op jit(solution)/shard_map/cond/branch_1_fun/jit(_take)/gather | solution.py:83
  1417.1 11.4 copy.712
  1428.6 108.2 %gather_fusion.8 = f32[32768,32]{1,0:T(8,128)} fusion(f32[64,32]{1,0:T(8,128)S(1)} %convert_element_type.925, s32[32768]{0:T(1024)S(1)} %broadcast_clamp_fusion.9), kind=kCustom, calls=%fused_computation.5.clone | custom fusion | bytes 8519680 | tf_op jit(solution)/shard_map/cond/branch_1_fun/jit(_take)/gather | solution.py:83
  1536.8 11.4 copy.710
  1548.5 8.3 fusion.140
  1565.5 25.1 conditional.30
  1597.3 53.2 %collective-permute-done.8 = bf16[256,768]{1,0:T(8,128)(2,1)} collective-permute-done((bf16[256,768]{1,0:T(8,128)(2,1)}, bf16[256,768]{1,0:T(8,128)(2,1)}, u32[]{:S(2)}, u32[]{:S(2)}) %collective-permute-start.8) | collective-permute-done | bytes 393248 | tf_op jit(solution)/shard_map/ppermute | solution.py:22
  1655.7 12.6 conditional.31
  1675.0 52.2 %collective-permute-done.10 = bf16[256,768]{1,0:T(8,128)(2,1)} collective-permute-done((bf16[256,768]{1,0:T(8,128)(2,1)}, bf16[256,768]{1,0:T(8,128)(2,1)}, u32[]{:S(2)}, u32[]{:S(2)}) %collective-permute-start.10) | collective-permute-done | bytes 393248 | tf_op jit(solution)/shard_map/ppermute | solution.py:22
  1732.5 12.9 conditional.32
  1752.1 150.6 %collective-permute-done.12 = bf16[256,768]{1,0:T(8,128)(2,1)} collective-permute-done((bf16[256,768]{1,0:T(8,128)(2,1)}, bf16[256,768]{1,0:T(8,128)(2,1)}, u32[]{:S(2)}, u32[]{:S(2)}) %collective-permute-start.12) | collective-permute-done | bytes 393248 | tf_op jit(solution)/shard_map/ppermute | solution.py:22
  1908.0 427.4 %conditional.33 = (f32[768,2304]{1,0:T(8,128)}, f32[768,768]{1,0:T(8,128)}, f32[768,768]{1,0:T(8,128)}, f32[768,768]{1,0:T(8,128)}, f32[768]{0:T(1024)}, /*index...) conditional(s32[]{:T(128)} %convert_element_type.1103, ...), branch_computations={%region_121.124_spmd, %region_122.145_spmd} | conditional | flops 7117012992 | bytes 281617248 | solution.py:395
  1956.0 7.3 convolution_add_fusion.21
  1982.8 348.9 %conditional.3 = ((f32[128,32]{0,1:T(8,128)}, f32[64,32]{1,0:T(8,128)}, f32[32,32]{1,0:T(8,128)})) conditional(s32[]{:T(128)} %convert_element_type.1037, (f32[128,32]{0,1:T(8,128)}, f32[64,32]{1,0:T(8,128)}, f32[32,32]{1,0:T(8,128)}) %tuple.192, (f32[4,3,128]{2,0,1:T(4,128)S(1)}, s32[]{:T(128)}, f32[2,32,128,128]{2,3,1,0:T(8,128)}, ...), branch_computations={%region_136.138_spmd, %region_137.142_spmd} | conditional | flops 1633947776 | bytes 49862752 | solution.py:380
  1988.7 12.2 fusion.48
  2001.7 14.5 copy.648
  2016.1 157.8 %scatter_fusion.6 = f32[64,32]{1,0:T(8,128)} fusion(f32[64,32]{1,0:T(8,128)} %get-tuple-element.2358, s32[32768]{0:T(1024)} %bitcast.1000, f32[32768,32]{1,0:T(8,128)} %bitcast.922), kind=kCustom, calls=%fused_computation.16 | custom fusion | flops 1048576 | bytes 12713984 | tf_op jit(solution)/shard_map/cond/branch_1_fun/cond/branch_1_fun/scatter-add | solution.py:97
  2173.9 157.8 %scatter_fusion.7 = f32[32,32]{1,0:T(8,128)} fusion(f32[32,32]{1,0:T(8,128)} %get-tuple-element.2360, s32[32768]{0:T(1024)} %bitcast.997, f32[32768,32]{1,0:T(8,128)} %bitcast.923), kind=kCustom, calls=%fused_computation.17 | custom fusion | flops 1048576 | bytes 12713984 | tf_op jit(solution)/shard_map/cond/branch_1_fun/cond/branch_1_fun/scatter-add | solution.py:100
  2343.3 50.7 %collective-permute-done.14 = bf16[256,768]{1,0:T(8,128)(2,1)} collective-permute-done((bf16[256,768]{1,0:T(8,128)(2,1)}, bf16[256,768]{1,0:T(8,128)(2,1)}, u32[]{:S(2)}, u32[]{:S(2)}) %collective-permute-start.14) | collective-permute-done | bytes 393248 | tf_op jit(solution)/shard_map/ppermute | solution.py:22
  2399.3 418.4 %conditional.34 = (f32[768,2304]{1,0:T(8,128)}, f32[768,768]{1,0:T(8,128)}, f32[768,768]{1,0:T(8,128)}, f32[768,768]{1,0:T(8,128)}, f32[768]{0:T(1024)}, /*index...) conditional(s32[]{:T(128)} %convert_element_type.1107, ...), branch_computations={%region_143.146_spmd, %region_144.167_spmd} | conditional | flops 7118061568 | bytes 318870592 | solution.py:395
  2438.4 7.3 convolution_add_fusion.26
  2465.2 348.7 %conditional.4 = ((f32[128,32]{0,1:T(8,128)}, f32[64,32]{1,0:T(8,128)}, f32[32,32]{1,0:T(8,128)})) conditional(s32[]{:T(128)} %convert_element_type.1062, (f32[128,32]{0,1:T(8,128)}, f32[64,32]{1,0:T(8,128)}, f32[32,32]{1,0:T(8,128)}) %tuple.197, (f32[4,3,128]{2,0,1:T(4,128)S(1)}, s32[]{:T(128)}, f32[2,32,128,128]{2,3,1,0:T(8,128)}, ...), branch_computations={%region_158.160_spmd, %region_159.164_spmd} | conditional | flops 1636044928 | bytes 98097248 | solution.py:380
  2471.2 13.7 fusion.64
  2488.0 10.3 copy.671
  2498.2 157.9 %scatter_fusion = f32[64,32]{1,0:T(8,128)} fusion(f32[64,32]{1,0:T(8,128)} %get-tuple-element.2409, s32[32768]{0:T(1024)S(1)} %bitcast.994, f32[32768,32]{1,0:T(8,128)} %bitcast.916), kind=kCustom, calls=%fused_computation.18 | custom fusion | flops 1048576 | bytes 12713984 | tf_op jit(solution)/shard_map/cond/branch_1_fun/cond/branch_1_fun/scatter-add | solution.py:97
  2656.1 157.8 %scatter_fusion.1 = f32[32,32]{1,0:T(8,128)} fusion(f32[32,32]{1,0:T(8,128)} %get-tuple-element.2411, s32[32768]{0:T(1024)S(1)} %bitcast.993, f32[32768,32]{1,0:T(8,128)} %bitcast.917), kind=kCustom, calls=%fused_computation.19 | custom fusion | flops 1048576 | bytes 12713984 | tf_op jit(solution)/shard_map/cond/branch_1_fun/cond/branch_1_fun/scatter-add | solution.py:100
  2835.3 14.9 all-reduce.3
  2852.9 28.0 reduce-scatter.24.cloned.1.call-done
  2882.4 23.2 reduce-scatter.20.cloned.1.call-done
  2905.6 29.0 all-reduce.2
  2934.6 10.3 reduce-scatter.14.cloned.1.call-done
  2944.9 38.5 %reduce-scatter.16.cloned.1.call-done = f32[96,768]{1,0:T(8,128)} async-done(((f32[768,768]{1,0:T(8,128)}), f32[96,768]{1,0:T(8,128)}) %reduce-scatter.16.cloned.1.call-update) | async-done | bytes 294928 | tf_op jit(solution)/shard_map/reduce_scatter | solution.py:412
  2983.5 38.3 %reduce-scatter.18.cloned.1.call-done = f32[96,768]{1,0:T(8,128)} async-done(((f32[768,768]{1,0:T(8,128)}), f32[96,768]{1,0:T(8,128)}) %reduce-scatter.18.cloned.1.call-update) | async-done | bytes 294928 | tf_op jit(solution)/shard_map/reduce_scatter | solution.py:413
  3021.7 79.5 %reduce-scatter.12.cloned.1.call-done = f32[96,2304]{1,0:T(8,128)} async-done(((f32[768,2304]{1,0:T(8,128)}), f32[96,2304]{1,0:T(8,128)}) %reduce-scatter.12.cloned.1.call-update) | async-done | bytes 884752 | tf_op jit(solution)/shard_map/reduce_scatter | solution.py:410
  (665 shorter events, 416.7 us)
Async XLA Ops:
  7.2 2844.2 %reduce-scatter.22.cloned.1.call-start = ((), (), s32[]{:S(2)}) async-start(), calls=%async_computation.12 | async-start | bytes 442368
  9.0 295.0 %copy-start.44 = (s32[4,128,128]{2,1,0:T(8,128)}, s32[4,128,128]{2,1,0:T(8,128)S(1)}, u32[]{:S(2)}) copy-start(s32[4,128,128]{2,1,0:T(8,128)S(1)} %get-tuple-element.3864) | copy-start | bytes 786436
  9.0 1556.5 %copy-start.37 = (s32[4,128,128]{2,1,0:T(8,128)}, s32[4,128,128]{2,1,0:T(8,128)S(1)}, u32[]{:S(2)}) copy-start(s32[4,128,128]{2,1,0:T(8,128)S(1)} %get-tuple-element.3863) | copy-start | bytes 786436
  256.8 47.1 %copy-start.12 = (bf16[2,32,128,128]{3,1,2,0:T(8,128)(2,1)}, bf16[2,32,128,128]{3,1,2,0:T(8,128)(2,1)S(1)}, u32[]{:S(2)}) copy-start(bf16[2,32,128,128]{3,1,2,0:T(8,128)(2,1)S(1)} %get-tuple-element.4031) | copy-start | bytes 6291460
  256.9 47.1 %collective-permute-start.1 = (bf16[2,32,128,128]{3,1,2,0:T(8,128)(2,1)S(1)}, bf16[2,32,128,128]{3,1,2,0:T(8,128)(2,1)}, u32[]{:S(2)}, u32[]{:S(2)}) collective-permute-start(bf16[2,32,128,128]{3,1,2,0:T(8,128)(2,1)S(1)} %get-tuple-element.4031), channel_id=1, source_target_pairs={{0,8},{8,16},{16,24},{1,9},{9,17},{17,25},{2,10},{10,18},{18,26},{... | collective-permute-start | bytes 6291464 | tf_op jit(solution)/shard_map/ppermute | solution.py:22
  552.7 46.8 %collective-permute-start.3 = (bf16[2,32,128,128]{3,1,2,0:T(8,128)(2,1)}, bf16[2,32,128,128]{3,1,2,0:T(8,128)(2,1)}, u32[]{:S(2)}, u32[]{:S(2)}) collective-permute-start(bf16[2,32,128,128]{3,1,2,0:T(8,128)(2,1)} %get-tuple-element.4033), channel_id=1, source_target_pairs={{0,8},{8,16},{16,24},{1,9},{9,17},{17,25},{2,10},{10,18},{18,26},{... | collective-permute-start | bytes 6291464 | tf_op jit(solution)/shard_map/ppermute | solution.py:22
  555.3 296.7 %copy-start.249 = (s32[2]{0:T(128)S(1)}, s32[2]{0:T(128)}, u32[]{:S(2)}) copy-start(s32[2]{0:T(128)} %param.64) | copy-start | bytes 28
  555.3 297.3 %copy-start.250 = (s32[4]{0:T(128)S(1)}, s32[4]{0:T(128)}, u32[]{:S(2)}) copy-start(s32[4]{0:T(128)} %param.63) | copy-start | bytes 52
  555.3 300.6 %copy-start = (bf16[1,768,768]{2,1,0:T(8,128)(2,1)S(1)}, bf16[1,768,768]{2,1,0:T(8,128)(2,1)}, u32[]{:S(2)}) copy-start(bf16[1,768,768]{2,1,0:T(8,128)(2,1)} %param.68) | copy-start | bytes 3538948
  555.3 300.6 %copy-start.5 = (bf16[1,768,768]{2,1,0:T(8,128)(2,1)S(1)}, bf16[1,768,768]{2,1,0:T(8,128)(2,1)}, u32[]{:S(2)}) copy-start(bf16[1,768,768]{2,1,0:T(8,128)(2,1)} %param.70) | copy-start | bytes 3538948
  555.3 300.6 %copy-start.157 = (bf16[1,768,2]{1,2,0:T(2,128)(2,1)S(1)}, bf16[1,768,2]{1,2,0:T(2,128)(2,1)}, u32[]{:S(2)}) copy-start(bf16[1,768,2]{1,2,0:T(2,128)(2,1)} %param.71) | copy-start | bytes 9220
  555.3 300.6 %copy-start.162 = (bf16[1,768,2]{1,2,0:T(2,128)(2,1)S(1)}, bf16[1,768,2]{1,2,0:T(2,128)(2,1)}, u32[]{:S(2)}) copy-start(bf16[1,768,2]{1,2,0:T(2,128)(2,1)} %param.72) | copy-start | bytes 9220
  849.4 112.1 %collective-permute-start.5 = (bf16[2,32,128,128]{3,1,2,0:T(8,128)(2,1)}, bf16[2,32,128,128]{3,1,2,0:T(8,128)(2,1)}, u32[]{:S(2)}, u32[]{:S(2)}) collective-permute-start(bf16[2,32,128,128]{3,1,2,0:T(8,128)(2,1)} %get-tuple-element.4035), channel_id=1, source_target_pairs={{0,8},{8,16},{16,24},{1,9},{9,17},{17,25},{2,10},{10,18},{18,26},{... | collective-permute-start | bytes 6291464 | tf_op jit(solution)/shard_map/ppermute | solution.py:22
  853.9 711.5 %copy-start.251 = (s32[4]{0:T(128)}, s32[4]{0:T(128)S(1)}, u32[]{:S(2)}) copy-start(s32[4]{0:T(128)S(1)} %broadcast_select_fusion.5) | copy-start | bytes 52
  892.9 11.1 collective-permute-start
  947.4 14.1 copy-start.167
  947.4 14.1 copy-start.171
  947.4 14.1 copy-start.262
  947.4 289.6 %collective-permute-start.2 = (bf16[256,768]{1,0:T(8,128)(2,1)}, bf16[256,768]{1,0:T(8,128)(2,1)}, u32[]{:S(2)}, u32[]{:S(2)}) collective-permute-start(bf16[256,768]{1,0:T(8,128)(2,1)} %get-tuple-element.4034), channel_id=1, source_target_pairs={{0,8},{8,16},{16,24},{1,9},{9,17},{17,25},{2,10},{10,18},{18,26},{... | collective-permute-start | bytes 1179656 | tf_op jit(solution)/shard_map/ppermute | solution.py:22
  1234.4 73.4 %collective-permute-start.7 = (bf16[2,32,128,128]{3,1,2,0:T(8,128)(2,1)}, bf16[2,32,128,128]{3,1,2,0:T(8,128)(2,1)}, u32[]{:S(2)}, u32[]{:S(2)}) collective-permute-start(bf16[2,32,128,128]{3,1,2,0:T(8,128)(2,1)} %get-tuple-element.4037), channel_id=1, source_target_pairs={{0,8},{8,16},{16,24},{1,9},{9,17},{17,25},{2,10},{10,18},{18,26},{... | collective-permute-start | bytes 6291464 | tf_op jit(solution)/shard_map/ppermute | solution.py:22
  1245.0 43.3 %copy-start.102 = (bf16[1,256,768]{2,1,0:T(8,128)(2,1)S(1)}, bf16[1,256,768]{2,1,0:T(8,128)(2,1)}, u32[]{:S(2)}) copy-start(bf16[1,256,768]{2,1,0:T(8,128)(2,1)} %constant_dynamic-slice_fusion.29) | copy-start | bytes 1179652
  1245.0 43.3 %collective-permute-start.4 = (bf16[256,768]{1,0:T(8,128)(2,1)}, bf16[256,768]{1,0:T(8,128)(2,1)S(1)}, u32[]{:S(2)}, u32[]{:S(2)}) collective-permute-start(bf16[256,768]{1,0:T(8,128)(2,1)} %get-tuple-element.4036), channel_id=1, source_target_pairs={{0,8},{8,16},{16,24},{1,9},{9,17},{17,25},{2,10},{10,18},{18,26},{... | collective-permute-start | bytes 1179656 | tf_op jit(solution)/shard_map/ppermute | solution.py:22
  1295.3 11.7 collective-permute-start.6
  1594.6 61.1 %copy-start.158 = (bf16[1,768,2]{1,2,0:T(2,128)(2,1)S(1)}, bf16[1,768,2]{1,2,0:T(2,128)(2,1)}, u32[]{:S(2)}) copy-start(bf16[1,768,2]{1,2,0:T(2,128)(2,1)} %param.71) | copy-start | bytes 9220
  1594.6 61.1 %copy-start.163 = (bf16[1,768,2]{1,2,0:T(2,128)(2,1)S(1)}, bf16[1,768,2]{1,2,0:T(2,128)(2,1)}, u32[]{:S(2)}) copy-start(bf16[1,768,2]{1,2,0:T(2,128)(2,1)} %param.72) | copy-start | bytes 9220
  1594.6 61.1 %copy-start.252 = (s32[4]{0:T(128)S(1)}, s32[4]{0:T(128)}, u32[]{:S(2)}) copy-start(s32[4]{0:T(128)} %copy-done.251) | copy-start | bytes 52
  1594.6 56.9 %collective-permute-start.9 = (bf16[2,32,128,128]{2,3,1,0:T(8,128)(2,1)}, bf16[2,32,128,128]{2,3,1,0:T(8,128)(2,1)}, u32[]{:S(2)}, u32[]{:S(2)}) collective-permute-start(bf16[2,32,128,128]{2,3,1,0:T(8,128)(2,1)} %convert_element_type.1097), channel_id=1, source_target_pairs={{8,0},{16,8},{24,16},{9,1},{17,9},{25,17},{10,2},{18,10},{26,18},{... | collective-permute-start | bytes 6291464 | tf_op jit(solution)/shard_map/ppermute | solution.py:22
  1596.0 54.5 %collective-permute-start.8 = (bf16[256,768]{1,0:T(8,128)(2,1)}, bf16[256,768]{1,0:T(8,128)(2,1)}, u32[]{:S(2)}, u32[]{:S(2)}) collective-permute-start(bf16[256,768]{1,0:T(8,128)(2,1)} %get-tuple-element.2519), channel_id=1, source_target_pairs={{8,0},{16,8},{24,16},{9,1},{17,9},{25,17},{10,2},{18,10},{26,18},{... | collective-permute-start | bytes 1179656 | tf_op jit(solution)/shard_map/ppermute | solution.py:22
  1672.3 60.2 %copy-start.159 = (bf16[1,768,2]{1,2,0:T(2,128)(2,1)S(1)}, bf16[1,768,2]{1,2,0:T(2,128)(2,1)}, u32[]{:S(2)}) copy-start(bf16[1,768,2]{1,2,0:T(2,128)(2,1)} %param.71) | copy-start | bytes 9220
  1672.3 60.2 %copy-start.164 = (bf16[1,768,2]{1,2,0:T(2,128)(2,1)S(1)}, bf16[1,768,2]{1,2,0:T(2,128)(2,1)}, u32[]{:S(2)}) copy-start(bf16[1,768,2]{1,2,0:T(2,128)(2,1)} %param.72) | copy-start | bytes 9220
  1672.3 60.2 %copy-start.253 = (s32[4]{0:T(128)S(1)}, s32[4]{0:T(128)}, u32[]{:S(2)}) copy-start(s32[4]{0:T(128)} %copy-done.251) | copy-start | bytes 52
  1672.3 56.0 %collective-permute-start.11 = (bf16[2,32,128,128]{2,3,1,0:T(8,128)(2,1)}, bf16[2,32,128,128]{2,3,1,0:T(8,128)(2,1)}, u32[]{:S(2)}, u32[]{:S(2)}) collective-permute-start(bf16[2,32,128,128]{2,3,1,0:T(8,128)(2,1)} %convert_element_type.1101), channel_id=1, source_target_pairs={{8,0},{16,8},{24,16},{9,1},{17,9},{25,17},{10,2},{18,10},{26,18},{... | collective-permute-start | bytes 6291464 | tf_op jit(solution)/shard_map/ppermute | solution.py:22
  1673.7 53.6 %collective-permute-start.10 = (bf16[256,768]{1,0:T(8,128)(2,1)}, bf16[256,768]{1,0:T(8,128)(2,1)}, u32[]{:S(2)}, u32[]{:S(2)}) collective-permute-start(bf16[256,768]{1,0:T(8,128)(2,1)} %get-tuple-element.2532), channel_id=1, source_target_pairs={{8,0},{16,8},{24,16},{9,1},{17,9},{25,17},{10,2},{18,10},{26,18},{... | collective-permute-start | bytes 1179656 | tf_op jit(solution)/shard_map/ppermute | solution.py:22
  1749.4 158.6 %copy-start.160 = (bf16[1,768,2]{1,2,0:T(2,128)(2,1)S(1)}, bf16[1,768,2]{1,2,0:T(2,128)(2,1)}, u32[]{:S(2)}) copy-start(bf16[1,768,2]{1,2,0:T(2,128)(2,1)} %param.71) | copy-start | bytes 9220
  1749.4 158.6 %copy-start.165 = (bf16[1,768,2]{1,2,0:T(2,128)(2,1)S(1)}, bf16[1,768,2]{1,2,0:T(2,128)(2,1)}, u32[]{:S(2)}) copy-start(bf16[1,768,2]{1,2,0:T(2,128)(2,1)} %param.72) | copy-start | bytes 9220
  1749.4 158.6 %copy-start.254 = (s32[4]{0:T(128)S(1)}, s32[4]{0:T(128)}, u32[]{:S(2)}) copy-start(s32[4]{0:T(128)} %copy-done.251) | copy-start | bytes 52
  1749.4 154.4 %collective-permute-start.13 = (bf16[2,32,128,128]{2,3,1,0:T(8,128)(2,1)}, bf16[2,32,128,128]{2,3,1,0:T(8,128)(2,1)}, u32[]{:S(2)}, u32[]{:S(2)}) collective-permute-start(bf16[2,32,128,128]{2,3,1,0:T(8,128)(2,1)} %convert_element_type.1105), channel_id=1, source_target_pairs={{8,0},{16,8},{24,16},{9,1},{17,9},{25,17},{10,2},{18,10},{26,18},{... | collective-permute-start | bytes 6291464 | tf_op jit(solution)/shard_map/ppermute | solution.py:22
  1750.8 151.9 %collective-permute-start.12 = (bf16[256,768]{1,0:T(8,128)(2,1)}, bf16[256,768]{1,0:T(8,128)(2,1)}, u32[]{:S(2)}, u32[]{:S(2)}) collective-permute-start(bf16[256,768]{1,0:T(8,128)(2,1)} %get-tuple-element.2545), channel_id=1, source_target_pairs={{8,0},{16,8},{24,16},{9,1},{17,9},{25,17},{10,2},{18,10},{26,18},{... | collective-permute-start | bytes 1179656 | tf_op jit(solution)/shard_map/ppermute | solution.py:22
  1909.4 65.5 %copy-start.180 = (f32[768]{0:T(1024)}, f32[768]{0:T(1024)S(1)}, u32[]{:S(2)}) copy-start(f32[768]{0:T(1024)S(1)} %get-tuple-element.3840) | copy-start | bytes 9220 | tf_op jit(solution)/shard_map/cond
  1909.5 65.4 %copy-start.201 = (f32[256]{0:T(256)}, f32[256]{0:T(256)S(1)}, u32[]{:S(2)}) copy-start(f32[256]{0:T(256)S(1)} %broadcast_multiply_fusion.33) | copy-start | bytes 3076 | tf_op jit(solution)/shard_map/cond
  1933.9 29.5 copy-start.27
  1982.8 350.3 %copy-start.28 = (f32[256,768]{1,0:T(8,128)S(1)}, f32[256,768]{1,0:T(8,128)}, u32[]{:S(2)}) copy-start(f32[256,768]{1,0:T(8,128)} %copy-done.27) | copy-start | bytes 2359300 | tf_op jit(solution)/shard_map/cond
  1982.8 350.3 %copy-start.181 = (f32[768]{0:T(1024)S(1)}, f32[768]{0:T(1024)}, u32[]{:S(2)}) copy-start(f32[768]{0:T(1024)} %copy-done.180) | copy-start | bytes 9220 | tf_op jit(solution)/shard_map/cond
  1982.8 350.3 %copy-start.202 = (f32[256]{0:T(256)S(1)}, f32[256]{0:T(256)}, u32[]{:S(2)}) copy-start(f32[256]{0:T(256)} %copy-done.201) | copy-start | bytes 3076 | tf_op jit(solution)/shard_map/cond
  2340.6 58.7 %copy-start.161 = (bf16[1,768,2]{1,2,0:T(2,128)(2,1)S(1)}, bf16[1,768,2]{1,2,0:T(2,128)(2,1)}, u32[]{:S(2)}) copy-start(bf16[1,768,2]{1,2,0:T(2,128)(2,1)} %param.71) | copy-start | bytes 9220
  2340.6 58.7 %copy-start.166 = (bf16[1,768,2]{1,2,0:T(2,128)(2,1)S(1)}, bf16[1,768,2]{1,2,0:T(2,128)(2,1)}, u32[]{:S(2)}) copy-start(bf16[1,768,2]{1,2,0:T(2,128)(2,1)} %param.72) | copy-start | bytes 9220
  2340.6 58.7 %copy-start.255 = (s32[4]{0:T(128)S(1)}, s32[4]{0:T(128)}, u32[]{:S(2)}) copy-start(s32[4]{0:T(128)} %copy-done.251) | copy-start | bytes 52
  2340.6 54.5 %collective-permute-start.15 = (bf16[2,32,128,128]{3,1,0,2:T(8,128)(2,1)}, bf16[2,32,128,128]{3,1,0,2:T(8,128)(2,1)}, u32[]{:S(2)}, u32[]{:S(2)}) collective-permute-start(bf16[2,32,128,128]{3,1,0,2:T(8,128)(2,1)} %copy.737), channel_id=1, source_target_pairs={{8,0},{16,8},{24,16},{9,1},{17,9},{25,17},{10,2},{18,10},{26,18},{... | collective-permute-start | bytes 6291464 | tf_op jit(solution)/shard_map/ppermute | solution.py:22
  2342.0 52.0 %collective-permute-start.14 = (bf16[256,768]{1,0:T(8,128)(2,1)}, bf16[256,768]{1,0:T(8,128)(2,1)}, u32[]{:S(2)}, u32[]{:S(2)}) collective-permute-start(bf16[256,768]{1,0:T(8,128)(2,1)} %get-tuple-element.2558), channel_id=1, source_target_pairs={{8,0},{16,8},{24,16},{9,1},{17,9},{25,17},{10,2},{18,10},{26,18},{... | collective-permute-start | bytes 1179656 | tf_op jit(solution)/shard_map/ppermute | solution.py:22
  2399.3 58.0 %copy-start.1 = (bf16[2,256,768]{2,1,0:T(8,128)(2,1)}, bf16[2,256,768]{2,1,0:T(8,128)(2,1)S(1)}, u32[]{:S(2)}) copy-start(bf16[2,256,768]{2,1,0:T(8,128)(2,1)S(1)} %get-tuple-element.2414) | copy-start | bytes 2359300 | tf_op jit(solution)/shard_map/cond
  2400.7 56.6 %copy-start.174 = (f32[768]{0:T(1024)}, f32[768]{0:T(1024)S(1)}, u32[]{:S(2)}) copy-start(f32[768]{0:T(1024)S(1)} %get-tuple-element.3857) | copy-start | bytes 9220 | tf_op jit(solution)/shard_map/cond
  2425.2 20.5 copy-start.21
  2465.2 350.1 %copy-start.2 = (bf16[2,256,768]{2,1,0:T(8,128)(2,1)S(1)}, bf16[2,256,768]{2,1,0:T(8,128)(2,1)}, u32[]{:S(2)}) copy-start(bf16[2,256,768]{2,1,0:T(8,128)(2,1)} %copy-done.1) | copy-start | bytes 2359300 | tf_op jit(solution)/shard_map/cond
  2465.2 350.1 %copy-start.22 = (f32[256,768]{1,0:T(8,128)S(1)}, f32[256,768]{1,0:T(8,128)}, u32[]{:S(2)}) copy-start(f32[256,768]{1,0:T(8,128)} %copy-done.21) | copy-start | bytes 2359300 | tf_op jit(solution)/shard_map/cond
  2465.2 350.1 %copy-start.175 = (f32[768]{0:T(1024)S(1)}, f32[768]{0:T(1024)}, u32[]{:S(2)}) copy-start(f32[768]{0:T(1024)} %copy-done.174) | copy-start | bytes 9220 | tf_op jit(solution)/shard_map/cond
  2465.2 350.1 %copy-start.196 = (f32[256]{0:T(256)S(1)}, f32[256]{0:T(256)}, u32[]{:S(2)}) copy-start(f32[256]{0:T(256)} %copy-done.194) | copy-start | bytes 3076 | tf_op jit(solution)/shard_map/cond
  2820.0 60.9 %reduce-scatter.24.cloned.1.call-start = ((), (), s32[]{:S(2)}) async-start(), calls=%async_computation.13 | async-start | bytes 442368
  2822.4 83.2 %reduce-scatter.20.cloned.1.call-start = ((), (), s32[]{:S(2)}) async-start(), calls=%async_computation.11 | async-start | bytes 81920 | tf_op jit(solution)/shard_map/reduce_scatter | solution.py:420
  2823.9 121.0 %reduce-scatter.14.cloned.1.call-start = ((), (), s32[]{:S(2)}) async-start(), calls=%async_computation.8 | async-start | bytes 2654208 | tf_op jit(solution)/shard_map/reduce_scatter | solution.py:411
  2824.5 159.0 %reduce-scatter.16.cloned.1.call-start = ((), (), s32[]{:S(2)}) async-start(), calls=%async_computation.9 | async-start | bytes 2654208 | tf_op jit(solution)/shard_map/reduce_scatter | solution.py:412
  2825.1 196.7 %reduce-scatter.18.cloned.1.call-start = ((), (), s32[]{:S(2)}) async-start(), calls=%async_computation.10 | async-start | bytes 2654208 | tf_op jit(solution)/shard_map/reduce_scatter | solution.py:413
  2825.7 275.6 %reduce-scatter.12.cloned.1.call-start = ((), (), s32[]{:S(2)}) async-start(), calls=%async_computation.7 | async-start | bytes 7962624 | tf_op jit(solution)/shard_map/reduce_scatter | solution.py:410
  2833.9 267.4 %copy-start.61 = (bf16[2,256,768]{2,1,0:T(8,128)(2,1)}, bf16[2,256,768]{2,1,0:T(8,128)(2,1)S(1)}, u32[]{:S(2)}) copy-start(bf16[2,256,768]{2,1,0:T(8,128)(2,1)S(1)} %bitcast_dynamic-update-slice_fusion.30) | copy-start | bytes 2359300
  2851.4 249.9 %copy-start.60 = (bf16[2,256,768]{2,1,0:T(8,128)(2,1)}, bf16[2,256,768]{2,1,0:T(8,128)(2,1)S(1)}, u32[]{:S(2)}) copy-start(bf16[2,256,768]{2,1,0:T(8,128)(2,1)S(1)} %bitcast_dynamic-update-slice_fusion.20) | copy-start | bytes 2359300
  (105 other events, 530.8 us)
Sparse Core Ops, SparseCore 0:
  2820.2 29.5 reduce-scatter.21
  2852.1 28.7 reduce-scatter.23
  2883.7 21.8 reduce-scatter.19
  2908.4 36.4 reduce-scatter.13
  2947.8 35.6 reduce-scatter.15
  2986.3 35.3 reduce-scatter.17
  3024.7 76.4 reduce-scatter.11

commit v2 on v0

v2 whole, which is shorter than its diff:
```python
import functools
import math

import jax
import jax.numpy as jnp
from jax import lax
from jax.experimental import pallas as pl
from jax.experimental.pallas import tpu as pltpu
from jax.sharding import PartitionSpec as P

F32, BF16 = jnp.float32, jnp.bfloat16
MESH = pl.DeviceIdType.MESH
EPS = 1e-05
NEG_BIG = -1e30
KERN_SPAN = 8.0
KERN_WIDTH = 0.4
LOG2E = math.log2(math.e)
LANES = 128
DEPTH = 256


def dot(a, b):
    return jnp.dot(a, b, preferred_element_type=F32)


def dot_nt(a, b):
    return lax.dot_general(a, b, (((1,), (1,)), ((), ())), preferred_element_type=F32)


def rows_of(ref, m, n):
    return ref.at[pl.ds(pl.multiple_of(m * n, n), n), :]


def norm_parts(values):
    center = values - jnp.mean(values, axis=-1, keepdims=True)
    inv_std = lax.rsqrt(jnp.mean(center * center, axis=-1, keepdims=True) + EPS)
    return center * inv_std, inv_std


def norm_back(dy, xh, inv_std, gain):
    dxh = dy * gain
    return inv_std * (
        dxh
        - jnp.mean(dxh, axis=-1, keepdims=True)
        - xh * jnp.mean(dxh * xh, axis=-1, keepdims=True)
    )


def gelu(u):
    return 0.5 * u * (1.0 + jnp.tanh(0.7978845608028654 * (u + 0.044715 * u * u * u)))


def gelu_slope(u):
    sq = u * u
    t = jnp.tanh(0.7978845608028654 * (u + 0.044715 * sq * u))
    return 0.5 * (1.0 + t) + 0.5 * u * (1.0 - t * t) * (
        0.7978845608028654 * (1.0 + 3 * 0.044715 * sq)
    )


def pair_windows(head_dim):
    out = []
    for pair in range(8):
        lo, hi = pair * 2 * head_dim, pair * 2 * head_dim + 2 * head_dim - 1
        first = lo // LANES
        out.append((first, hi // LANES - first + 1, lo - first * LANES))
    return out


def both_heads(block, off, head_dim):
    lane = lax.broadcasted_iota(jnp.int32, (1, block.shape[1]), 1)
    one = ((lane >= off) & (lane < off + head_dim)).astype(F32).astype(BF16)
    two = ((lane >= off + head_dim) & (lane < off + 2 * head_dim)).astype(F32).astype(BF16)
    return jnp.concatenate([block * one, block * two], axis=0)


def features(dist8, path8, edge8, row, spd, edges, kern):
    atoms = dist8.shape[1]
    alpha = math.sqrt(0.5 * LOG2E) / KERN_WIDTH
    center = lax.broadcasted_iota(jnp.int32, (kern, atoms), 0).astype(F32) * (
        KERN_SPAN / kern * alpha
    )
    t = dist8[row : row + 1, :] * alpha - center
    gauss = jnp.exp2(-(t * t))
    path_id = lax.broadcasted_iota(jnp.int32, (spd, atoms), 0).astype(F32)
    edge_id = lax.broadcasted_iota(jnp.int32, (edges, atoms), 0).astype(F32)
    path = jnp.where(path8[row : row + 1, :] == path_id, 1.0, 0.0)
    edge = jnp.where(edge8[row : row + 1, :] == edge_id, 1.0, 0.0)
    rest = jnp.zeros((DEPTH - kern - spd - edges, atoms), F32)
    return jnp.concatenate([gauss, path, edge, rest], axis=0).astype(BF16)


def body(
    sections, micro, atoms, heads, kern, spd, edges,
    group, counts, tokens, cot, posn, path_in, edge_in, win, wout, wup, wdown, norms, tab,
    hidden, igrad, g_in, g_out, g_up, g_down, g_norm, g_tab,
    xs, grecv, a_s, qkv_s, o_s, mid_s, c_s, u_s, act_s, df_s, du_s, dat_s, dqkv_s,
    pairs, probs, dist_s, path_s, edge_s, tr_b, tr_f, dk_s, dv_s, left_s,
    fsend, frecv, bsend, brecv,
):
    width = wout.shape[0]
    head_dim = width // heads
    scale = 1.0 / math.sqrt(head_dim)
    windows = pair_windows(head_dim)
    s = lax.axis_index("section") if sections > 1 else 0
    d = lax.axis_index("dp") if sections > 1 else 0
    last = s == sections - 1

    if sections > 1:
        barrier = pltpu.get_barrier_semaphore()

        @pl.when(s > 0)
        def _():
            pl.semaphore_signal(barrier, inc=1, device_id=(s - 1, d), device_id_type=MESH)

        @pl.when(s < sections - 1)
        def _():
            pl.semaphore_signal(barrier, inc=1, device_id=(s + 1, d), device_id_type=MESH)

        pl.semaphore_wait(barrier, jnp.where((s > 0) & (s < sections - 1), 2, 1))

    def forward_copy(m):
        return pltpu.make_async_remote_copy(
            src_ref=rows_of(hidden, m, atoms), dst_ref=rows_of(xs, m, atoms),
            send_sem=fsend.at[m], recv_sem=frecv.at[m],
            device_id=(jnp.minimum(s + 1, sections - 1), d), device_id_type=MESH,
        )

    def backward_copy(m):
        return pltpu.make_async_remote_copy(
            src_ref=rows_of(igrad, m, atoms), dst_ref=rows_of(grecv, m, atoms),
            send_sem=bsend.at[m], recv_sem=brecv.at[m],
            device_id=(jnp.maximum(s - 1, 0), d), device_id_type=MESH,
        )

    @pl.when(s == 0)
    def _():
        xs[...] = tokens[...]

    @pl.when(last)
    def _():
        grecv[...] = jnp.zeros_like(grecv)

    g_norm[...] = jnp.zeros_like(g_norm)
    g_tab[...] = jnp.zeros_like(g_tab)

    def make_bias(m):
        mol = group[m]
        count = counts[mol]
        pos = posn[m]
        pos_t = jnp.transpose(jnp.concatenate([pos, jnp.zeros((5, atoms), F32)], axis=0))
        total = jnp.zeros((atoms, atoms), F32)
        for axis in range(3):
            diff = pos_t[:, axis : axis + 1] - pos[axis : axis + 1, :]
            total = total + diff * diff
        dist_s[m] = jnp.sqrt(total)
        path_s[m] = jnp.transpose(path_in[mol].astype(F32))
        edge_s[m] = jnp.transpose(edge_in[mol].astype(F32))
        out_ref = pairs.at[m]

        @pl.loop(0, atoms // 8)
        def _(t):
            eight = pl.ds(pl.multiple_of(t * 8, 8), 8)
            d8, p8, e8 = dist_s[m, eight, :], path_s[m, eight, :], edge_s[m, eight, :]
            for r in range(0, 8, 2):
                feats = jnp.concatenate(
                    [features(d8, p8, e8, r + q, spd, edges, kern) for q in range(2)], axis=1
                )
                got = dot(tab[...], feats) * LOG2E
                for q in range(2):
                    j = t * 8 + r + q
                    row = jnp.where(j < count, got[:, q * atoms : (q + 1) * atoms], NEG_BIG)
                    out_ref[pl.ds(j, heads, stride=atoms), :] = row

    def table_grads(m):
        in_ref = pairs.at[m]

        def step(t, acc):
            eight = pl.ds(pl.multiple_of(t * 8, 8), 8)
            d8, p8, e8 = dist_s[m, eight, :], path_s[m, eight, :], edge_s[m, eight, :]
            for r in range(0, 8, 2):
                feats = jnp.concatenate(
                    [features(d8, p8, e8, r + q, spd, edges, kern) for q in range(2)], axis=1
                )
                halves = []
                for q in range(2):
                    j = t * 8 + r + q
                    halves.append(in_ref[pl.ds(j, heads, stride=atoms), :])
                ds = jnp.concatenate(halves, axis=1).astype(BF16)
                acc = acc + dot_nt(feats, ds)
            return acc

        g_tab[...] += lax.fori_loop(0, atoms // 8, step, jnp.zeros((DEPTH, heads), F32))

    def forward(m):
        x = rows_of(xs, m, atoms)[...].astype(F32)
        xh, _ = norm_parts(x)
        a = (xh * norms[0:1, :] + norms[2:3, :]).astype(BF16)
        rows_of(a_s, m, atoms)[...] = a
        qkv = rows_of(qkv_s, m, atoms)
        for blk in range(3):
            got = dot(a, win[:, blk * width : (blk + 1) * width])
            qkv[:, blk * width : (blk + 1) * width] = got.astype(BF16)
            if blk == 2:
                tr_b[...] = jnp.transpose(got).astype(BF16)

        @pl.loop(0, heads // 16)
        def _(g):
            base = g * 16 * head_dim
            for pair, (tile, tiles, off) in enumerate(windows):
                lane = pl.multiple_of(base + tile * LANES, LANES)
                span = tiles * LANES
                rows = pl.ds(pl.multiple_of((g * 8 + pair) * atoms, atoms), atoms)
                one = pl.ds(pl.multiple_of((g * 8 + pair) * 2 * atoms, atoms), atoms)
                two = pl.ds(pl.multiple_of((g * 8 + pair) * 2 * atoms + atoms, atoms), atoms)
                qm = both_heads(qkv[:, pl.ds(lane, span)], off, head_dim)
                z = dot_nt(qkv[:, pl.ds(width + lane, span)], qm) * (scale * LOG2E)
                z = z + jnp.concatenate([pairs[m, one, :], pairs[m, two, :]], axis=1)
                e = jnp.exp2(z - jnp.max(z, axis=0, keepdims=True))
                p = (e * (1.0 / jnp.sum(e, axis=0, keepdims=True))).astype(BF16)
                probs[m, rows, :] = p
                first = pl.multiple_of(base + pair * 2 * head_dim, 16)
                got = dot(tr_b[pl.ds(first, 2 * head_dim), :], p)
                tr_f[pl.ds(first, head_dim), :] = got[:head_dim, :atoms]
                tr_f[pl.ds(pl.multiple_of(first + head_dim, 8), head_dim), :] = got[head_dim:, atoms:]

        o = jnp.transpose(tr_f[...]).astype(BF16)
        rows_of(o_s, m, atoms)[...] = o
        mid = x + dot(o, wout[...])
        rows_of(mid_s, m, atoms)[...] = mid
        xh, _ = norm_parts(mid)
        c = (xh * norms[1:2, :] + norms[3:4, :]).astype(BF16)
        rows_of(c_s, m, atoms)[...] = c
        u = dot(c, wup[...])
        rows_of(u_s, m, atoms)[...] = u
        act = gelu(u).astype(BF16)
        rows_of(act_s, m, atoms)[...] = act
        rows_of(hidden, m, atoms)[...] = (mid + dot(act, wdown[...])).astype(BF16)

    def backward(m):
        grad = rows_of(cot, m, atoms)[...].astype(F32) + rows_of(grecv, m, atoms)[...].astype(F32)
        df = grad.astype(BF16)
        rows_of(df_s, m, atoms)[...] = df
        du = (dot_nt(df, wdown[...]) * gelu_slope(rows_of(u_s, m, atoms)[...])).astype(BF16)
        rows_of(du_s, m, atoms)[...] = du
        dc = dot_nt(du, wup[...])
        xh, inv_std = norm_parts(rows_of(mid_s, m, atoms)[...])
        g_norm[1:2, :] += jnp.sum(dc * xh, axis=0, keepdims=True)
        g_norm[3:4, :] += jnp.sum(dc, axis=0, keepdims=True)
        dmid = grad + norm_back(dc, xh, inv_std, norms[1:2, :])
        rows_of(mid_s, m, atoms)[...] = dmid
        dat = dmid.astype(BF16)
        rows_of(dat_s, m, atoms)[...] = dat
        qkv = rows_of(qkv_s, m, atoms)
        dqkv = rows_of(dqkv_s, m, atoms)
        dqkv[:, 0:width] = dot_nt(dat, wout[...]).astype(BF16)
        tr_b[...] = jnp.transpose(qkv[:, width : 2 * width].astype(F32)).astype(BF16)
        dk_s[...] = jnp.zeros_like(dk_s)
        dv_s[...] = jnp.zeros_like(dv_s)

        @pl.loop(0, heads // 16)
        def _(g):
            base = g * 16 * head_dim
            for pair, (tile, tiles, off) in enumerate(windows):
                lane = pl.multiple_of(base + tile * LANES, LANES)
                span = tiles * LANES
                rows = pl.ds(pl.multiple_of((g * 8 + pair) * atoms, atoms), atoms)
                one = pl.ds(pl.multiple_of((g * 8 + pair) * 2 * atoms, atoms), atoms)
                two = pl.ds(pl.multiple_of((g * 8 + pair) * 2 * atoms + atoms, atoms), atoms)
                dom = both_heads(dqkv[:, pl.ds(lane, span)], off, head_dim)
                dp = dot_nt(qkv[:, pl.ds(2 * width + lane, span)], dom)
                p_low = probs[m, rows, :]
                p = p_low.astype(F32)
                pd = p * dp
                ds = pd - p * jnp.sum(pd, axis=0, keepdims=True)
                pairs[m, one, :] = ds[:, :atoms]
                pairs[m, two, :] = ds[:, atoms:]
                ds_low = ds.astype(BF16)
                dv_s[:, pl.ds(lane, span)] += dot(p_low, dom)
                qm = both_heads(qkv[:, pl.ds(lane, span)], off, head_dim)
                dk_s[:, pl.ds(lane, span)] += dot(ds_low, qm)
                first = pl.multiple_of(base + pair * 2 * head_dim, 16)
                got = dot(tr_b[pl.ds(first, 2 * head_dim), :], ds_low)
                tr_f[pl.ds(first, head_dim), :] = got[:head_dim, :atoms]
                tr_f[pl.ds(pl.multiple_of(first + head_dim, 8), head_dim), :] = got[head_dim:, atoms:]

        dqkv[:, 0:width] = (jnp.transpose(tr_f[...]) * scale).astype(BF16)
        dqkv[:, width : 2 * width] = (dk_s[...] * scale).astype(BF16)
        dqkv[:, 2 * width :] = dv_s[...].astype(BF16)
        da = dot_nt(dqkv[...], win[...])
        xh, inv_std = norm_parts(rows_of(xs, m, atoms)[...].astype(F32))
        g_norm[0:1, :] += jnp.sum(da * xh, axis=0, keepdims=True)
        g_norm[2:3, :] += jnp.sum(da, axis=0, keepdims=True)
        out = rows_of(mid_s, m, atoms)[...] + norm_back(da, xh, inv_std, norms[0:1, :])
        rows_of(igrad, m, atoms)[...] = out.astype(BF16)

    def weight_grads():
        for left, right, out in (
            (act_s, df_s, g_down), (c_s, du_s, g_up), (o_s, dat_s, g_out), (a_s, dqkv_s, g_in),
        ):
            for m in range(micro):
                part = left[m * atoms : (m + 1) * atoms, :].astype(F32)
                left_s[:, m * atoms : (m + 1) * atoms] = jnp.transpose(part).astype(BF16)

            @pl.loop(0, right.shape[1] // 256)
            def _(n):
                cols = pl.ds(pl.multiple_of(n * 256, 256), 256)
                out[:, cols] = dot(left_s[...], right[:, cols]).astype(out.dtype)

    heads_up = 2 * micro
    total = 4 * micro + 1

    @pl.loop(0, total)
    def _(t):
        first = s == 0
        tail = t - heads_up
        is_bias = jnp.where(first, (t < heads_up) & (t % 2 == 0), t < micro)
        is_fwd = jnp.where(
            last,
            (t >= micro) & (t < 3 * micro) & ((t - micro) % 2 == 0),
            jnp.where(first, (t < heads_up) & (t % 2 == 1), (t >= micro) & (t < heads_up)),
        )
        is_back = jnp.where(
            last,
            (t >= micro) & (t < 3 * micro) & ((t - micro) % 2 == 1),
            (tail >= 0) & (tail < 2 * micro - 1) & (tail % 2 == 0),
        )
        is_sum = jnp.where(last, t == 3 * micro, tail == 2 * micro - 1)
        is_tab = jnp.where(
            last,
            t > 3 * micro,
            ((tail >= 0) & (tail < 2 * micro - 1) & (tail % 2 == 1)) | (tail == 2 * micro),
        )
        m_bias = jnp.where(first, t // 2, t)
        m_fwd = jnp.where(last, (t - micro) // 2, jnp.where(first, t // 2, t - micro))
        m_back = jnp.where(last, (t - micro) // 2, tail // 2)
        m_tab = jnp.where(last, t - 3 * micro - 1, jnp.where(tail == 2 * micro, micro - 1, tail // 2))
        if sections == 1:
            is_bias, m_bias = t < micro, t

        @pl.when(is_bias)
        def _():
            make_bias(m_bias)

        @pl.when(is_fwd)
        def _():
            if sections > 1:
                @pl.when(s > 0)
                def _():
                    forward_copy(m_fwd).wait_recv()

            forward(m_fwd)
            if sections > 1:
                @pl.when(jnp.logical_not(last))
                def _():
                    forward_copy(m_fwd).start()

        @pl.when(is_back)
        def _():
            if sections > 1:
                @pl.when(jnp.logical_not(last))
                def _():
                    backward_copy(m_back).wait_recv()

            backward(m_back)
            if sections > 1:
                @pl.when(s > 0)
                def _():
                    backward_copy(m_back).start()

        @pl.when(is_sum)
        def _():
            weight_grads()

        @pl.when(is_tab)
        def _():
            table_grads(m_tab)

    if sections > 1:
        @pl.loop(0, micro)
        def _(m):
            @pl.when(jnp.logical_not(last))
            def _():
                forward_copy(m).wait_send()

            @pl.when(s > 0)
            def _():
                backward_copy(m).wait_send()


def layer_call(
    sections, grad_type, tokens, cot, posn, group, counts, path_in, edge_in, win, wout, wup, wdown, norms, tab,
    kern, spd, edges,
):
    micro, _, atoms = posn.shape
    rows, width = tokens.shape
    heads = tab.shape[0]
    shape = jax.ShapeDtypeStruct
    vmem, smem = pl.BlockSpec(memory_space=pltpu.VMEM), pl.BlockSpec(memory_space=pltpu.SMEM)
    outs = (
        shape((rows, width), BF16), shape((rows, width), BF16),
        shape(win.shape, grad_type), shape(wout.shape, grad_type), shape(wup.shape, grad_type),
        shape(wdown.shape, grad_type), shape((4, width), F32), shape((DEPTH, heads), F32),
    )
    low = lambda *dims: pltpu.VMEM(dims, BF16)
    wide = lambda *dims: pltpu.VMEM(dims, F32)
    pair_rows = heads // 2 * atoms
    scratch = [
        low(rows, width), low(rows, width), low(rows, width), low(rows, 3 * width), low(rows, width),
        wide(rows, width), low(rows, width), wide(rows, width), low(rows, width), low(rows, width),
        low(rows, width), low(rows, width), low(rows, 3 * width),
        wide(micro, 2 * pair_rows, atoms), low(micro, pair_rows, 2 * atoms),
        wide(micro, atoms, atoms), wide(micro, atoms, atoms), wide(micro, atoms, atoms),
        low(width, atoms), wide(width, atoms), wide(atoms, width), wide(atoms, width), low(width, rows),
    ] + [pltpu.SemaphoreType.DMA((micro,))] * 4
    params = dict(vmem_limit_bytes=60 * 2**20, has_side_effects=True)
    if sections > 1:
        params["collective_id"] = 0
    return pl.pallas_call(
        functools.partial(body, sections, micro, atoms, heads, kern, spd, edges),
        out_shape=outs,
        in_specs=[smem, smem] + [vmem] * 11,
        out_specs=[vmem] * len(outs),
        scratch_shapes=scratch,
        compiler_params=pltpu.CompilerParams(**params),
        name="sections",
    )(group, counts, tokens, cot, posn, path_in, edge_in, win, wout, wup, wdown, norms, tab)


def on_device(
    tokens, cotangent, positions, conformer_group, atom_counts, path_dist, edge_kind, attn_in, attn_out,
    ffn_up, ffn_down, norm_gain, norm_shift, kernel_proj, path_table, edge_table,
):
    sections = lax.axis_size("section")
    kern, heads = kernel_proj.shape
    spd, edges = path_table.shape[0], edge_table.shape[0]
    norms = jnp.concatenate([norm_gain[0].T, norm_shift[0].T], axis=0).astype(F32)
    rest = jnp.zeros((DEPTH - kern - spd - edges, heads), BF16)
    tab = jnp.concatenate([kernel_proj, path_table, edge_table, rest], axis=0).T
    hidden, igrad, *grads, g_norm, g_tab = layer_call(
        sections, BF16, tokens, cotangent[0], positions, conformer_group, atom_counts, path_dist, edge_kind,
        attn_in[0], attn_out[0], ffn_up[0], ffn_down[0], norms, tab, kern, spd, edges,
    )
    sums = [lax.psum_scatter(g, "dp", scatter_dimension=0, tiled=True)[None].astype(F32) for g in grads]
    norm_sum = lax.psum(g_norm, "dp").T
    share = norm_sum.shape[0] // lax.axis_size("dp")
    norm_sum = lax.dynamic_slice_in_dim(norm_sum, lax.axis_index("dp") * share, share, 0)[None]
    tab_sum = lax.psum(g_tab, ("section", "dp"))
    tabs, start = [], 0
    for count in (kern, spd, edges):
        own = count // sections
        tabs.append(lax.dynamic_slice_in_dim(tab_sum, start + lax.axis_index("section") * own, own, 0))
        start += count
    return (hidden[None], igrad[None], *sums, norm_sum[:, :, :2], norm_sum[:, :, 2:], *tabs)


def solution(mesh):
    in_specs = (
        P("dp", None),
        P("section", "dp", None),
        P("dp", None, None),
        P("dp"),
        P("dp"),
        P("dp", None, None),
        P("dp", None, None),
        P("section", None, None),
        P("section", None, None),
        P("section", None, None),
        P("section", None, None),
        P("section", None, None),
        P("section", None, None),
        P(),
        P(),
        P(),
    )
    out_specs = (
        P("section", "dp", None),
        P("section", "dp", None),
        P("section", "dp", None),
        P("section", "dp", None),
        P("section", "dp", None),
        P("section", "dp", None),
        P("section", "dp", None),
        P("section", "dp", None),
        P("section", None),
        P("section", None),
        P("section", None),
    )
    return jax.shard_map(
        on_device, mesh=mesh, in_specs=in_specs, out_specs=out_specs, check_vma=False
    )
```

time: 3140 us -> 316 us (0.10)
  local copies, waits for them, and re-layouts: 1420 us -> 6.73 us
  other arithmetic: 745 us -> 9.69 us
  waiting for transfers between devices: 603 us -> 68 us
  matrix products: 193 us -> 0 us
  Pallas kernels: 0 us -> 149 us
  starting transfers between devices: 68.9 us -> 0.16 us
    gather x23 -> x0, local copies, waits for them, and re-layouts: 1240 us -> none  [the longest x10 619 us: make_bias(): jnp.take(path_table.astype(jnp.float32), path_blk, axis=0)]
    scatter-add x4 -> x0, other arithmetic: 631 us -> none  [the longest x2 316 us: table_grads(): jax.ops.segment_sum(pair_rows, path_blk.reshape(-1), num_segments=path_ta...]
    ppermute x16 -> x0, waiting for transfers between devices: 383 us -> none  [shifted(): lax.ppermute(value, axis, [(source, source + steps) for source in range(f...]
    dot_general x47 -> x0, matrix products: 169 us -> none  [the longest x5 41.8 us: make_bias(): jnp.einsum('kh,skij->shij', kernel_proj, feats_low, preferred_element_typ...]
    pallas_call x0 -> x1, Pallas kernels: none -> 149 us  [layer_call(): pl.pallas_call(functools.partial(body, sections, micro, atoms, heads, ker...]
    reduce_scatter x5 -> x4, waiting for transfers between devices: 190 us -> 66.1 us  [on_device(): lax.psum_scatter(g, 'dp', scatter_dimension=0, tiled=True)[None].astype(F32)]
    ppermute x16 -> x0, starting transfers between devices: 68.6 us -> none  [shifted(): lax.ppermute(value, axis, [(source, source + steps) for source in range(f...]
    another operation x41 -> x0, local copies, waits for them, and re-layouts: 43.4 us -> none
  transfers between devices with their start and end apart: 23 -> 4, of which waited for: 13 -> 2; matrix products, arithmetic and copies ran while one was open for 22% -> 2% of each run, Pallas kernels for 0% -> 0%
where the time goes in v2:
time: 316 us; the launch traced here: 315 us
  Pallas kernels  149 us (47%)
  waiting for transfers between devices  68 us (22%)
  blocking collectives  67.8 us (21%)
  between operations  13.8 us (4%)
  other arithmetic  9.69 us (3%)
  local copies, waits for them, and re-layouts  6.73 us (2%)
    pallas_call x1, Pallas kernels, layer_call(): pl.pallas_call(functools.partial(body, sections, micro, atoms, heads, ker...  149 us
    reduce_scatter x4, waiting for transfers between devices, on_device(): lax.psum_scatter(g, 'dp', scatter_dimension=0, tiled=True)[None].astype(F32)  66.1 us
    psum x1, blocking collectives, on_device(): tab_sum = lax.psum(g_tab, ('section', 'dp'))  40.9 us
    psum x1, blocking collectives, on_device(): norm_sum = lax.psum(g_norm, 'dp').T  26.8 us
    convert_element_type x4, other arithmetic, on_device(): lax.psum_scatter(g, 'dp', scatter_dimension=0, tiled=True)[None].astype(F32)  6.99 us
  transfers between devices with their start and end apart: 4, of which 2 were waited for; matrix products, arithmetic and copies ran while one was open for 2% of the time, Pallas kernels for 0%

profile of v2, /device:TPU:0, one launch (start us, length us, event | category | flops | bytes accessed | tf_op | source)
XLA Modules:
  0.0 315.1 jit_solution(15921086795015953515)
XLA Ops:
  7.2 0.0 reduce-scatter.11.cloned.1.call-start
  7.2 0.8 copy.27
  8.0 1.3 copy.28.posn
  9.3 0.1 pad.3.clone
  9.4 1.3 maximum_convert_fusion.norms
  10.7 1.4 maximum_bitcast_fusion.tab
  12.1 149.0 %sections.1 = (bf16[512,768]{1,0:T(8,128)(2,1)}, bf16[512,768]{1,0:T(8,128)(2,1)}, bf16[768,2304]{1,0:T(8,128)(2,1)}, bf16[768,768]{1,0:T(8,128)(2,1)}, bf16[768...) custom-call(s32[4]{0:T(128)} %group.1, s32[2]{0:T(128)} %counts.1, ...), custom_call_target="tpu_custom_call" | custom-call | tf_op jit(solution)/shard_map/sections/pallas_call | solution.py:419
  161.1 0.0 reduce-scatter.11.cloned.1.call-update
  161.1 0.0 reduce-scatter.9.cloned.1.call-start
  161.1 0.7 reduce-scatter.9.cloned.1.call-update
  161.8 0.0 reduce-scatter.7.cloned.1.call-start
  161.9 0.7 reduce-scatter.7.cloned.1.call-update
  162.6 0.0 reduce-scatter.5.cloned.1.call-start
  162.6 0.0 copy-start.2
  162.6 0.0 copy-start.3
  162.6 0.5 reduce-scatter.5.cloned.1.call-update
  163.2 0.4 copy-done.2
  163.5 40.9 %psum.15 = f32[256,32]{1,0:T(8,128)S(1)} all-reduce(f32[256,32]{1,0:T(8,128)S(1)} %copy-done.2), channel_id=1, replica_groups=mesh['section'=4,'dp'=8] {'section','dp'}, use_global_device_ids=true, to_apply=%region_5.0 | all-reduce | flops 8192 | bytes 65536 | tf_op jit(solution)/shard_map/psum | solution.py:448
  204.5 0.0 copy-done.3
  204.5 26.8 %psum.14 = f32[4,768]{1,0:T(4,128)S(1)} all-reduce(f32[4,768]{1,0:T(4,128)S(1)} %copy-done.3), channel_id=1, replica_groups=mesh['section'=4,'dp'=8] {'dp'}, use_global_device_ids=true, to_apply=%region_4.0 | all-reduce | flops 3072 | bytes 24576 | tf_op jit(solution)/shard_map/psum | solution.py:445
  231.3 0.1 dynamic-slice_bitcast_fusion
  231.4 0.6 constant_dynamic-slice_fusion
  232.0 0.6 constant_dynamic-slice_fusion.1
  232.6 0.6 constant_dynamic-slice_fusion.2
  233.2 0.6 fusion
  233.7 0.0 reduce-scatter.11.cloned.1.call-done
  233.7 1.6 bitcast_convert_fusion.1
  235.4 0.0 copy-start.1
  235.4 0.0 reduce-scatter.9.cloned.1.call-done
  235.4 1.7 bitcast_convert_fusion.2
  237.1 23.7 %reduce-scatter.7.cloned.1.call-done = bf16[96,768]{1,0:T(8,128)(2,1)} async-done(((bf16[768,768]{1,0:T(8,128)(2,1)}), bf16[96,768]{1,0:T(8,128)(2,1)}) %reduce-scatter.7.cloned.1.call-update) | async-done | bytes 147472 | tf_op jit(solution)/shard_map/reduce_scatter | solution.py:444
  260.8 1.6 bitcast_convert_fusion.3
  262.4 0.0 copy-start
  262.4 42.4 %reduce-scatter.5.cloned.1.call-done = bf16[96,2304]{1,0:T(8,128)(2,1)} async-done(((bf16[768,2304]{1,0:T(8,128)(2,1)}), bf16[96,2304]{1,0:T(8,128)(2,1)}) %reduce-scatter.5.cloned.1.call-update) | async-done | bytes 442384 | tf_op jit(solution)/shard_map/reduce_scatter | solution.py:444
  304.9 2.0 bitcast_convert_fusion
  306.8 0.0 copy-done.1
  306.8 0.9 copy.31
  307.7 0.0 copy-done
  307.7 0.9 copy.32
  (1 shorter events, 0.0 us)
Async XLA Ops:
  7.2 226.6 %reduce-scatter.11.cloned.1.call-start = ((), (), s32[]{:S(2)}) async-start(), calls=%async_computation.7 | async-start | bytes 1327104 | tf_op jit(solution)/shard_map/reduce_scatter | solution.py:444
  161.1 74.3 %reduce-scatter.9.cloned.1.call-start = ((), (), s32[]{:S(2)}) async-start(), calls=%async_computation.6 | async-start | bytes 1327104 | tf_op jit(solution)/shard_map/reduce_scatter | solution.py:444
  161.8 99.0 %reduce-scatter.7.cloned.1.call-start = ((), (), s32[]{:S(2)}) async-start(), calls=%async_computation.5 | async-start | bytes 1327104 | tf_op jit(solution)/shard_map/reduce_scatter | solution.py:444
  162.6 142.3 %reduce-scatter.5.cloned.1.call-start = ((), (), s32[]{:S(2)}) async-start(), calls=%async_computation.4 | async-start | bytes 3981312 | tf_op jit(solution)/shard_map/reduce_scatter | solution.py:444
  162.6 0.9 copy-start.2
  162.6 41.8 %copy-start.3 = (f32[4,768]{1,0:T(4,128)S(1)}, f32[4,768]{1,0:T(4,128)}, u32[]{:S(2)}) copy-start(f32[4,768]{1,0:T(4,128)} %get-tuple-element.25) | copy-start | bytes 36868
  235.4 71.4 %copy-start.1 = (bf16[512,768]{1,0:T(8,128)(2,1)S(1)}, bf16[512,768]{1,0:T(8,128)(2,1)}, u32[]{:S(2)}) copy-start(bf16[512,768]{1,0:T(8,128)(2,1)} %get-tuple-element.19) | copy-start | bytes 2359300
  262.4 45.3 %copy-start = (bf16[512,768]{1,0:T(8,128)(2,1)S(1)}, bf16[512,768]{1,0:T(8,128)(2,1)}, u32[]{:S(2)}) copy-start(bf16[512,768]{1,0:T(8,128)(2,1)} %get-tuple-element.20) | copy-start | bytes 2359300
Sparse Core Ops, SparseCore 0:
  161.2 32.1 reduce-scatter.10
  195.7 31.4 reduce-scatter.8
  229.5 31.3 reduce-scatter.6
  263.0 41.8 reduce-scatter.4

commit v3 on v2

--- a/solution.py
+++ b/solution.py
@@ -91,13 +91,26 @@
 
 
 def body(
-    sections, micro, atoms, heads, kern, spd, edges,
+    sections, chips, micro, atoms, heads, kern, spd, edges,
     group, counts, tokens, cot, posn, path_in, edge_in, win, wout, wup, wdown, norms, tab,
-    hidden, igrad, g_in, g_out, g_up, g_down, g_norm, g_tab,
-    xs, grecv, a_s, qkv_s, o_s, mid_s, c_s, u_s, act_s, df_s, du_s, dat_s, dqkv_s,
-    pairs, probs, dist_s, path_s, edge_s, tr_b, tr_f, dk_s, dv_s, left_s,
-    fsend, frecv, bsend, brecv,
+    *refs,
 ):
+    hidden, igrad, *refs = refs
+    if chips:
+        (s_in, s_out, s_up, s_down, s_norm, s_tab, grads, g_norm, g_tab, *refs) = refs
+    else:
+        (grads, g_norm, g_tab, *refs) = refs
+    (
+        xs, grecv, a_s, qkv_s, o_s, mid_s, c_s, u_s, act_s, df_s, du_s, dat_s, dqkv_s,
+        pairs, probs, dist_s, path_s, edge_s, tr_b, tr_f, dk_s, dv_s, left_s,
+        fsend, frecv, bsend, brecv, *refs,
+    ) = refs
+    if chips:
+        (
+            core_in, line_in, norm_core, norm_sum, norm_in, tab_own, tab_core, tab_sum, tab_sec, tab_line,
+            core_send, core_recv, line_send, line_recv, back_send, back_recv,
+            nc_sem, nz_send, nz_recv, tc_sem, ts_send, ts_recv, tz_send, tz_recv,
+        ) = refs
     width = wout.shape[0]
     head_dim = width // heads
     scale = 1.0 / math.sqrt(head_dim)
@@ -106,7 +119,26 @@
     d = lax.axis_index("dp") if sections > 1 else 0
     last = s == sections - 1
 
-    if sections > 1:
+    z, c = d // 2, d % 2
+
+    def to(sec, dp, src, dst, send, recv):
+        return pltpu.make_async_remote_copy(
+            src_ref=src, dst_ref=dst, send_sem=send, recv_sem=recv, device_id=(sec, dp), device_id_type=MESH
+        )
+
+    if chips:
+        barrier = pltpu.get_barrier_semaphore()
+        pl.semaphore_signal(barrier, inc=1, device_id=(s, 2 * z + 1 - c), device_id_type=MESH)
+        for other in range(1, sections):
+            pl.semaphore_signal(
+                barrier, inc=1, device_id=((s + other) % sections, d), device_id_type=MESH
+            )
+        for other in range(1, chips):
+            pl.semaphore_signal(
+                barrier, inc=1, device_id=(s, (d + 2 * other) % (2 * chips)), device_id_type=MESH
+            )
+        pl.semaphore_wait(barrier, sections + chips - 1)
+    elif sections > 1:
         barrier = pltpu.get_barrier_semaphore()
 
         @pl.when(s > 0)
@@ -294,18 +326,188 @@
         out = rows_of(mid_s, m, atoms)[...] + norm_back(da, xh, inv_std, norms[0:1, :])
         rows_of(igrad, m, atoms)[...] = out.astype(BF16)
 
+    parts = grads.shape[-1] // width
+    share = grads.shape[2]
+
+    def chunk(n):
+        return pl.ds(n * width if isinstance(n, int) else pl.multiple_of(n * width, LANES), width)
+
+    def core_copy(n):
+        return to(
+            s, 2 * z + 1 - c, grads.at[:, 1 - c, :, chunk(n)], core_in.at[:, :, chunk(n)],
+            core_send.at[n], core_recv.at[n],
+        )
+
+    def right_copy(n, target):
+        return to(
+            s, jnp.minimum(d + 2, 2 * chips - 1), grads.at[target, c, :, chunk(n)],
+            line_in.at[target + 1, :, chunk(n)], line_send.at[n, target], line_recv.at[n, target],
+        )
+
+    def left_copy(n, target):
+        return to(
+            s, jnp.maximum(d - 2, 0), grads.at[target, c, :, chunk(n)],
+            line_in.at[target, :, chunk(n)], back_send.at[n, target], back_recv.at[n, target],
+        )
+
+    def add_in(target, slot, cols):
+        both = grads[target, c, :, cols].astype(F32) + line_in[slot, :, cols].astype(F32)
+        grads[target, c, :, cols] = both.astype(BF16)
+
+    def settle(n):
+        core_copy(n).wait_recv()
+        for target in range(chips):
+            both = grads[target, c, :, chunk(n)].astype(F32) + core_in[target, :, chunk(n)].astype(F32)
+            grads[target, c, :, chunk(n)] = both.astype(BF16)
+
+        @pl.when(z == 0)
+        def _():
+            for target in range(chips - 1, 0, -1):
+                right_copy(n, target).start()
+
+        @pl.when(z == chips - 1)
+        def _():
+            for target in range(chips - 1):
+                left_copy(n, target).start()
+
+    def norm_copy():
+        return to(s, 2 * z + 1 - c, g_norm, norm_core, nc_sem.at[0], nc_sem.at[1])
+
     def weight_grads():
-        for left, right, out in (
-            (act_s, df_s, g_down), (c_s, du_s, g_up), (o_s, dat_s, g_out), (a_s, dqkv_s, g_in),
-        ):
-            for m in range(micro):
-                part = left[m * atoms : (m + 1) * atoms, :].astype(F32)
-                left_s[:, m * atoms : (m + 1) * atoms] = jnp.transpose(part).astype(BF16)
-
-            @pl.loop(0, right.shape[1] // 256)
-            def _(n):
-                cols = pl.ds(pl.multiple_of(n * 256, 256), 256)
-                out[:, cols] = dot(left_s[...], right[:, cols]).astype(out.dtype)
+        if chips:
+            norm_copy().start()
+        jobs = [(act_s, df_s, 0), (c_s, du_s, 0), (o_s, dat_s, 0)] + [(a_s, dqkv_s, q) for q in range(3)]
+        for n, (left, right, col) in enumerate(jobs):
+            if col == 0:
+                for m in range(micro):
+                    part = left[m * atoms : (m + 1) * atoms, :].astype(F32)
+                    left_s[:, m * atoms : (m + 1) * atoms] = jnp.transpose(part).astype(BF16)
+
+            @pl.loop(0, width // 256)
+            def _(q):
+                cols = pl.ds(pl.multiple_of(col * width + q * 256, 256), 256)
+                got = dot(left_s[...], right[:, cols]).astype(BF16)
+                cols = pl.ds(pl.multiple_of(n * width + q * 256, 256), 256)
+                grads[:, :, :, cols] = got.reshape(grads.shape[:3] + (256,))
+
+            if chips:
+                core_copy(n).start()
+                if n:
+                    settle(n - 1)
+        if chips:
+            settle(parts - 1)
+
+    def norm_window(dp):
+        first = jnp.minimum(dp * share // LANES, width // LANES - 2)
+        return pl.ds(pl.multiple_of(first * LANES, LANES), 2 * LANES)
+
+    def norm_line(there, here):
+        return to(
+            s, 2 * there + c, norm_sum.at[:, norm_window(2 * there + c)], norm_in.at[here],
+            nz_send.at[there], nz_recv.at[here],
+        )
+
+    def tab_copy():
+        return to(s, 2 * z + 1 - c, tab_own, tab_core, tc_sem.at[0], tc_sem.at[1])
+
+    def tab_section(there, here):
+        return to(there, d, tab_sum.at[0], tab_sec.at[here], ts_send.at[there], ts_recv.at[here])
+
+    def tab_chip(there, here):
+        return to(s, 2 * there + c, tab_sum.at[1], tab_line.at[here], tz_send.at[there], tz_recv.at[here])
+
+    def others(mine, count, act):
+        for other in range(count):
+            @pl.when(other != mine)
+            def _():
+                act(other)
+
+    def reduce_all():
+        wide_tab = jnp.concatenate(
+            [g_tab[...], jnp.zeros((DEPTH, LANES - heads), F32)], axis=1
+        )
+        tab_own[...] = jnp.transpose(wide_tab)[:heads, :]
+        tab_copy().start()
+        norm_copy().wait_recv()
+        norm_sum[...] = g_norm[...] + norm_core[...]
+        norm_in[z] = norm_sum[:, norm_window(d)]
+        others(z, chips, lambda o: norm_line(o, z).start())
+
+        def relay(n):
+            for target in range(chips - 1, 0, -1):
+                @pl.when((z > 0) & (z < target))
+                def _():
+                    right_copy(n, target).wait_recv()
+                    add_in(target, target + 1, chunk(n))
+                    right_copy(n, target).start()
+
+            for target in range(chips - 1):
+                @pl.when((z < chips - 1) & (z > target))
+                def _():
+                    left_copy(n, target).wait_recv()
+                    add_in(target, target, chunk(n))
+                    left_copy(n, target).start()
+
+            @pl.when(z > 0)
+            def _():
+                right_copy(n, z).wait_recv()
+
+            @pl.when(z < chips - 1)
+            def _():
+                left_copy(n, z).wait_recv()
+
+            cols = chunk(n)
+            mine = grads[z, c, :, cols].astype(F32)
+            mine = mine + jnp.where(z > 0, line_in[z + 1, :, cols].astype(F32), 0.0)
+            mine = mine + jnp.where(z < chips - 1, line_in[z, :, cols].astype(F32), 0.0)
+            return mine
+
+        @pl.loop(0, parts)
+        def _(n):
+            @pl.when(n == 1)
+            def _():
+                tab_copy().wait_recv()
+                tab_sum[0] = tab_own[...] + tab_core[...]
+                tab_sec[s] = tab_sum[0]
+                others(s, sections, lambda o: tab_section(o, s).start())
+
+            @pl.when(n == parts // 2 + 1)
+            def _():
+                others(s, sections, lambda o: tab_section(o, o).wait_recv())
+                tab_sum[1] = sum(tab_sec[o] for o in range(sections))
+                tab_line[z] = tab_sum[1]
+                others(z, chips, lambda o: tab_chip(o, z).start())
+
+            mine = relay(n)
+            for k, (ref, col) in enumerate(
+                [(s_down, 0), (s_up, 0), (s_out, 0)] + [(s_in, q) for q in range(3)]
+            ):
+                @pl.when(n == k)
+                def _():
+                    ref[:, col * width : (col + 1) * width] = mine
+
+        others(z, chips, lambda o: norm_line(o, o).wait_recv())
+        s_norm[...] = sum(norm_in[o] for o in range(chips))
+        others(z, chips, lambda o: tab_chip(o, o).wait_recv())
+        s_tab[...] = sum(tab_line[o] for o in range(chips))
+
+        norm_copy().wait_send()
+        tab_copy().wait_send()
+        others(z, chips, lambda o: norm_line(o, z).wait_send())
+        others(s, sections, lambda o: tab_section(o, s).wait_send())
+        others(z, chips, lambda o: tab_chip(o, z).wait_send())
+
+        @pl.loop(0, parts)
+        def _(n):
+            core_copy(n).wait_send()
+            for target in range(chips):
+                @pl.when(target > z)
+                def _():
+                    right_copy(n, target).wait_send()
+
+                @pl.when(target < z)
+                def _():
+                    left_copy(n, target).wait_send()
 
     heads_up = 2 * micro
     total = 4 * micro + 1
@@ -376,6 +578,9 @@
         def _():
             table_grads(m_tab)
 
+    if chips:
+        reduce_all()
+
     if sections > 1:
         @pl.loop(0, micro)
         def _(m):
@@ -389,7 +594,7 @@
 
 
 def layer_call(
-    sections, grad_type, tokens, cot, posn, group, counts, path_in, edge_in, win, wout, wup, wdown, norms, tab,
+    sections, chips, tokens, cot, posn, group, counts, path_in, edge_in, win, wout, wup, wdown, norms, tab,
     kern, spd, edges,
 ):
     micro, _, atoms = posn.shape
@@ -397,27 +602,44 @@
     heads = tab.shape[0]
     shape = jax.ShapeDtypeStruct
     vmem, smem = pl.BlockSpec(memory_space=pltpu.VMEM), pl.BlockSpec(memory_space=pltpu.SMEM)
-    outs = (
-        shape((rows, width), BF16), shape((rows, width), BF16),
-        shape(win.shape, grad_type), shape(wout.shape, grad_type), shape(wup.shape, grad_type),
-        shape(wdown.shape, grad_type), shape((4, width), F32), shape((DEPTH, heads), F32),
-    )
     low = lambda *dims: pltpu.VMEM(dims, BF16)
     wide = lambda *dims: pltpu.VMEM(dims, F32)
+    sems = lambda *dims: pltpu.SemaphoreType.DMA(dims)
+    parts = 3 + win.shape[1] // width
     pair_rows = heads // 2 * atoms
-    scratch = [
+    outs = [shape((rows, width), BF16), shape((rows, width), BF16)]
+    share = width // (2 * chips) if chips else width
+    grads = (chips, 2, share, parts * width) if chips else (1, 1, width, parts * width)
+    local = [(grads, BF16), ((8, width), F32), ((DEPTH, heads), F32)]
+    scratch = []
+    if chips:
+        outs += [shape((share, w.shape[1]), F32) for w in (win, wout, wup, wdown)]
+        outs += [shape((8, 2 * LANES), F32), shape((heads, DEPTH), F32)]
+        scratch += [pltpu.VMEM(dims, kind) for dims, kind in local]
+    else:
+        outs += [shape(dims, kind) for dims, kind in local]
+    scratch += [
         low(rows, width), low(rows, width), low(rows, width), low(rows, 3 * width), low(rows, width),
         wide(rows, width), low(rows, width), wide(rows, width), low(rows, width), low(rows, width),
         low(rows, width), low(rows, width), low(rows, 3 * width),
         wide(micro, 2 * pair_rows, atoms), low(micro, pair_rows, 2 * atoms),
         wide(micro, atoms, atoms), wide(micro, atoms, atoms), wide(micro, atoms, atoms),
         low(width, atoms), wide(width, atoms), wide(atoms, width), wide(atoms, width), low(width, rows),
-    ] + [pltpu.SemaphoreType.DMA((micro,))] * 4
+    ] + [sems(micro)] * 4
+    if chips:
+        scratch += [
+            low(chips, share, parts * width), low(chips + 1, share, parts * width),
+            wide(8, width), wide(8, width), wide(chips, 8, 2 * LANES),
+            wide(heads, DEPTH), wide(heads, DEPTH), wide(2, heads, DEPTH),
+            wide(sections, heads, DEPTH), wide(chips, heads, DEPTH),
+            sems(parts), sems(parts), sems(parts, chips), sems(parts, chips), sems(parts, chips), sems(parts, chips),
+            sems(2), sems(chips), sems(chips), sems(2), sems(sections), sems(sections), sems(chips), sems(chips),
+        ]
     params = dict(vmem_limit_bytes=60 * 2**20, has_side_effects=True)
     if sections > 1:
         params["collective_id"] = 0
     return pl.pallas_call(
-        functools.partial(body, sections, micro, atoms, heads, kern, spd, edges),
+        functools.partial(body, sections, chips, micro, atoms, heads, kern, spd, edges),
         out_shape=outs,
         in_specs=[smem, smem] + [vmem] * 11,
         out_specs=[vmem] * len(outs),
@@ -431,27 +653,41 @@
     tokens, cotangent, positions, conformer_group, atom_counts, path_dist, edge_kind, attn_in, attn_out,
     ffn_up, ffn_down, norm_gain, norm_shift, kernel_proj, path_table, edge_table,
 ):
-    sections = lax.axis_size("section")
+    sections, count = lax.axis_size("section"), lax.axis_size("dp")
+    section, place = lax.axis_index("section"), lax.axis_index("dp")
     kern, heads = kernel_proj.shape
     spd, edges = path_table.shape[0], edge_table.shape[0]
+    width = attn_out.shape[1]
+    share = width // count
+    chips = count // 2 if count <= 8 and share % 16 == 0 and share <= LANES else 0
     norms = jnp.concatenate([norm_gain[0].T, norm_shift[0].T], axis=0).astype(F32)
     rest = jnp.zeros((DEPTH - kern - spd - edges, heads), BF16)
     tab = jnp.concatenate([kernel_proj, path_table, edge_table, rest], axis=0).T
-    hidden, igrad, *grads, g_norm, g_tab = layer_call(
-        sections, BF16, tokens, cotangent[0], positions, conformer_group, atom_counts, path_dist, edge_kind,
+    hidden, igrad, *sums = layer_call(
+        sections, chips, tokens, cotangent[0], positions, conformer_group, atom_counts, path_dist, edge_kind,
         attn_in[0], attn_out[0], ffn_up[0], ffn_down[0], norms, tab, kern, spd, edges,
     )
-    sums = [lax.psum_scatter(g, "dp", scatter_dimension=0, tiled=True)[None].astype(F32) for g in grads]
-    norm_sum = lax.psum(g_norm, "dp").T
-    share = norm_sum.shape[0] // lax.axis_size("dp")
-    norm_sum = lax.dynamic_slice_in_dim(norm_sum, lax.axis_index("dp") * share, share, 0)[None]
-    tab_sum = lax.psum(g_tab, ("section", "dp"))
+    if chips:
+        *sums, norm_sum, tab_sum = sums
+        first = jnp.minimum(place * share // LANES, width // LANES - 2) * LANES
+        norm_sum = lax.dynamic_slice_in_dim(norm_sum[:4], place * share - first, share, 1).T[None]
+        tab_sum = tab_sum.T
+    else:
+        grads, g_norm, g_tab = sums
+        split = lambda a, n: grads[0, 0, :, a * width : (a + n) * width]
+        sums = [
+            lax.psum_scatter(g, "dp", scatter_dimension=0, tiled=True).astype(F32)
+            for g in (split(3, 3), split(2, 1), split(1, 1), split(0, 1))
+        ]
+        norm_sum = lax.psum(g_norm[:4], "dp").T
+        norm_sum = lax.dynamic_slice_in_dim(norm_sum, place * share, share, 0)[None]
+        tab_sum = lax.psum(g_tab, ("section", "dp"))
     tabs, start = [], 0
-    for count in (kern, spd, edges):
-        own = count // sections
-        tabs.append(lax.dynamic_slice_in_dim(tab_sum, start + lax.axis_index("section") * own, own, 0))
-        start += count
-    return (hidden[None], igrad[None], *sums, norm_sum[:, :, :2], norm_sum[:, :, 2:], *tabs)
+    for rows in (kern, spd, edges):
+        own = rows // sections
+        tabs.append(lax.dynamic_slice_in_dim(tab_sum, start + section * own, own, 0))
+        start += rows
+    return (hidden[None], igrad[None], *(g[None] for g in sums), norm_sum[:, :, :2], norm_sum[:, :, 2:], *tabs)
 
 
 def solution(mesh):

time: 316 us -> 243 us (0.77)
  Pallas kernels: 149 us -> 225 us
  waiting for transfers between devices: 68 us -> 0 us
  blocking collectives: 67.8 us -> 0 us
  between operations: 13.8 us -> 0.71 us
  local copies, waits for them, and re-layouts: 6.73 us -> 14.7 us
  other arithmetic: 9.69 us -> 2.71 us
    pallas_call x1, Pallas kernels: 149 us -> 225 us  [layer_call(): pl.pallas_call(functools.partial(body, sections, chips, micro, atoms, hea...]
    psum x2 -> x0, blocking collectives: 67.8 us -> none  [the longest x1 40.9 us: on_device(): tab_sum = lax.psum(g_tab, ('section', 'dp'))]
    reduce_scatter x4 -> x0, waiting for transfers between devices: 66.1 us -> none  [on_device(): lax.psum_scatter(g, 'dp', scatter_dimension=0, tiled=True)[None].astype(F32)]
    convert_element_type x4 -> x0, other arithmetic: 6.99 us -> none  [on_device(): lax.psum_scatter(g, 'dp', scatter_dimension=0, tiled=True)[None].astype(F32)]
    unnamed x12 -> x21, local copies, waits for them, and re-layouts: 4.21 us -> 10.9 us
  transfers between devices with their start and end apart: 4 -> 0, of which waited for: 2 -> 0; matrix products, arithmetic and copies ran while one was open for 2% -> 0% of each run, Pallas kernels for 0% -> 0%
where the time goes in v3:
time: 243 us
  Pallas kernels  225 us (93%)
  local copies, waits for them, and re-layouts  14.7 us (6%)
  other arithmetic  2.71 us (1%)
    pallas_call x1, Pallas kernels, layer_call(): pl.pallas_call(functools.partial(body, sections, chips, micro, atoms, hea...  225 us
    unnamed x21, local copies, waits for them, and re-layouts  10.9 us

profile of v3, /device:TPU:0, one launch (start us, length us, event | category | flops | bytes accessed | tf_op | source)
XLA Modules:
  0.0 242.8 jit_solution(14315615923827586059)
XLA Ops:
  0.7 0.1 pad.3.clone
  0.8 1.3 copy.28.posn
  2.0 0.8 copy.27
  2.8 1.4 maximum_bitcast_fusion.tab
  4.2 1.3 maximum_convert_fusion.norms
  5.5 224.6 %sections.1 = (bf16[512,768]{1,0:T(8,128)(2,1)}, bf16[512,768]{1,0:T(8,128)(2,1)}, f32[96,2304]{1,0:T(8,128)}, f32[96,768]{1,0:T(8,128)}, f32[96,768]{1,0:T(8,12...) custom-call(s32[4]{0:T(128)} %group.1, s32[2]{0:T(128)} %counts.1, bf16[512,768]{1,0:T(8,128)(2,1)} %tokens.1, ...), custom_call_target="tpu_custom_call" | custom-call | tf_op jit(solution)/shard_map/sections/pallas_call | solution.py:641
  230.2 0.0 copy-start.1
  230.2 0.8 slice.9
  231.0 0.1 dynamic-slice_bitcast_fusion.3
  231.0 0.6 fusion
  231.6 0.8 dynamic-slice_bitcast_fusion
  232.4 0.7 copy.31
  233.1 0.8 dynamic-slice_bitcast_fusion.1
  233.8 0.8 dynamic-slice_bitcast_fusion.2
  234.6 0.7 copy.30
  235.3 0.7 copy.29
  236.0 2.1 copy.38
  238.0 0.0 copy-done.1
  238.0 0.0 copy-start
  238.1 0.9 copy.39
  238.9 0.6 copy-done
  239.5 0.0 copy-start.4
  239.5 0.0 copy-start.3
  239.5 0.0 copy-start.2
  239.5 0.9 copy.40
  240.4 0.2 copy-done.4
  240.6 0.7 copy.41
  241.3 0.0 copy-done.3
  241.3 0.7 copy.42
  242.1 0.0 copy-done.2
  242.1 0.7 copy.43
  (1 shorter events, 0.0 us)
Async XLA Ops:
  230.2 7.9 %copy-start.1 = (bf16[512,768]{1,0:T(8,128)(2,1)S(1)}, bf16[512,768]{1,0:T(8,128)(2,1)}, u32[]{:S(2)}) copy-start(bf16[512,768]{1,0:T(8,128)(2,1)} %get-tuple-element.20) | copy-start | bytes 2359300
  238.0 1.5 copy-start
  239.5 1.1 copy-start.4
  239.5 1.8 copy-start.3
  239.5 2.6 %copy-start.2 = (f32[96,768]{1,0:T(8,128)S(1)}, f32[96,768]{1,0:T(8,128)}, u32[]{:S(2)}) copy-start(f32[96,768]{1,0:T(8,128)} %get-tuple-element.24) | copy-start | bytes 884740

commit v4 on v3

--- a/solution.py
+++ b/solution.py
@@ -17,6 +17,7 @@
 LOG2E = math.log2(math.e)
 LANES = 128
 DEPTH = 256
+LAG = 3
 
 
 def dot(a, b):
@@ -72,6 +73,14 @@
     one = ((lane >= off) & (lane < off + head_dim)).astype(F32).astype(BF16)
     two = ((lane >= off + head_dim) & (lane < off + 2 * head_dim)).astype(F32).astype(BF16)
     return jnp.concatenate([block * one, block * two], axis=0)
+
+
+def tile_pairs(tile, windows):
+    return [
+        (pair, (first - tile) * LANES + off)
+        for pair, (first, tiles, off) in enumerate(windows)
+        if first <= tile < first + tiles
+    ]
 
 
 def features(dist8, path8, edge8, row, spd, edges, kern):
@@ -97,12 +106,12 @@
 ):
     hidden, igrad, *refs = refs
     if chips:
-        (s_in, s_out, s_up, s_down, s_norm, s_tab, grads, g_norm, g_tab, *refs) = refs
+        (sums, s_norm, s_tab, grads, g_norm, g_tab, *refs) = refs
     else:
         (grads, g_norm, g_tab, *refs) = refs
     (
         xs, grecv, a_s, qkv_s, o_s, mid_s, c_s, u_s, act_s, df_s, du_s, dat_s, dqkv_s,
-        pairs, probs, dist_s, path_s, edge_s, tr_b, tr_f, dk_s, dv_s, left_s,
+        pairs, probs, dist_s, path_s, edge_s, tr_b, tr_f, ds_s, left_s,
         fsend, frecv, bsend, brecv, *refs,
     ) = refs
     if chips:
@@ -165,6 +174,12 @@
             device_id=(jnp.maximum(s - 1, 0), d), device_id_type=MESH,
         )
 
+    def head_rows(g, head):
+        return pl.ds(pl.multiple_of((g * 16 + head) * atoms, atoms), atoms)
+
+    def pair_rows(g, pair):
+        return pl.ds(pl.multiple_of((g * 8 + pair) * atoms, atoms), atoms)
+
     @pl.when(s == 0)
     def _():
         xs[...] = tokens[...]
@@ -242,17 +257,18 @@
             for pair, (tile, tiles, off) in enumerate(windows):
                 lane = pl.multiple_of(base + tile * LANES, LANES)
                 span = tiles * LANES
-                rows = pl.ds(pl.multiple_of((g * 8 + pair) * atoms, atoms), atoms)
-                one = pl.ds(pl.multiple_of((g * 8 + pair) * 2 * atoms, atoms), atoms)
-                two = pl.ds(pl.multiple_of((g * 8 + pair) * 2 * atoms + atoms, atoms), atoms)
                 qm = both_heads(qkv[:, pl.ds(lane, span)], off, head_dim)
                 z = dot_nt(qkv[:, pl.ds(width + lane, span)], qm) * (scale * LOG2E)
-                z = z + jnp.concatenate([pairs[m, one, :], pairs[m, two, :]], axis=1)
+                for q in range(2):
+                    pairs[m, head_rows(g, 2 * pair + q), :] += z[:, q * atoms : (q + 1) * atoms]
+            for head in range(16):
+                z = pairs[m, head_rows(g, head), :]
                 e = jnp.exp2(z - jnp.max(z, axis=0, keepdims=True))
                 p = (e * (1.0 / jnp.sum(e, axis=0, keepdims=True))).astype(BF16)
-                probs[m, rows, :] = p
+                probs[m, pair_rows(g, head // 2), head % 2 * atoms : (head % 2 + 1) * atoms] = p
+            for pair in range(8):
                 first = pl.multiple_of(base + pair * 2 * head_dim, 16)
-                got = dot(tr_b[pl.ds(first, 2 * head_dim), :], p)
+                got = dot(tr_b[pl.ds(first, 2 * head_dim), :], probs[m, pair_rows(g, pair), :])
                 tr_f[pl.ds(first, head_dim), :] = got[:head_dim, :atoms]
                 tr_f[pl.ds(pl.multiple_of(first + head_dim, 8), head_dim), :] = got[head_dim:, atoms:]
 
@@ -287,8 +303,6 @@
         dqkv = rows_of(dqkv_s, m, atoms)
         dqkv[:, 0:width] = dot_nt(dat, wout[...]).astype(BF16)
         tr_b[...] = jnp.transpose(qkv[:, width : 2 * width].astype(F32)).astype(BF16)
-        dk_s[...] = jnp.zeros_like(dk_s)
-        dv_s[...] = jnp.zeros_like(dv_s)
 
         @pl.loop(0, heads // 16)
         def _(g):
@@ -296,29 +310,35 @@
             for pair, (tile, tiles, off) in enumerate(windows):
                 lane = pl.multiple_of(base + tile * LANES, LANES)
                 span = tiles * LANES
-                rows = pl.ds(pl.multiple_of((g * 8 + pair) * atoms, atoms), atoms)
-                one = pl.ds(pl.multiple_of((g * 8 + pair) * 2 * atoms, atoms), atoms)
-                two = pl.ds(pl.multiple_of((g * 8 + pair) * 2 * atoms + atoms, atoms), atoms)
                 dom = both_heads(dqkv[:, pl.ds(lane, span)], off, head_dim)
                 dp = dot_nt(qkv[:, pl.ds(2 * width + lane, span)], dom)
-                p_low = probs[m, rows, :]
-                p = p_low.astype(F32)
-                pd = p * dp
+                for q in range(2):
+                    pairs[m, head_rows(g, 2 * pair + q), :] = dp[:, q * atoms : (q + 1) * atoms]
+            for head in range(16):
+                half = pl.ds(head % 2 * atoms, atoms)
+                p = probs[m, pair_rows(g, head // 2), half].astype(F32)
+                pd = p * pairs[m, head_rows(g, head), :]
                 ds = pd - p * jnp.sum(pd, axis=0, keepdims=True)
-                pairs[m, one, :] = ds[:, :atoms]
-                pairs[m, two, :] = ds[:, atoms:]
-                ds_low = ds.astype(BF16)
-                dv_s[:, pl.ds(lane, span)] += dot(p_low, dom)
-                qm = both_heads(qkv[:, pl.ds(lane, span)], off, head_dim)
-                dk_s[:, pl.ds(lane, span)] += dot(ds_low, qm)
+                pairs[m, head_rows(g, head), :] = ds
+                ds_s[head // 2, :, half] = ds.astype(BF16)
+            for tile in range(16 * head_dim // LANES):
+                lane = pl.multiple_of(base + tile * LANES, LANES)
+                inside = tile_pairs(tile, windows)
+                left = jnp.concatenate([probs[m, pair_rows(g, pair), :] for pair, _ in inside], axis=1)
+                block = dqkv[:, pl.ds(lane, LANES)]
+                right = jnp.concatenate([both_heads(block, off, head_dim) for _, off in inside], axis=0)
+                dqkv[:, pl.ds(2 * width + lane, LANES)] = dot(left, right).astype(BF16)
+                left = jnp.concatenate([ds_s[pair] for pair, _ in inside], axis=1)
+                block = qkv[:, pl.ds(lane, LANES)]
+                right = jnp.concatenate([both_heads(block, off, head_dim) for _, off in inside], axis=0)
+                dqkv[:, pl.ds(width + lane, LANES)] = (dot(left, right) * scale).astype(BF16)
+            for pair in range(8):
                 first = pl.multiple_of(base + pair * 2 * head_dim, 16)
-                got = dot(tr_b[pl.ds(first, 2 * head_dim), :], ds_low)
+                got = dot(tr_b[pl.ds(first, 2 * head_dim), :], ds_s[pair])
                 tr_f[pl.ds(first, head_dim), :] = got[:head_dim, :atoms]
                 tr_f[pl.ds(pl.multiple_of(first + head_dim, 8), head_dim), :] = got[head_dim:, atoms:]
 
         dqkv[:, 0:width] = (jnp.transpose(tr_f[...]) * scale).astype(BF16)
-        dqkv[:, width : 2 * width] = (dk_s[...] * scale).astype(BF16)
-        dqkv[:, 2 * width :] = dv_s[...].astype(BF16)
         da = dot_nt(dqkv[...], win[...])
         xh, inv_std = norm_parts(rows_of(xs, m, atoms)[...].astype(F32))
         g_norm[0:1, :] += jnp.sum(da * xh, axis=0, keepdims=True)
@@ -360,15 +380,17 @@
             both = grads[target, c, :, chunk(n)].astype(F32) + core_in[target, :, chunk(n)].astype(F32)
             grads[target, c, :, chunk(n)] = both.astype(BF16)
 
+            @pl.when(z == target)
+            def _():
+                sums[:, chunk(n)] = both
+
         @pl.when(z == 0)
         def _():
-            for target in range(chips - 1, 0, -1):
-                right_copy(n, target).start()
+            right_copy(n, chips - 1).start()
 
         @pl.when(z == chips - 1)
         def _():
-            for target in range(chips - 1):
-                left_copy(n, target).start()
+            left_copy(n, 0).start()
 
     def norm_copy():
         return to(s, 2 * z + 1 - c, g_norm, norm_core, nc_sem.at[0], nc_sem.at[1])
@@ -433,58 +455,72 @@
         norm_in[z] = norm_sum[:, norm_window(d)]
         others(z, chips, lambda o: norm_line(o, z).start())
 
-        def relay(n):
-            for target in range(chips - 1, 0, -1):
-                @pl.when((z > 0) & (z < target))
-                def _():
-                    right_copy(n, target).wait_recv()
-                    add_in(target, target + 1, chunk(n))
-                    right_copy(n, target).start()
-
-            for target in range(chips - 1):
-                @pl.when((z < chips - 1) & (z > target))
-                def _():
-                    left_copy(n, target).wait_recv()
-                    add_in(target, target, chunk(n))
-                    left_copy(n, target).start()
-
-            @pl.when(z > 0)
-            def _():
-                right_copy(n, z).wait_recv()
-
-            @pl.when(z < chips - 1)
-            def _():
-                left_copy(n, z).wait_recv()
-
-            cols = chunk(n)
-            mine = grads[z, c, :, cols].astype(F32)
-            mine = mine + jnp.where(z > 0, line_in[z + 1, :, cols].astype(F32), 0.0)
-            mine = mine + jnp.where(z < chips - 1, line_in[z, :, cols].astype(F32), 0.0)
-            return mine
-
-        @pl.loop(0, parts)
-        def _(n):
-            @pl.when(n == 1)
+        steps = (chips - 1) * parts
+
+        def end_send(i, act):
+            hop, n = i // parts, i % parts
+
+            @pl.when(z == 0)
+            def _():
+                act(right_copy(n, chips - 1 - hop))
+
+            @pl.when(z == chips - 1)
+            def _():
+                act(left_copy(n, hop))
+
+        @pl.loop(0, steps)
+        def _(i):
+            @pl.when(i == 1)
             def _():
                 tab_copy().wait_recv()
                 tab_sum[0] = tab_own[...] + tab_core[...]
                 tab_sec[s] = tab_sum[0]
                 others(s, sections, lambda o: tab_section(o, s).start())
 
-            @pl.when(n == parts // 2 + 1)
+            @pl.when(i == steps - parts)
             def _():
                 others(s, sections, lambda o: tab_section(o, o).wait_recv())
                 tab_sum[1] = sum(tab_sec[o] for o in range(sections))
                 tab_line[z] = tab_sum[1]
                 others(z, chips, lambda o: tab_chip(o, z).start())
 
-            mine = relay(n)
-            for k, (ref, col) in enumerate(
-                [(s_down, 0), (s_up, 0), (s_out, 0)] + [(s_in, q) for q in range(3)]
-            ):
-                @pl.when(n == k)
-                def _():
-                    ref[:, col * width : (col + 1) * width] = mine
+            at_right, at_left = i - LAG * (z - 1), i - LAG * (chips - 2 - z)
+            right, right_n = chips - 1 - at_right // parts, at_right % parts
+            left, left_n = at_left // parts, at_left % parts
+
+            @pl.when((z > 0) & (at_right >= 0) & (z <= right))
+            def _():
+                cols = chunk(right_n)
+                right_copy(right_n, right).wait_recv()
+
+                @pl.when(z < right)
+                def _():
+                    add_in(right, right + 1, cols)
+                    right_copy(right_n, right).start()
+
+                @pl.when(z == right)
+                def _():
+                    sums[:, cols] += line_in[right + 1, :, cols].astype(F32)
+
+            @pl.when((z < chips - 1) & (at_left >= 0) & (z >= left))
+            def _():
+                cols = chunk(left_n)
+                left_copy(left_n, left).wait_recv()
+
+                @pl.when(z > left)
+                def _():
+                    add_in(left, left, cols)
+                    left_copy(left_n, left).start()
+
+                @pl.when(z == left)
+                def _():
+                    sums[:, cols] += line_in[left, :, cols].astype(F32)
+
+            end_send(i, lambda copy: copy.wait_send())
+
+            @pl.when(i + parts < steps)
+            def _():
+                end_send(i + parts, lambda copy: copy.start())
 
         others(z, chips, lambda o: norm_line(o, o).wait_recv())
         s_norm[...] = sum(norm_in[o] for o in range(chips))
@@ -501,11 +537,11 @@
         def _(n):
             core_copy(n).wait_send()
             for target in range(chips):
-                @pl.when(target > z)
+                @pl.when((target > z) & (z > 0))
                 def _():
                     right_copy(n, target).wait_send()
 
-                @pl.when(target < z)
+                @pl.when((target < z) & (z < chips - 1))
                 def _():
                     left_copy(n, target).wait_send()
 
@@ -606,14 +642,14 @@
     wide = lambda *dims: pltpu.VMEM(dims, F32)
     sems = lambda *dims: pltpu.SemaphoreType.DMA(dims)
     parts = 3 + win.shape[1] // width
-    pair_rows = heads // 2 * atoms
+    all_pairs = heads // 2 * atoms
     outs = [shape((rows, width), BF16), shape((rows, width), BF16)]
     share = width // (2 * chips) if chips else width
     grads = (chips, 2, share, parts * width) if chips else (1, 1, width, parts * width)
     local = [(grads, BF16), ((8, width), F32), ((DEPTH, heads), F32)]
     scratch = []
     if chips:
-        outs += [shape((share, w.shape[1]), F32) for w in (win, wout, wup, wdown)]
+        outs += [shape((share, parts * width), F32)]
         outs += [shape((8, 2 * LANES), F32), shape((heads, DEPTH), F32)]
         scratch += [pltpu.VMEM(dims, kind) for dims, kind in local]
     else:
@@ -622,9 +658,9 @@
         low(rows, width), low(rows, width), low(rows, width), low(rows, 3 * width), low(rows, width),
         wide(rows, width), low(rows, width), wide(rows, width), low(rows, width), low(rows, width),
         low(rows, width), low(rows, width), low(rows, 3 * width),
-        wide(micro, 2 * pair_rows, atoms), low(micro, pair_rows, 2 * atoms),
+        wide(micro, 2 * all_pairs, atoms), low(micro, all_pairs, 2 * atoms),
         wide(micro, atoms, atoms), wide(micro, atoms, atoms), wide(micro, atoms, atoms),
-        low(width, atoms), wide(width, atoms), wide(atoms, width), wide(atoms, width), low(width, rows),
+        low(width, atoms), wide(width, atoms), low(8, atoms, 2 * atoms), low(width, rows),
     ] + [sems(micro)] * 4
     if chips:
         scratch += [
@@ -649,6 +685,51 @@
     )(group, counts, tokens, cot, posn, path_in, edge_in, win, wout, wup, wdown, norms, tab)
 
 
+def finish_body(
+    width, kern, spd, edges, sections,
+    place, hidden, igrad, sums, norm, tab,
+    hidden_o, igrad_o, in_o, out_o, up_o, down_o, gain_o, shift_o, kern_o, path_o, edge_o, tab_s, norm_s,
+):
+    hidden_o[...] = hidden[...]
+    igrad_o[...] = igrad[...]
+    down_o[...] = sums[:, 0:width]
+    up_o[...] = sums[:, width : 2 * width]
+    out_o[...] = sums[:, 2 * width : 3 * width]
+    in_o[...] = sums[:, 3 * width :]
+    norm_s[...] = jnp.transpose(norm[...])
+    rows = norm_s[pl.ds(pl.multiple_of(place[1], 8), gain_o.shape[0]), :]
+    gain_o[...] = rows[:, 0:2]
+    shift_o[...] = rows[:, 2:4]
+    tab_s[...] = jnp.transpose(tab[...])
+    start = 0
+    for count, ref in ((kern, kern_o), (spd, path_o), (edges, edge_o)):
+        own = count // sections
+        ref[...] = tab_s[pl.ds(pl.multiple_of(start + place[0] * own, 8), own), :]
+        start += count
+
+
+def finish(hidden, igrad, sums, norm, tab, place, kern, spd, edges, sections):
+    width, heads = hidden.shape[1], tab.shape[0]
+    share = sums.shape[0]
+    shape = jax.ShapeDtypeStruct
+    vmem, smem = pl.BlockSpec(memory_space=pltpu.VMEM), pl.BlockSpec(memory_space=pltpu.SMEM)
+    outs = (
+        [shape(hidden.shape, BF16), shape(igrad.shape, BF16), shape((share, sums.shape[1] - 3 * width), F32)]
+        + [shape((share, width), F32)] * 3
+        + [shape((share, 2), F32)] * 2
+        + [shape((count // sections, heads), F32) for count in (kern, spd, edges)]
+    )
+    return pl.pallas_call(
+        functools.partial(finish_body, width, kern, spd, edges, sections),
+        out_shape=outs,
+        in_specs=[smem] + [vmem] * 5,
+        out_specs=[vmem] * len(outs),
+        scratch_shapes=[pltpu.VMEM((DEPTH, heads), F32), pltpu.VMEM((2 * LANES, 8), F32)],
+        compiler_params=pltpu.CompilerParams(vmem_limit_bytes=32 * 2**20),
+        name="finish",
+    )(place, hidden, igrad, sums, norm, tab)
+
+
 def on_device(
     tokens, cotangent, positions, conformer_group, atom_counts, path_dist, edge_kind, attn_in, attn_out,
     ffn_up, ffn_down, norm_gain, norm_shift, kernel_proj, path_table, edge_table,
@@ -668,20 +749,19 @@
         attn_in[0], attn_out[0], ffn_up[0], ffn_down[0], norms, tab, kern, spd, edges,
     )
     if chips:
-        *sums, norm_sum, tab_sum = sums
         first = jnp.minimum(place * share // LANES, width // LANES - 2) * LANES
-        norm_sum = lax.dynamic_slice_in_dim(norm_sum[:4], place * share - first, share, 1).T[None]
-        tab_sum = tab_sum.T
-    else:
-        grads, g_norm, g_tab = sums
-        split = lambda a, n: grads[0, 0, :, a * width : (a + n) * width]
-        sums = [
-            lax.psum_scatter(g, "dp", scatter_dimension=0, tiled=True).astype(F32)
-            for g in (split(3, 3), split(2, 1), split(1, 1), split(0, 1))
-        ]
-        norm_sum = lax.psum(g_norm[:4], "dp").T
-        norm_sum = lax.dynamic_slice_in_dim(norm_sum, place * share, share, 0)[None]
-        tab_sum = lax.psum(g_tab, ("section", "dp"))
+        where = jnp.stack([section, place * share - first]).astype(jnp.int32)
+        outs = finish(hidden, igrad, *sums, where, kern, spd, edges, sections)
+        return tuple(o[None] for o in outs[:8]) + tuple(outs[8:])
+    grads, g_norm, g_tab = sums
+    split = lambda a, n: grads[0, 0, :, a * width : (a + n) * width]
+    sums = [
+        lax.psum_scatter(g, "dp", scatter_dimension=0, tiled=True).astype(F32)
+        for g in (split(3, 3), split(2, 1), split(1, 1), split(0, 1))
+    ]
+    norm_sum = lax.psum(g_norm[:4], "dp").T
+    norm_sum = lax.dynamic_slice_in_dim(norm_sum, place * share, share, 0)[None]
+    tab_sum = lax.psum(g_tab, ("section", "dp"))
     tabs, start = [], 0
     for rows in (kern, spd, edges):
         own = rows // sections

time: 243 us -> 205 us (0.84)
  Pallas kernels: 225 us -> 192 us
  local copies, waits for them, and re-layouts: 14.7 us -> 8.61 us
    pallas_call x1, Pallas kernels: 225 us -> 190 us  [layer_call(): pl.pallas_call(functools.partial(body, sections, chips, micro, atoms, hea...]
    unnamed x21 -> x14, local copies, waits for them, and re-layouts: 10.9 us -> 8.53 us
where the time goes in v4:
time: 205 us; the launch traced here: 204 us
  Pallas kernels  192 us (94%)
  local copies, waits for them, and re-layouts  8.61 us (4%)
  other arithmetic  2.79 us (1%)
    pallas_call x1, Pallas kernels, layer_call(): pl.pallas_call(functools.partial(body, sections, chips, micro, atoms, hea...  190 us
    unnamed x14, local copies, waits for them, and re-layouts  8.53 us

profile of v4, /device:TPU:0, one launch (start us, length us, event | category | flops | bytes accessed | tf_op | source)
XLA Modules:
  0.0 204.1 jit_solution(8010201549648004940)
XLA Ops:
  0.7 0.1 pad_add_fusion.place
  0.7 0.1 pad.3.clone
  0.8 1.3 copy.28.posn
  2.1 0.8 copy.27
  2.9 1.4 maximum_bitcast_fusion.tab
  4.3 1.3 maximum_convert_fusion.norms
  5.6 189.6 %sections.1 = (bf16[512,768]{1,0:T(8,128)(2,1)}, bf16[512,768]{1,0:T(8,128)(2,1)}, f32[96,4608]{1,0:T(8,128)}, f32[8,256]{1,0:T(8,128)}, f32[32,256]{1,0:T(8,128)}) custom-call(s32[4]{0:T(128)} %group.1, s32[2]{0:T(128)} %counts.1, bf16[512,768]{1,0:T(8,128)(2,1)} %tokens.1, bf16[512,768]{1,0:T(8,128)(2,1)} %bitcast.29, f32[4,3,128]{2,1,0:T(4,128)} %copy.28.posn, ...), custom_call_target="tpu_custom_call" | custom-call | tf_op jit(solution)/shard_map/sections/pallas_call | solution.py:677
  195.2 0.0 copy-start
  195.2 1.5 copy-done
  196.7 0.0 copy-start.1
  196.7 1.1 copy-done.1
  197.8 0.0 copy-start.2
  197.9 1.1 copy-done.2
  199.0 0.0 copy-start.3
  199.0 0.8 copy-done.3
  199.7 0.0 copy-start.4
  199.7 0.7 copy-done.4
  200.4 2.4 %finish.1 = (bf16[512,768]{1,0:T(8,128)(2,1)}, bf16[512,768]{1,0:T(8,128)(2,1)}, f32[96,2304]{1,0:T(8,128)}, f32[96,768]{1,0:T(8,128)}, f32[96,768]{1,0:T(8,128)...) custom-call(s32[2]{0:T(128)S(1)} %pad_add_fusion.place, ...), custom_call_target="tpu_custom_call" | custom-call | tf_op jit(solution)/shard_map/finish/pallas_call | solution.py:722
  202.9 0.6 copy.29
  203.5 0.6 copy.30
  (1 shorter events, 0.0 us)
Async XLA Ops:
  195.2 1.5 copy-start
  196.7 1.1 copy-start.1
  197.8 1.1 copy-start.2
  199.0 0.8 copy-start.3
  199.7 0.7 copy-start.4

commit v5 on v4

--- a/solution.py
+++ b/solution.py
@@ -101,7 +101,8 @@
 
 def body(
     sections, chips, micro, atoms, heads, kern, spd, edges,
-    group, counts, tokens, cot, posn, path_in, edge_in, win, wout, wup, wdown, norms, tab,
+    group, counts, posn, path_in, edge_in, gains, shifts, kern_in, path_tab, edge_tab,
+    tokens, cot_in, win_in, wout_in, wup_in, wdown_in,
     *refs,
 ):
     hidden, igrad, *refs = refs
@@ -112,7 +113,7 @@
     (
         xs, grecv, a_s, qkv_s, o_s, mid_s, c_s, u_s, act_s, df_s, du_s, dat_s, dqkv_s,
         pairs, probs, dist_s, path_s, edge_s, tr_b, tr_f, ds_s, left_s,
-        fsend, frecv, bsend, brecv, *refs,
+        cot, win, wout, wup, wdown, norms, tab_f, tab, load_sem, fsend, frecv, bsend, brecv, *refs,
     ) = refs
     if chips:
         (
@@ -180,9 +181,30 @@
     def pair_rows(g, pair):
         return pl.ds(pl.multiple_of((g * 8 + pair) * atoms, atoms), atoms)
 
+    loads = [(win_in, win), (wout_in, wout), (wup_in, wup), (wdown_in, wdown), (cot_in, cot)]
+
+    def load(k):
+        return pltpu.make_async_copy(*loads[k], load_sem.at[k])
+
+    def load_tokens():
+        return pltpu.make_async_copy(tokens, xs, load_sem.at[len(loads)])
+
     @pl.when(s == 0)
     def _():
-        xs[...] = tokens[...]
+        load_tokens().start()
+
+    for k in range(len(loads)):
+        load(k).start()
+
+    norms[0:2, :] = gains[...].astype(F32)
+    norms[2:4, :] = shifts[...].astype(F32)
+    square = jnp.concatenate([edge_tab[...].astype(F32), jnp.zeros((heads, LANES - heads), F32)], axis=1)
+    square = jnp.concatenate([square, jnp.zeros((LANES - edges, LANES), F32)], axis=0)
+    tab_f[...] = jnp.zeros_like(tab_f)
+    tab_f[:, 0:kern] = kern_in[...].astype(F32)
+    tab_f[:, kern : kern + spd] = path_tab[...].astype(F32)
+    tab_f[:, kern + spd : kern + spd + edges] = jnp.transpose(square)[:heads, :edges]
+    tab[...] = tab_f[...].astype(BF16)
 
     @pl.when(last)
     def _():
@@ -191,22 +213,28 @@
     g_norm[...] = jnp.zeros_like(g_norm)
     g_tab[...] = jnp.zeros_like(g_tab)
 
-    def make_bias(m):
+    def make_bias(unit):
+        m, half = unit // 2, unit % 2
         mol = group[m]
         count = counts[mol]
-        pos = posn[m]
-        pos_t = jnp.transpose(jnp.concatenate([pos, jnp.zeros((5, atoms), F32)], axis=0))
-        total = jnp.zeros((atoms, atoms), F32)
-        for axis in range(3):
-            diff = pos_t[:, axis : axis + 1] - pos[axis : axis + 1, :]
-            total = total + diff * diff
-        dist_s[m] = jnp.sqrt(total)
-        path_s[m] = jnp.transpose(path_in[mol].astype(F32))
-        edge_s[m] = jnp.transpose(edge_in[mol].astype(F32))
+
+        @pl.when(half == 0)
+        def _():
+            pos = jnp.concatenate([posn[axis, pl.ds(m, 1), :] for axis in range(3)], axis=0)
+            pos_t = jnp.transpose(jnp.concatenate([pos, jnp.zeros((5, atoms), F32)], axis=0))
+            total = jnp.zeros((atoms, atoms), F32)
+            for axis in range(3):
+                diff = pos_t[:, axis : axis + 1] - pos[axis : axis + 1, :]
+                total = total + diff * diff
+            dist_s[m] = jnp.sqrt(total)
+            path_s[m] = jnp.transpose(path_in[mol].astype(F32))
+            edge_s[m] = jnp.transpose(edge_in[mol].astype(F32))
+
         out_ref = pairs.at[m]
 
-        @pl.loop(0, atoms // 8)
-        def _(t):
+        @pl.loop(0, atoms // 16)
+        def _(step):
+            t = half * (atoms // 16) + step
             eight = pl.ds(pl.multiple_of(t * 8, 8), 8)
             d8, p8, e8 = dist_s[m, eight, :], path_s[m, eight, :], edge_s[m, eight, :]
             for r in range(0, 8, 2):
@@ -219,25 +247,21 @@
                     row = jnp.where(j < count, got[:, q * atoms : (q + 1) * atoms], NEG_BIG)
                     out_ref[pl.ds(j, heads, stride=atoms), :] = row
 
-    def table_grads(m):
+    tab_blocks = micro * (atoms // 8)
+
+    def table_grads(block):
+        m, t = block // (atoms // 8), block % (atoms // 8)
         in_ref = pairs.at[m]
-
-        def step(t, acc):
-            eight = pl.ds(pl.multiple_of(t * 8, 8), 8)
-            d8, p8, e8 = dist_s[m, eight, :], path_s[m, eight, :], edge_s[m, eight, :]
-            for r in range(0, 8, 2):
-                feats = jnp.concatenate(
-                    [features(d8, p8, e8, r + q, spd, edges, kern) for q in range(2)], axis=1
-                )
-                halves = []
-                for q in range(2):
-                    j = t * 8 + r + q
-                    halves.append(in_ref[pl.ds(j, heads, stride=atoms), :])
-                ds = jnp.concatenate(halves, axis=1).astype(BF16)
-                acc = acc + dot_nt(feats, ds)
-            return acc
-
-        g_tab[...] += lax.fori_loop(0, atoms // 8, step, jnp.zeros((DEPTH, heads), F32))
+        eight = pl.ds(pl.multiple_of(t * 8, 8), 8)
+        d8, p8, e8 = dist_s[m, eight, :], path_s[m, eight, :], edge_s[m, eight, :]
+        acc = jnp.zeros((DEPTH, heads), F32)
+        for r in range(0, 8, 2):
+            feats = jnp.concatenate(
+                [features(d8, p8, e8, r + q, spd, edges, kern) for q in range(2)], axis=1
+            )
+            halves = [in_ref[pl.ds(t * 8 + r + q, heads, stride=atoms), :] for q in range(2)]
+            acc = acc + dot_nt(feats, jnp.concatenate(halves, axis=1).astype(BF16))
+        g_tab[...] += acc
 
     def forward(m):
         x = rows_of(xs, m, atoms)[...].astype(F32)
@@ -445,17 +469,14 @@
                 act(other)
 
     def reduce_all():
-        wide_tab = jnp.concatenate(
-            [g_tab[...], jnp.zeros((DEPTH, LANES - heads), F32)], axis=1
-        )
-        tab_own[...] = jnp.transpose(wide_tab)[:heads, :]
-        tab_copy().start()
         norm_copy().wait_recv()
         norm_sum[...] = g_norm[...] + norm_core[...]
         norm_in[z] = norm_sum[:, norm_window(d)]
         others(z, chips, lambda o: norm_line(o, z).start())
 
         steps = (chips - 1) * parts
+        tab_steps = steps - 6
+        tab_each = -(-tab_blocks // tab_steps)
 
         def end_send(i, act):
             hop, n = i // parts, i % parts
@@ -470,14 +491,26 @@
 
         @pl.loop(0, steps)
         def _(i):
-            @pl.when(i == 1)
+            @pl.when(i < tab_steps)
+            def _():
+                @pl.loop(i * tab_each, jnp.minimum((i + 1) * tab_each, tab_blocks))
+                def _(block):
+                    table_grads(block)
+
+            @pl.when(i == tab_steps)
+            def _():
+                wide_tab = jnp.concatenate([g_tab[...], jnp.zeros((DEPTH, LANES - heads), F32)], axis=1)
+                tab_own[...] = jnp.transpose(wide_tab)[:heads, :]
+                tab_copy().start()
+
+            @pl.when(i == tab_steps + 1)
             def _():
                 tab_copy().wait_recv()
                 tab_sum[0] = tab_own[...] + tab_core[...]
                 tab_sec[s] = tab_sum[0]
                 others(s, sections, lambda o: tab_section(o, s).start())
 
-            @pl.when(i == steps - parts)
+            @pl.when(i == tab_steps + 3)
             def _():
                 others(s, sections, lambda o: tab_section(o, o).wait_recv())
                 tab_sum[1] = sum(tab_sec[o] for o in range(sections))
@@ -545,43 +578,37 @@
                 def _():
                     left_copy(n, target).wait_send()
 
-    heads_up = 2 * micro
-    total = 4 * micro + 1
+    total = 4 * micro
 
     @pl.loop(0, total)
     def _(t):
-        first = s == 0
-        tail = t - heads_up
-        is_bias = jnp.where(first, (t < heads_up) & (t % 2 == 0), t < micro)
+        ahead = jnp.where(last, micro, jnp.minimum(micro, jnp.where(s == 0, 1, 2 * s * s)))
+        gap = micro - ahead
+        r = t - 2 * ahead
+        mixed = (r >= 0) & (r < 3 * gap)
+        unit = jnp.where(r < 0, t, 2 * (ahead + r // 3) + r % 3 - 1)
+        is_bias = (r < 0) | (mixed & (r % 3 != 0))
         is_fwd = jnp.where(
-            last,
-            (t >= micro) & (t < 3 * micro) & ((t - micro) % 2 == 0),
-            jnp.where(first, (t < heads_up) & (t % 2 == 1), (t >= micro) & (t < heads_up)),
+            last, (r >= 0) & (r % 2 == 0), (mixed & (r % 3 == 0)) | ((r >= 3 * gap) & (t < 3 * micro))
         )
-        is_back = jnp.where(
-            last,
-            (t >= micro) & (t < 3 * micro) & ((t - micro) % 2 == 1),
-            (tail >= 0) & (tail < 2 * micro - 1) & (tail % 2 == 0),
-        )
-        is_sum = jnp.where(last, t == 3 * micro, tail == 2 * micro - 1)
-        is_tab = jnp.where(
-            last,
-            t > 3 * micro,
-            ((tail >= 0) & (tail < 2 * micro - 1) & (tail % 2 == 1)) | (tail == 2 * micro),
-        )
-        m_bias = jnp.where(first, t // 2, t)
-        m_fwd = jnp.where(last, (t - micro) // 2, jnp.where(first, t // 2, t - micro))
-        m_back = jnp.where(last, (t - micro) // 2, tail // 2)
-        m_tab = jnp.where(last, t - 3 * micro - 1, jnp.where(tail == 2 * micro, micro - 1, tail // 2))
-        if sections == 1:
-            is_bias, m_bias = t < micro, t
-
+        m_fwd = jnp.where(last, r // 2, jnp.where(mixed, r // 3, r - 2 * gap))
+        is_back = jnp.where(last, (r >= 0) & (r % 2 == 1), t >= 3 * micro)
+        m_back = jnp.where(last, r // 2, t - 3 * micro)
         @pl.when(is_bias)
         def _():
-            make_bias(m_bias)
+            make_bias(unit)
 
         @pl.when(is_fwd)
         def _():
+            @pl.when(m_fwd == 0)
+            def _():
+                for k in range(len(loads) - 1):
+                    load(k).wait()
+
+                @pl.when(s == 0)
+                def _():
+                    load_tokens().wait()
+
             if sections > 1:
                 @pl.when(s > 0)
                 def _():
@@ -595,6 +622,10 @@
 
         @pl.when(is_back)
         def _():
+            @pl.when(m_back == 0)
+            def _():
+                load(len(loads) - 1).wait()
+
             if sections > 1:
                 @pl.when(jnp.logical_not(last))
                 def _():
@@ -606,16 +637,11 @@
                 def _():
                     backward_copy(m_back).start()
 
-        @pl.when(is_sum)
-        def _():
-            weight_grads()
-
-        @pl.when(is_tab)
-        def _():
-            table_grads(m_tab)
-
+    weight_grads()
     if chips:
         reduce_all()
+    else:
+        pl.loop(0, tab_blocks)(table_grads)
 
     if sections > 1:
         @pl.loop(0, micro)
@@ -630,12 +656,13 @@
 
 
 def layer_call(
-    sections, chips, tokens, cot, posn, group, counts, path_in, edge_in, win, wout, wup, wdown, norms, tab,
-    kern, spd, edges,
+    sections, chips, tokens, cot, posn, group, counts, path_in, edge_in, win, wout, wup, wdown,
+    norm_gain, norm_shift, kernel_proj, path_table, edge_table,
 ):
     micro, _, atoms = posn.shape
     rows, width = tokens.shape
-    heads = tab.shape[0]
+    kern, heads = kernel_proj.shape
+    spd, edges = path_table.shape[0], edge_table.shape[0]
     shape = jax.ShapeDtypeStruct
     vmem, smem = pl.BlockSpec(memory_space=pltpu.VMEM), pl.BlockSpec(memory_space=pltpu.SMEM)
     low = lambda *dims: pltpu.VMEM(dims, BF16)
@@ -661,6 +688,8 @@
         wide(micro, 2 * all_pairs, atoms), low(micro, all_pairs, 2 * atoms),
         wide(micro, atoms, atoms), wide(micro, atoms, atoms), wide(micro, atoms, atoms),
         low(width, atoms), wide(width, atoms), low(8, atoms, 2 * atoms), low(width, rows),
+        low(rows, width), low(*win.shape), low(*wout.shape), low(*wup.shape), low(*wdown.shape),
+        wide(4, width), wide(heads, DEPTH), low(heads, DEPTH), sems(6),
     ] + [sems(micro)] * 4
     if chips:
         scratch += [
@@ -677,12 +706,15 @@
     return pl.pallas_call(
         functools.partial(body, sections, chips, micro, atoms, heads, kern, spd, edges),
         out_shape=outs,
-        in_specs=[smem, smem] + [vmem] * 11,
+        in_specs=[smem, smem] + [vmem] * 8 + [pl.BlockSpec(memory_space=pl.ANY)] * 6,
         out_specs=[vmem] * len(outs),
         scratch_shapes=scratch,
         compiler_params=pltpu.CompilerParams(**params),
         name="sections",
-    )(group, counts, tokens, cot, posn, path_in, edge_in, win, wout, wup, wdown, norms, tab)
+    )(
+        group, counts, jnp.transpose(posn, (1, 0, 2)), path_in, edge_in, norm_gain.T, norm_shift.T,
+        kernel_proj.T, path_table.T, edge_table, tokens, cot, win, wout, wup, wdown,
+    )
 
 
 def finish_body(
@@ -692,14 +724,15 @@
 ):
     hidden_o[...] = hidden[...]
     igrad_o[...] = igrad[...]
-    down_o[...] = sums[:, 0:width]
-    up_o[...] = sums[:, width : 2 * width]
-    out_o[...] = sums[:, 2 * width : 3 * width]
+    for k, ref in enumerate((down_o, up_o, out_o)):
+        ref[...] = sums[:, k * width : (k + 1) * width]
     in_o[...] = sums[:, 3 * width :]
+    share = gain_o.shape[1]
     norm_s[...] = jnp.transpose(norm[...])
-    rows = norm_s[pl.ds(pl.multiple_of(place[1], 8), gain_o.shape[0]), :]
-    gain_o[...] = rows[:, 0:2]
-    shift_o[...] = rows[:, 2:4]
+    rows = norm_s[pl.ds(pl.multiple_of(place[1], 8), share), :]
+    rows = jnp.transpose(jnp.concatenate([rows, jnp.zeros((share, LANES - 8), F32)], axis=1))
+    gain_o[...] = rows[0:2, :]
+    shift_o[...] = rows[2:4, :]
     tab_s[...] = jnp.transpose(tab[...])
     start = 0
     for count, ref in ((kern, kern_o), (spd, path_o), (edges, edge_o)):
@@ -716,7 +749,7 @@
     outs = (
         [shape(hidden.shape, BF16), shape(igrad.shape, BF16), shape((share, sums.shape[1] - 3 * width), F32)]
         + [shape((share, width), F32)] * 3
-        + [shape((share, 2), F32)] * 2
+        + [shape((2, share), F32)] * 2
         + [shape((count // sections, heads), F32) for count in (kern, spd, edges)]
     )
     return pl.pallas_call(
@@ -725,7 +758,7 @@
         in_specs=[smem] + [vmem] * 5,
         out_specs=[vmem] * len(outs),
         scratch_shapes=[pltpu.VMEM((DEPTH, heads), F32), pltpu.VMEM((2 * LANES, 8), F32)],
-        compiler_params=pltpu.CompilerParams(vmem_limit_bytes=32 * 2**20),
+        compiler_params=pltpu.CompilerParams(vmem_limit_bytes=60 * 2**20),
         name="finish",
     )(place, hidden, igrad, sums, norm, tab)
 
@@ -740,19 +773,18 @@
     spd, edges = path_table.shape[0], edge_table.shape[0]
     width = attn_out.shape[1]
     share = width // count
-    chips = count // 2 if count <= 8 and share % 16 == 0 and share <= LANES else 0
-    norms = jnp.concatenate([norm_gain[0].T, norm_shift[0].T], axis=0).astype(F32)
-    rest = jnp.zeros((DEPTH - kern - spd - edges, heads), BF16)
-    tab = jnp.concatenate([kernel_proj, path_table, edge_table, rest], axis=0).T
+    chips = 4 if count == 8 and share % 16 == 0 and share <= LANES else 0
     hidden, igrad, *sums = layer_call(
         sections, chips, tokens, cotangent[0], positions, conformer_group, atom_counts, path_dist, edge_kind,
-        attn_in[0], attn_out[0], ffn_up[0], ffn_down[0], norms, tab, kern, spd, edges,
+        attn_in[0], attn_out[0], ffn_up[0], ffn_down[0], norm_gain[0], norm_shift[0],
+        kernel_proj, path_table, edge_table,
     )
     if chips:
         first = jnp.minimum(place * share // LANES, width // LANES - 2) * LANES
         where = jnp.stack([section, place * share - first]).astype(jnp.int32)
         outs = finish(hidden, igrad, *sums, where, kern, spd, edges, sections)
-        return tuple(o[None] for o in outs[:8]) + tuple(outs[8:])
+        norms = [jnp.transpose(o) for o in outs[6:8]]
+        return tuple(o[None] for o in [*outs[:6], *norms]) + tuple(outs[8:])
     grads, g_norm, g_tab = sums
     split = lambda a, n: grads[0, 0, :, a * width : (a + n) * width]
     sums = [

time: 205 us -> 179 us (0.87)
  Pallas kernels: 192 us -> 178 us
  local copies, waits for them, and re-layouts: 8.61 us -> 0 us
  other arithmetic: 2.79 us -> 0.66 us
    pallas_call x1, Pallas kernels: 190 us -> 174 us  [layer_call(): pl.pallas_call(functools.partial(body, sections, chips, micro, atoms, hea...]
    unnamed x14 -> x0, local copies, waits for them, and re-layouts: 8.53 us -> none
where the time goes in v5:
time: 179 us
  Pallas kernels  178 us (99%)
    pallas_call x1, Pallas kernels, layer_call(): pl.pallas_call(functools.partial(body, sections, chips, micro, atoms, hea...  174 us
    pallas_call x1, Pallas kernels, finish(): pl.pallas_call(functools.partial(finish_body, width, kern, spd, edges, se...  3.94 us

profile of v5, /device:TPU:0, one launch (start us, length us, event | category | flops | bytes accessed | tf_op | source)
XLA Modules:
  0.0 179.3 jit_solution(17863938603087010824)
XLA Ops:
  0.7 0.7 pad_add_fusion.place
  1.3 174.0 %sections.1 = (bf16[512,768]{1,0:T(8,128)(2,1)}, bf16[512,768]{1,0:T(8,128)(2,1)}, f32[96,4608]{1,0:T(8,128)}, f32[8,256]{1,0:T(8,128)}, f32[32,256]{1,0:T(8,128)}) custom-call(s32[4]{0:T(128)} %group.1, s32[2]{0:T(128)} %counts.1, f32[3,4,128]{2,1,0:T(4,128)} %bitcast.35, s32[2,128,128]{2,1,0:T(8,128)} %path_in.1, s32[2,128,128]{2,1,0:T(8,128)} %edge_in.1, ...), custom_call_target="tpu_custom_call" | custom-call | tf_op jit(solution)/shard_map/sections/pallas_call | solution.py:706
  175.4 3.9 %finish.1 = (bf16[512,768]{1,0:T(8,128)(2,1)}, bf16[512,768]{1,0:T(8,128)(2,1)}, f32[96,2304]{1,0:T(8,128)}, f32[96,768]{1,0:T(8,128)}, f32[96,768]{1,0:T(8,128)...) custom-call(s32[2]{0:T(128)} %pad_add_fusion.place, ...), custom_call_target="tpu_custom_call" | custom-call | tf_op jit(solution)/shard_map/finish/pallas_call | solution.py:755

commit v6 on v5

--- a/solution.py
+++ b/solution.py
@@ -18,6 +18,12 @@
 LANES = 128
 DEPTH = 256
 LAG = 3
+FORWARD_UNIT = 4
+BACKWARD_UNIT = 4
+BIAS_UNIT = 2
+BLOCK = 64
+TABLE_BLOCK = 16
+SLOTS = 4
 
 
 def dot(a, b):
@@ -68,11 +74,32 @@
     return out
 
 
+def in_turn(stages, count, unit):
+    units = count // unit
+    for step in range(units + len(stages) - 1):
+        for late, stage in enumerate(stages):
+            if 0 <= step - late < units:
+                for pair in range((step - late) * unit, (step - late + 1) * unit):
+                    stage(pair)
+
+
 def both_heads(block, off, head_dim):
     lane = lax.broadcasted_iota(jnp.int32, (1, block.shape[1]), 1)
     one = ((lane >= off) & (lane < off + head_dim)).astype(F32).astype(BF16)
     two = ((lane >= off + head_dim) & (lane < off + 2 * head_dim)).astype(F32).astype(BF16)
     return jnp.concatenate([block * one, block * two], axis=0)
+
+
+def both_columns(ref, first, tiles, off, head_dim):
+    span, atoms = tiles * LANES, ref.shape[1]
+    out = []
+    for q in range(2):
+        at = off + q * head_dim
+        own = ref[first + at : first + at + head_dim, :]
+        pieces = [jnp.zeros((at, atoms), F32)] * (at > 0) + [own]
+        pieces += [jnp.zeros((span - at - head_dim, atoms), F32)] * (at + head_dim < span)
+        out.append(jnp.concatenate(pieces, axis=0))
+    return jnp.concatenate(out, axis=1).astype(BF16)
 
 
 def tile_pairs(tile, windows):
@@ -112,7 +139,7 @@
         (grads, g_norm, g_tab, *refs) = refs
     (
         xs, grecv, a_s, qkv_s, o_s, mid_s, c_s, u_s, act_s, df_s, du_s, dat_s, dqkv_s,
-        pairs, probs, dist_s, path_s, edge_s, tr_b, tr_f, ds_s, left_s,
+        pairs, probs, dist_s, path_s, edge_s, tr_b, tr_f, tr_q, feats_s, ds_s, left_s,
         cot, win, wout, wup, wdown, norms, tab_f, tab, load_sem, fsend, frecv, bsend, brecv, *refs,
     ) = refs
     if chips:
@@ -175,11 +202,10 @@
             device_id=(jnp.maximum(s - 1, 0), d), device_id_type=MESH,
         )
 
-    def head_rows(g, head):
-        return pl.ds(pl.multiple_of((g * 16 + head) * atoms, atoms), atoms)
-
-    def pair_rows(g, pair):
-        return pl.ds(pl.multiple_of((g * 8 + pair) * atoms, atoms), atoms)
+    def head_rows(head):
+        return slice(head * atoms, (head + 1) * atoms)
+
+    pair_rows = head_rows
 
     loads = [(win_in, win), (wout_in, wout), (wup_in, wup), (wdown_in, wdown), (cot_in, cot)]
 
@@ -232,36 +258,61 @@
 
         out_ref = pairs.at[m]
 
-        @pl.loop(0, atoms // 16)
+        @pl.loop(0, atoms // 2 // BLOCK)
         def _(step):
-            t = half * (atoms // 16) + step
-            eight = pl.ds(pl.multiple_of(t * 8, 8), 8)
-            d8, p8, e8 = dist_s[m, eight, :], path_s[m, eight, :], edge_s[m, eight, :]
-            for r in range(0, 8, 2):
-                feats = jnp.concatenate(
-                    [features(d8, p8, e8, r + q, spd, edges, kern) for q in range(2)], axis=1
-                )
-                got = dot(tab[...], feats) * LOG2E
+            t = half * (atoms // 2 // BLOCK) + step
+            rows = pl.ds(pl.multiple_of(t * BLOCK, BLOCK), BLOCK)
+            d8, p8, e8 = dist_s[m, rows, :], path_s[m, rows, :], edge_s[m, rows, :]
+
+            def make(r):
                 for q in range(2):
-                    j = t * 8 + r + q
+                    feats_s[r % SLOTS, :, q * atoms : (q + 1) * atoms] = features(
+                        d8, p8, e8, 2 * r + q, spd, edges, kern
+                    )
+
+            def project(r):
+                got = dot(tab[...], feats_s[r % SLOTS]) * LOG2E
+                for q in range(2):
+                    j = t * BLOCK + 2 * r + q
                     row = jnp.where(j < count, got[:, q * atoms : (q + 1) * atoms], NEG_BIG)
                     out_ref[pl.ds(j, heads, stride=atoms), :] = row
 
-    tab_blocks = micro * (atoms // 8)
+            in_turn((make, project), BLOCK // 2, BIAS_UNIT)
+
+    tab_blocks = micro * (atoms // TABLE_BLOCK)
 
     def table_grads(block):
-        m, t = block // (atoms // 8), block % (atoms // 8)
+        m, t = block // (atoms // TABLE_BLOCK), block % (atoms // TABLE_BLOCK)
         in_ref = pairs.at[m]
-        eight = pl.ds(pl.multiple_of(t * 8, 8), 8)
-        d8, p8, e8 = dist_s[m, eight, :], path_s[m, eight, :], edge_s[m, eight, :]
-        acc = jnp.zeros((DEPTH, heads), F32)
-        for r in range(0, 8, 2):
-            feats = jnp.concatenate(
-                [features(d8, p8, e8, r + q, spd, edges, kern) for q in range(2)], axis=1
-            )
-            halves = [in_ref[pl.ds(t * 8 + r + q, heads, stride=atoms), :] for q in range(2)]
-            acc = acc + dot_nt(feats, jnp.concatenate(halves, axis=1).astype(BF16))
-        g_tab[...] += acc
+        rows = pl.ds(pl.multiple_of(t * TABLE_BLOCK, TABLE_BLOCK), TABLE_BLOCK)
+        d8, p8, e8 = dist_s[m, rows, :], path_s[m, rows, :], edge_s[m, rows, :]
+        acc = [jnp.zeros((DEPTH, heads), F32)]
+
+        def make(r):
+            for q in range(2):
+                feats_s[r % SLOTS, :, q * atoms : (q + 1) * atoms] = features(
+                    d8, p8, e8, 2 * r + q, spd, edges, kern
+                )
+
+        def collect(r):
+            halves = [
+                in_ref[pl.ds(t * TABLE_BLOCK + 2 * r + q, heads, stride=atoms), :] for q in range(2)
+            ]
+            acc[0] += dot_nt(feats_s[r % SLOTS], jnp.concatenate(halves, axis=1).astype(BF16))
+
+        in_turn((make, collect), TABLE_BLOCK // 2, BIAS_UNIT)
+        g_tab[...] += acc[0]
+
+    def turned(n):
+        return grads[:, :, :, n * width : (n + 1) * width].reshape(width, width)
+
+    def turn_weights():
+        for n, (ref, col) in enumerate([(wdown, 0), (wup, 0), (wout, 0)] + [(win, q) for q in range(3)]):
+            for k in range(width // 256):
+                block = ref[k * 256 : (k + 1) * 256, col * width : (col + 1) * width].astype(F32)
+                block = jnp.transpose(block).astype(BF16)
+                first = n * width + k * 256
+                grads[:, :, :, first : first + 256] = block.reshape(grads.shape[:3] + (256,))
 
     def forward(m):
         x = rows_of(xs, m, atoms)[...].astype(F32)
@@ -272,29 +323,33 @@
         for blk in range(3):
             got = dot(a, win[:, blk * width : (blk + 1) * width])
             qkv[:, blk * width : (blk + 1) * width] = got.astype(BF16)
+            if blk == 0:
+                tr_q[...] = jnp.transpose(got.astype(BF16).astype(F32))
             if blk == 2:
                 tr_b[...] = jnp.transpose(got).astype(BF16)
 
-        @pl.loop(0, heads // 16)
-        def _(g):
-            base = g * 16 * head_dim
-            for pair, (tile, tiles, off) in enumerate(windows):
-                lane = pl.multiple_of(base + tile * LANES, LANES)
-                span = tiles * LANES
-                qm = both_heads(qkv[:, pl.ds(lane, span)], off, head_dim)
-                z = dot_nt(qkv[:, pl.ds(width + lane, span)], qm) * (scale * LOG2E)
-                for q in range(2):
-                    pairs[m, head_rows(g, 2 * pair + q), :] += z[:, q * atoms : (q + 1) * atoms]
-            for head in range(16):
-                z = pairs[m, head_rows(g, head), :]
+        def scores(pair):
+            g, (tile, tiles, off) = pair // 8, windows[pair % 8]
+            lane = g * 16 * head_dim + tile * LANES
+            qm = both_columns(tr_q, lane, tiles, off, head_dim)
+            z = dot(qkv[:, width + lane : width + lane + tiles * LANES], qm) * (scale * LOG2E)
+            for q in range(2):
+                pairs[m, head_rows(2 * pair + q), :] += z[:, q * atoms : (q + 1) * atoms]
+
+        def softmax(pair):
+            for q in range(2):
+                z = pairs[m, head_rows(2 * pair + q), :]
                 e = jnp.exp2(z - jnp.max(z, axis=0, keepdims=True))
                 p = (e * (1.0 / jnp.sum(e, axis=0, keepdims=True))).astype(BF16)
-                probs[m, pair_rows(g, head // 2), head % 2 * atoms : (head % 2 + 1) * atoms] = p
-            for pair in range(8):
-                first = pl.multiple_of(base + pair * 2 * head_dim, 16)
-                got = dot(tr_b[pl.ds(first, 2 * head_dim), :], probs[m, pair_rows(g, pair), :])
-                tr_f[pl.ds(first, head_dim), :] = got[:head_dim, :atoms]
-                tr_f[pl.ds(pl.multiple_of(first + head_dim, 8), head_dim), :] = got[head_dim:, atoms:]
+                probs[m, pair_rows(pair), q * atoms : (q + 1) * atoms] = p
+
+        def attend(pair):
+            first = pair * 2 * head_dim
+            got = dot(tr_b[first : first + 2 * head_dim, :], probs[m, pair_rows(pair), :])
+            tr_f[first : first + head_dim, :] = got[:head_dim, :atoms]
+            tr_f[first + head_dim : first + 2 * head_dim, :] = got[head_dim:, atoms:]
+
+        in_turn((scores, softmax, attend), heads // 2, FORWARD_UNIT)
 
         o = jnp.transpose(tr_f[...]).astype(BF16)
         rows_of(o_s, m, atoms)[...] = o
@@ -309,13 +364,13 @@
         rows_of(act_s, m, atoms)[...] = act
         rows_of(hidden, m, atoms)[...] = (mid + dot(act, wdown[...])).astype(BF16)
 
-    def backward(m):
+    def backward_ffn(m):
         grad = rows_of(cot, m, atoms)[...].astype(F32) + rows_of(grecv, m, atoms)[...].astype(F32)
         df = grad.astype(BF16)
         rows_of(df_s, m, atoms)[...] = df
-        du = (dot_nt(df, wdown[...]) * gelu_slope(rows_of(u_s, m, atoms)[...])).astype(BF16)
+        du = (dot(df, turned(0)) * gelu_slope(rows_of(u_s, m, atoms)[...])).astype(BF16)
         rows_of(du_s, m, atoms)[...] = du
-        dc = dot_nt(du, wup[...])
+        dc = dot(du, turned(1))
         xh, inv_std = norm_parts(rows_of(mid_s, m, atoms)[...])
         g_norm[1:2, :] += jnp.sum(dc * xh, axis=0, keepdims=True)
         g_norm[3:4, :] += jnp.sum(dc, axis=0, keepdims=True)
@@ -323,47 +378,56 @@
         rows_of(mid_s, m, atoms)[...] = dmid
         dat = dmid.astype(BF16)
         rows_of(dat_s, m, atoms)[...] = dat
+        do = dot(dat, turned(2)).astype(BF16)
+        rows_of(dqkv_s, m, atoms)[:, 0:width] = do
+        tr_q[...] = jnp.transpose(do.astype(F32))
+
+    def backward_attn(m):
         qkv = rows_of(qkv_s, m, atoms)
         dqkv = rows_of(dqkv_s, m, atoms)
-        dqkv[:, 0:width] = dot_nt(dat, wout[...]).astype(BF16)
         tr_b[...] = jnp.transpose(qkv[:, width : 2 * width].astype(F32)).astype(BF16)
 
-        @pl.loop(0, heads // 16)
-        def _(g):
-            base = g * 16 * head_dim
-            for pair, (tile, tiles, off) in enumerate(windows):
-                lane = pl.multiple_of(base + tile * LANES, LANES)
-                span = tiles * LANES
-                dom = both_heads(dqkv[:, pl.ds(lane, span)], off, head_dim)
-                dp = dot_nt(qkv[:, pl.ds(2 * width + lane, span)], dom)
-                for q in range(2):
-                    pairs[m, head_rows(g, 2 * pair + q), :] = dp[:, q * atoms : (q + 1) * atoms]
-            for head in range(16):
-                half = pl.ds(head % 2 * atoms, atoms)
-                p = probs[m, pair_rows(g, head // 2), half].astype(F32)
-                pd = p * pairs[m, head_rows(g, head), :]
+        def slopes(pair):
+            g, (tile, tiles, off) = pair // 8, windows[pair % 8]
+            lane = g * 16 * head_dim + tile * LANES
+            dom = both_columns(tr_q, lane, tiles, off, head_dim)
+            dp = dot(qkv[:, 2 * width + lane : 2 * width + lane + tiles * LANES], dom)
+            for q in range(2):
+                pairs[m, head_rows(2 * pair + q), :] = dp[:, q * atoms : (q + 1) * atoms]
+
+        def softmax_back(pair):
+            for q in range(2):
+                half = slice(q * atoms, (q + 1) * atoms)
+                p = probs[m, pair_rows(pair), half].astype(F32)
+                pd = p * pairs[m, head_rows(2 * pair + q), :]
                 ds = pd - p * jnp.sum(pd, axis=0, keepdims=True)
-                pairs[m, head_rows(g, head), :] = ds
-                ds_s[head // 2, :, half] = ds.astype(BF16)
+                pairs[m, head_rows(2 * pair + q), :] = ds
+                ds_s[pair, :, half] = ds.astype(BF16)
+
+        def products(pair):
+            first = pair * 2 * head_dim
+            got = dot(tr_b[first : first + 2 * head_dim, :], ds_s[pair])
+            tr_f[first : first + head_dim, :] = got[:head_dim, :atoms]
+            tr_f[first + head_dim : first + 2 * head_dim, :] = got[head_dim:, atoms:]
             for tile in range(16 * head_dim // LANES):
-                lane = pl.multiple_of(base + tile * LANES, LANES)
                 inside = tile_pairs(tile, windows)
-                left = jnp.concatenate([probs[m, pair_rows(g, pair), :] for pair, _ in inside], axis=1)
-                block = dqkv[:, pl.ds(lane, LANES)]
-                right = jnp.concatenate([both_heads(block, off, head_dim) for _, off in inside], axis=0)
-                dqkv[:, pl.ds(2 * width + lane, LANES)] = dot(left, right).astype(BF16)
-                left = jnp.concatenate([ds_s[pair] for pair, _ in inside], axis=1)
-                block = qkv[:, pl.ds(lane, LANES)]
-                right = jnp.concatenate([both_heads(block, off, head_dim) for _, off in inside], axis=0)
-                dqkv[:, pl.ds(width + lane, LANES)] = (dot(left, right) * scale).astype(BF16)
-            for pair in range(8):
-                first = pl.multiple_of(base + pair * 2 * head_dim, 16)
-                got = dot(tr_b[pl.ds(first, 2 * head_dim), :], ds_s[pair])
-                tr_f[pl.ds(first, head_dim), :] = got[:head_dim, :atoms]
-                tr_f[pl.ds(pl.multiple_of(first + head_dim, 8), head_dim), :] = got[head_dim:, atoms:]
+                if inside[-1][0] != pair % 8:
+                    continue
+                lane = pair // 8 * 16 * head_dim + tile * LANES
+                these = [(pair // 8 * 8 + one, off) for one, off in inside]
+                left = jnp.concatenate([probs[m, pair_rows(one), :] for one, _ in these], axis=1)
+                block = dqkv[:, lane : lane + LANES]
+                right = jnp.concatenate([both_heads(block, off, head_dim) for _, off in these], axis=0)
+                dqkv[:, 2 * width + lane : 2 * width + lane + LANES] = dot(left, right).astype(BF16)
+                left = jnp.concatenate([ds_s[one] for one, _ in these], axis=1)
+                block = qkv[:, lane : lane + LANES]
+                right = jnp.concatenate([both_heads(block, off, head_dim) for _, off in these], axis=0)
+                dqkv[:, width + lane : width + lane + LANES] = (dot(left, right) * scale).astype(BF16)
+
+        in_turn((slopes, softmax_back, products), heads // 2, BACKWARD_UNIT)
 
         dqkv[:, 0:width] = (jnp.transpose(tr_f[...]) * scale).astype(BF16)
-        da = dot_nt(dqkv[...], win[...])
+        da = sum(dot(dqkv[:, q * width : (q + 1) * width], turned(3 + q)) for q in range(3))
         xh, inv_std = norm_parts(rows_of(xs, m, atoms)[...].astype(F32))
         g_norm[0:1, :] += jnp.sum(da * xh, axis=0, keepdims=True)
         g_norm[2:3, :] += jnp.sum(da, axis=0, keepdims=True)
@@ -419,11 +483,9 @@
     def norm_copy():
         return to(s, 2 * z + 1 - c, g_norm, norm_core, nc_sem.at[0], nc_sem.at[1])
 
-    def weight_grads():
-        if chips:
-            norm_copy().start()
+    def weight_grads(lo, hi):
         jobs = [(act_s, df_s, 0), (c_s, du_s, 0), (o_s, dat_s, 0)] + [(a_s, dqkv_s, q) for q in range(3)]
-        for n, (left, right, col) in enumerate(jobs):
+        for n, (left, right, col) in list(enumerate(jobs))[lo:hi]:
             if col == 0:
                 for m in range(micro):
                     part = left[m * atoms : (m + 1) * atoms, :].astype(F32)
@@ -440,8 +502,6 @@
                 core_copy(n).start()
                 if n:
                     settle(n - 1)
-        if chips:
-            settle(parts - 1)
 
     def norm_window(dp):
         first = jnp.minimum(dp * share // LANES, width // LANES - 2)
@@ -598,17 +658,21 @@
         def _():
             make_bias(unit)
 
+        @pl.when(is_fwd & (m_fwd == 0))
+        def _():
+            for k in range(len(loads) - 1):
+                load(k).wait()
+
+            @pl.when(s == 0)
+            def _():
+                load_tokens().wait()
+
+        @pl.when(jnp.where(s >= 2, is_fwd & (m_fwd == 0), is_back & (m_back == 0)))
+        def _():
+            turn_weights()
+
         @pl.when(is_fwd)
         def _():
-            @pl.when(m_fwd == 0)
-            def _():
-                for k in range(len(loads) - 1):
-                    load(k).wait()
-
-                @pl.when(s == 0)
-                def _():
-                    load_tokens().wait()
-
             if sections > 1:
                 @pl.when(s > 0)
                 def _():
@@ -631,13 +695,27 @@
                 def _():
                     backward_copy(m_back).wait_recv()
 
-            backward(m_back)
+            backward_ffn(m_back)
+
+            @pl.when((s == 0) & (m_back == micro - 1))
+            def _():
+                weight_grads(0, 3)
+
+            backward_attn(m_back)
             if sections > 1:
                 @pl.when(s > 0)
                 def _():
                     backward_copy(m_back).start()
 
-    weight_grads()
+    @pl.when(s != 0)
+    def _():
+        weight_grads(0, 3)
+
+    if chips:
+        norm_copy().start()
+    weight_grads(3, parts)
+    if chips:
+        settle(parts - 1)
     if chips:
         reduce_all()
     else:
@@ -687,7 +765,7 @@
         low(rows, width), low(rows, width), low(rows, 3 * width),
         wide(micro, 2 * all_pairs, atoms), low(micro, all_pairs, 2 * atoms),
         wide(micro, atoms, atoms), wide(micro, atoms, atoms), wide(micro, atoms, atoms),
-        low(width, atoms), wide(width, atoms), low(8, atoms, 2 * atoms), low(width, rows),
+        low(width, atoms), wide(width, atoms), wide(width, atoms), low(SLOTS, DEPTH, 2 * atoms), low(heads // 2, atoms, 2 * atoms), low(width, rows),
         low(rows, width), low(*win.shape), low(*wout.shape), low(*wup.shape), low(*wdown.shape),
         wide(4, width), wide(heads, DEPTH), low(heads, DEPTH), sems(6),
     ] + [sems(micro)] * 4

time: 179 us -> 163 us (0.911)
  Pallas kernels: 178 us -> 161 us
    pallas_call x1, Pallas kernels: 174 us -> 158 us  [layer_call(): pl.pallas_call(functools.partial(body, sections, chips, micro, atoms, hea...]
where the time goes in v6:
time: 163 us
  Pallas kernels  161 us (99%)
    pallas_call x1, Pallas kernels, layer_call(): pl.pallas_call(functools.partial(body, sections, chips, micro, atoms, hea...  158 us
    pallas_call x1, Pallas kernels, finish(): pl.pallas_call(functools.partial(finish_body, width, kern, spd, edges, se...  3.94 us

profile of v6, /device:TPU:0, one launch (start us, length us, event | category | flops | bytes accessed | tf_op | source)
XLA Modules:
  0.0 162.9 jit_solution(15929587035312270617)
XLA Ops:
  0.7 0.7 pad_add_fusion.place
  1.3 157.5 %sections.1 = (bf16[512,768]{1,0:T(8,128)(2,1)}, bf16[512,768]{1,0:T(8,128)(2,1)}, f32[96,4608]{1,0:T(8,128)}, f32[8,256]{1,0:T(8,128)}, f32[32,256]{1,0:T(8,128)}) custom-call(s32[4]{0:T(128)} %group.1, s32[2]{0:T(128)} %counts.1, f32[3,4,128]{2,1,0:T(4,128)} %bitcast.35, s32[2,128,128]{2,1,0:T(8,128)} %path_in.1, s32[2,128,128]{2,1,0:T(8,128)} %edge_in.1, ...), custom_call_target="tpu_custom_call" | custom-call | tf_op jit(solution)/shard_map/sections/pallas_call | solution.py:784
  158.8 3.9 %finish.1 = (bf16[512,768]{1,0:T(8,128)(2,1)}, bf16[512,768]{1,0:T(8,128)(2,1)}, f32[96,2304]{1,0:T(8,128)}, f32[96,768]{1,0:T(8,128)}, f32[96,768]{1,0:T(8,128)...) custom-call(s32[2]{0:T(128)} %pad_add_fusion.place, ...), custom_call_target="tpu_custom_call" | custom-call | tf_op jit(solution)/shard_map/finish/pallas_call | solution.py:833

commit v7 on v6

--- a/solution.py
+++ b/solution.py
@@ -139,7 +139,7 @@
         (grads, g_norm, g_tab, *refs) = refs
     (
         xs, grecv, a_s, qkv_s, o_s, mid_s, c_s, u_s, act_s, df_s, du_s, dat_s, dqkv_s,
-        pairs, probs, dist_s, path_s, edge_s, tr_b, tr_f, tr_q, feats_s, ds_s, left_s,
+        pairs, probs, dist_s, path_s, edge_s, tr_b, tr_f, tr_q, feats_s, ds_s,
         cot, win, wout, wup, wdown, norms, tab_f, tab, load_sem, fsend, frecv, bsend, brecv, *refs,
     ) = refs
     if chips:
@@ -147,6 +147,7 @@
             core_in, line_in, norm_core, norm_sum, norm_in, tab_own, tab_core, tab_sum, tab_sec, tab_line,
             core_send, core_recv, line_send, line_recv, back_send, back_recv,
             nc_sem, nz_send, nz_recv, tc_sem, ts_send, ts_recv, tz_send, tz_recv,
+            guest_in, guest_line, guest_low, gl_send, gl_recv, gb_send, gb_recv, guest_sem,
         ) = refs
     width = wout.shape[0]
     head_dim = width // heads
@@ -402,11 +403,11 @@
                 pd = p * pairs[m, head_rows(2 * pair + q), :]
                 ds = pd - p * jnp.sum(pd, axis=0, keepdims=True)
                 pairs[m, head_rows(2 * pair + q), :] = ds
-                ds_s[pair, :, half] = ds.astype(BF16)
+                ds_s[pair_rows(pair), half] = ds.astype(BF16)
 
         def products(pair):
             first = pair * 2 * head_dim
-            got = dot(tr_b[first : first + 2 * head_dim, :], ds_s[pair])
+            got = dot(tr_b[first : first + 2 * head_dim, :], ds_s[pair_rows(pair), :])
             tr_f[first : first + head_dim, :] = got[:head_dim, :atoms]
             tr_f[first + head_dim : first + 2 * head_dim, :] = got[head_dim:, atoms:]
             for tile in range(16 * head_dim // LANES):
@@ -419,7 +420,7 @@
                 block = dqkv[:, lane : lane + LANES]
                 right = jnp.concatenate([both_heads(block, off, head_dim) for _, off in these], axis=0)
                 dqkv[:, 2 * width + lane : 2 * width + lane + LANES] = dot(left, right).astype(BF16)
-                left = jnp.concatenate([ds_s[one] for one, _ in these], axis=1)
+                left = jnp.concatenate([ds_s[pair_rows(one), :] for one, _ in these], axis=1)
                 block = qkv[:, lane : lane + LANES]
                 right = jnp.concatenate([both_heads(block, off, head_dim) for _, off in these], axis=0)
                 dqkv[:, width + lane : width + lane + LANES] = (dot(left, right) * scale).astype(BF16)
@@ -446,21 +447,109 @@
             core_send.at[n], core_recv.at[n],
         )
 
-    def right_copy(n, target):
+    class Line:
+        def __init__(self, ref_of, into, out, sems, cols, count):
+            self.ref_of, self.into, self.out, self.sems = ref_of, into, out, sems
+            self.cols, self.count, self.steps = cols, count, (chips - 1) * count
+
+        def right(self, n, target):
+            return to(
+                s, jnp.minimum(d + 2, 2 * chips - 1), self.ref_of(target).at[:, self.cols(n)],
+                self.into.at[target + 1, :, self.cols(n)], self.sems[0].at[n, target], self.sems[1].at[n, target],
+            )
+
+        def left(self, n, target):
+            return to(
+                s, jnp.maximum(d - 2, 0), self.ref_of(target).at[:, self.cols(n)],
+                self.into.at[target, :, self.cols(n)], self.sems[2].at[n, target], self.sems[3].at[n, target],
+            )
+
+        def end_copy(self, hop, n, act):
+            @pl.when(z == 0)
+            def _():
+                act(self.right(n, chips - 1 - hop))
+
+            @pl.when(z == chips - 1)
+            def _():
+                act(self.left(n, hop))
+
+        def add_in(self, target, slot, cols):
+            ref = self.ref_of(target)
+            ref[:, cols] = (ref[:, cols].astype(F32) + self.into[slot, :, cols].astype(F32)).astype(BF16)
+
+        def step(self, i):
+            at_right, at_left = i - LAG * (z - 1), i - LAG * (chips - 2 - z)
+            right, right_n = chips - 1 - at_right // self.count, at_right % self.count
+            left, left_n = at_left // self.count, at_left % self.count
+
+            @pl.when((z > 0) & (at_right >= 0) & (z <= right))
+            def _():
+                cols = self.cols(right_n)
+                self.right(right_n, right).wait_recv()
+
+                @pl.when(z < right)
+                def _():
+                    self.add_in(right, right + 1, cols)
+                    self.right(right_n, right).start()
+
+                @pl.when(z == right)
+                def _():
+                    self.out[:, cols] += self.into[right + 1, :, cols].astype(F32)
+
+            @pl.when((z < chips - 1) & (at_left >= 0) & (z >= left))
+            def _():
+                cols = self.cols(left_n)
+                self.left(left_n, left).wait_recv()
+
+                @pl.when(z > left)
+                def _():
+                    self.add_in(left, left, cols)
+                    self.left(left_n, left).start()
+
+                @pl.when(z == left)
+                def _():
+                    self.out[:, cols] += self.into[left, :, cols].astype(F32)
+
+            self.end_copy(i // self.count, i % self.count, lambda copy: copy.wait_send())
+
+            @pl.when(i + self.count < self.steps)
+            def _():
+                self.end_copy(i // self.count + 1, i % self.count, lambda copy: copy.start())
+
+        def drain(self, n):
+            for target in range(chips):
+                @pl.when((target > z) & (z > 0))
+                def _():
+                    self.right(n, target).wait_send()
+
+                @pl.when((target < z) & (z < chips - 1))
+                def _():
+                    self.left(n, target).wait_send()
+
+    donor, helper = s == 0, s == sections - 1
+    own_parts = jnp.where(donor, parts - 1, parts)
+    if chips:
+        main = Line(
+            lambda target: grads.at[target, c], line_in, sums, (line_send, line_recv, back_send, back_recv),
+            chunk, own_parts,
+        )
+
+        def part_cols(n):
+            return pl.ds(n * 2 * LANES if isinstance(n, int) else pl.multiple_of(n * 2 * LANES, LANES), 2 * LANES)
+
+        guest_sum = mid_s.at[0:share, :]
+        guest = Line(
+            lambda target: guest_in.at[target], guest_line, guest_sum, (gl_send, gl_recv, gb_send, gb_recv),
+            part_cols, width // (2 * LANES),
+        )
+
+    def guest_copy():
         return to(
-            s, jnp.minimum(d + 2, 2 * chips - 1), grads.at[target, c, :, chunk(n)],
-            line_in.at[target + 1, :, chunk(n)], line_send.at[n, target], line_recv.at[n, target],
+            sections - 1, d, grads.at[:, c, :, chunk(parts - 1)], guest_in, guest_sem.at[0], guest_sem.at[1]
         )
 
-    def left_copy(n, target):
-        return to(
-            s, jnp.maximum(d - 2, 0), grads.at[target, c, :, chunk(n)],
-            line_in.at[target, :, chunk(n)], back_send.at[n, target], back_recv.at[n, target],
-        )
-
-    def add_in(target, slot, cols):
-        both = grads[target, c, :, cols].astype(F32) + line_in[slot, :, cols].astype(F32)
-        grads[target, c, :, cols] = both.astype(BF16)
+    def result_copy():
+        return to(0, d, guest_low, guest_low, guest_sem.at[2], guest_sem.at[3])
 
     def settle(n):
         core_copy(n).wait_recv()
@@ -472,13 +561,16 @@
             def _():
                 sums[:, chunk(n)] = both
 
-        @pl.when(z == 0)
-        def _():
-            right_copy(n, chips - 1).start()
-
-        @pl.when(z == chips - 1)
-        def _():
-            left_copy(n, 0).start()
+        if n < parts - 1:
+            main.end_copy(0, n, lambda copy: copy.start())
+        else:
+            @pl.when(donor)
+            def _():
+                guest_copy().start()
+
+            @pl.when(jnp.logical_not(donor))
+            def _():
+                main.end_copy(0, n, lambda copy: copy.start())
 
     def norm_copy():
         return to(s, 2 * z + 1 - c, g_norm, norm_core, nc_sem.at[0], nc_sem.at[1])
@@ -489,12 +581,16 @@
             if col == 0:
                 for m in range(micro):
                     part = left[m * atoms : (m + 1) * atoms, :].astype(F32)
-                    left_s[:, m * atoms : (m + 1) * atoms] = jnp.transpose(part).astype(BF16)
+                    first = m // 2 * width
+                    ds_s[first : first + width, m % 2 * atoms : (m % 2 + 1) * atoms] = jnp.transpose(
+                        part
+                    ).astype(BF16)
 
             @pl.loop(0, width // 256)
             def _(q):
                 cols = pl.ds(pl.multiple_of(col * width + q * 256, 256), 256)
-                got = dot(left_s[...], right[:, cols]).astype(BF16)
+                turned_left = [ds_s[k * width : (k + 1) * width, :] for k in range(micro // 2)]
+                got = dot(jnp.concatenate(turned_left, axis=1), right[:, cols]).astype(BF16)
                 cols = pl.ds(pl.multiple_of(n * width + q * 256, 256), 256)
                 grads[:, :, :, cols] = got.reshape(grads.shape[:3] + (256,))
 
@@ -534,22 +630,16 @@
         norm_in[z] = norm_sum[:, norm_window(d)]
         others(z, chips, lambda o: norm_line(o, z).start())
 
-        steps = (chips - 1) * parts
-        tab_steps = steps - 6
+        tab_steps = (chips - 1) * (parts - 1) - 6
         tab_each = -(-tab_blocks // tab_steps)
 
-        def end_send(i, act):
-            hop, n = i // parts, i % parts
-
-            @pl.when(z == 0)
-            def _():
-                act(right_copy(n, chips - 1 - hop))
-
-            @pl.when(z == chips - 1)
-            def _():
-                act(left_copy(n, hop))
-
-        @pl.loop(0, steps)
+        def tab_over_chips():
+            others(s, sections, lambda o: tab_section(o, o).wait_recv())
+            tab_sum[1] = sum(tab_sec[o] for o in range(sections))
+            tab_line[z] = tab_sum[1]
+            others(z, chips, lambda o: tab_chip(o, z).start())
+
+        @pl.loop(0, main.steps)
         def _(i):
             @pl.when(i < tab_steps)
             def _():
@@ -570,50 +660,26 @@
                 tab_sec[s] = tab_sum[0]
                 others(s, sections, lambda o: tab_section(o, s).start())
 
-            @pl.when(i == tab_steps + 3)
-            def _():
-                others(s, sections, lambda o: tab_section(o, o).wait_recv())
-                tab_sum[1] = sum(tab_sec[o] for o in range(sections))
-                tab_line[z] = tab_sum[1]
-                others(z, chips, lambda o: tab_chip(o, z).start())
-
-            at_right, at_left = i - LAG * (z - 1), i - LAG * (chips - 2 - z)
-            right, right_n = chips - 1 - at_right // parts, at_right % parts
-            left, left_n = at_left // parts, at_left % parts
-
-            @pl.when((z > 0) & (at_right >= 0) & (z <= right))
-            def _():
-                cols = chunk(right_n)
-                right_copy(right_n, right).wait_recv()
-
-                @pl.when(z < right)
-                def _():
-                    add_in(right, right + 1, cols)
-                    right_copy(right_n, right).start()
-
-                @pl.when(z == right)
-                def _():
-                    sums[:, cols] += line_in[right + 1, :, cols].astype(F32)
-
-            @pl.when((z < chips - 1) & (at_left >= 0) & (z >= left))
-            def _():
-                cols = chunk(left_n)
-                left_copy(left_n, left).wait_recv()
-
-                @pl.when(z > left)
-                def _():
-                    add_in(left, left, cols)
-                    left_copy(left_n, left).start()
-
-                @pl.when(z == left)
-                def _():
-                    sums[:, cols] += line_in[left, :, cols].astype(F32)
-
-            end_send(i, lambda copy: copy.wait_send())
-
-            @pl.when(i + parts < steps)
-            def _():
-                end_send(i + parts, lambda copy: copy.start())
+            @pl.when((i == tab_steps + 3) & (s < 2))
+            def _():
+                tab_over_chips()
+
+            main.step(i)
+
+        @pl.when(helper)
+        def _():
+            guest_copy().wait_recv()
+            guest_sum[...] = guest_in[z].astype(F32)
+            for n in range(guest.count):
+                guest.end_copy(0, n, lambda copy: copy.start())
+
+            pl.loop(0, guest.steps)(guest.step)
+            guest_low[...] = guest_sum[...].astype(BF16)
+            result_copy().start()
+
+        @pl.when(s >= 2)
+        def _():
+            tab_over_chips()
 
         others(z, chips, lambda o: norm_line(o, o).wait_recv())
         s_norm[...] = sum(norm_in[o] for o in range(chips))
@@ -629,14 +695,21 @@
         @pl.loop(0, parts)
         def _(n):
             core_copy(n).wait_send()
-            for target in range(chips):
-                @pl.when((target > z) & (z > 0))
-                def _():
-                    right_copy(n, target).wait_send()
-
-                @pl.when((target < z) & (z < chips - 1))
-                def _():
-                    left_copy(n, target).wait_send()
+
+            @pl.when(n < own_parts)
+            def _():
+                main.drain(n)
+
+        @pl.when(helper)
+        def _():
+            pl.loop(0, guest.count)(guest.drain)
+            result_copy().wait_send()
+
+        @pl.when(donor)
+        def _():
+            guest_copy().wait_send()
+            result_copy().wait_recv()
+            sums[:, chunk(parts - 1)] = guest_low[...].astype(F32)
 
     total = 4 * micro
 
@@ -765,7 +838,7 @@
         low(rows, width), low(rows, width), low(rows, 3 * width),
         wide(micro, 2 * all_pairs, atoms), low(micro, all_pairs, 2 * atoms),
         wide(micro, atoms, atoms), wide(micro, atoms, atoms), wide(micro, atoms, atoms),
-        low(width, atoms), wide(width, atoms), wide(width, atoms), low(SLOTS, DEPTH, 2 * atoms), low(heads // 2, atoms, 2 * atoms), low(width, rows),
+        low(width, atoms), wide(width, atoms), wide(width, atoms), low(SLOTS, DEPTH, 2 * atoms), low(all_pairs, 2 * atoms),
         low(rows, width), low(*win.shape), low(*wout.shape), low(*wup.shape), low(*wdown.shape),
         wide(4, width), wide(heads, DEPTH), low(heads, DEPTH), sems(6),
     ] + [sems(micro)] * 4
@@ -777,6 +850,9 @@
             wide(sections, heads, DEPTH), wide(chips, heads, DEPTH),
             sems(parts), sems(parts), sems(parts, chips), sems(parts, chips), sems(parts, chips), sems(parts, chips),
             sems(2), sems(chips), sems(chips), sems(2), sems(sections), sems(sections), sems(chips), sems(chips),
+            low(chips, share, width), low(chips + 1, share, width), low(share, width),
+        ] + [sems(width // (2 * LANES), chips)] * 4 + [
+            sems(4),
         ]
     params = dict(vmem_limit_bytes=60 * 2**20, has_side_effects=True)
     if sections > 1:

time: 163 us -> 156 us (0.957); the launches traced: 163 us -> 154 us
  Pallas kernels: 161 us -> 153 us
    pallas_call x1, Pallas kernels: 158 us -> 149 us  [layer_call(): pl.pallas_call(functools.partial(body, sections, chips, micro, atoms, hea...]
where the time goes in v7:
time: 156 us; the launch traced here: 154 us
  Pallas kernels  153 us (98%)
    pallas_call x1, Pallas kernels, layer_call(): pl.pallas_call(functools.partial(body, sections, chips, micro, atoms, hea...  149 us
    pallas_call x1, Pallas kernels, finish(): pl.pallas_call(functools.partial(finish_body, width, kern, spd, edges, se...  3.94 us

profile of v7, /device:TPU:0, one launch (start us, length us, event | category | flops | bytes accessed | tf_op | source)
XLA Modules:
  0.0 154.0 jit_solution(2840435890281545131)
XLA Ops:
  0.7 0.7 pad_add_fusion.place
  1.3 148.6 %sections.1 = (bf16[512,768]{1,0:T(8,128)(2,1)}, bf16[512,768]{1,0:T(8,128)(2,1)}, f32[96,4608]{1,0:T(8,128)}, f32[8,256]{1,0:T(8,128)}, f32[32,256]{1,0:T(8,128)}) custom-call(s32[4]{0:T(128)} %group.1, s32[2]{0:T(128)} %counts.1, f32[3,4,128]{2,1,0:T(4,128)} %bitcast.35, s32[2,128,128]{2,1,0:T(8,128)} %path_in.1, s32[2,128,128]{2,1,0:T(8,128)} %edge_in.1, ...), custom_call_target="tpu_custom_call" | custom-call | tf_op jit(solution)/shard_map/sections/pallas_call | solution.py:860
  149.9 3.9 %finish.1 = (bf16[512,768]{1,0:T(8,128)(2,1)}, bf16[512,768]{1,0:T(8,128)(2,1)}, f32[96,2304]{1,0:T(8,128)}, f32[96,768]{1,0:T(8,128)}, f32[96,768]{1,0:T(8,128)...) custom-call(s32[2]{0:T(128)} %pad_add_fusion.place, ...), custom_call_target="tpu_custom_call" | custom-call | tf_op jit(solution)/shard_map/finish/pallas_call | solution.py:909

commit v8 on v7

--- a/solution.py
+++ b/solution.py
@@ -175,7 +175,6 @@
             pl.semaphore_signal(
                 barrier, inc=1, device_id=(s, (d + 2 * other) % (2 * chips)), device_id_type=MESH
             )
-        pl.semaphore_wait(barrier, sections + chips - 1)
     elif sections > 1:
         barrier = pltpu.get_barrier_semaphore()
 
@@ -186,8 +185,6 @@
         @pl.when(s < sections - 1)
         def _():
             pl.semaphore_signal(barrier, inc=1, device_id=(s + 1, d), device_id_type=MESH)
-
-        pl.semaphore_wait(barrier, jnp.where((s > 0) & (s < sections - 1), 2, 1))
 
     def forward_copy(m):
         return pltpu.make_async_remote_copy(
@@ -711,9 +708,15 @@
             result_copy().wait_recv()
             sums[:, chunk(parts - 1)] = guest_low[...].astype(F32)
 
+    pl.loop(0, 2)(make_bias)
+    if chips:
+        pl.semaphore_wait(barrier, sections + chips - 1)
+    elif sections > 1:
+        pl.semaphore_wait(barrier, jnp.where((s > 0) & (s < sections - 1), 2, 1))
+
     total = 4 * micro
 
-    @pl.loop(0, total)
+    @pl.loop(2, total)
     def _(t):
         ahead = jnp.where(last, micro, jnp.minimum(micro, jnp.where(s == 0, 1, 2 * s * s)))
         gap = micro - ahead
@@ -873,7 +876,7 @@
 
 def finish_body(
     width, kern, spd, edges, sections,
-    place, hidden, igrad, sums, norm, tab,
+    hidden, igrad, sums, norm, tab,
     hidden_o, igrad_o, in_o, out_o, up_o, down_o, gain_o, shift_o, kern_o, path_o, edge_o, tab_s, norm_s,
 ):
     hidden_o[...] = hidden[...]
@@ -882,8 +885,10 @@
         ref[...] = sums[:, k * width : (k + 1) * width]
     in_o[...] = sums[:, 3 * width :]
     share = gain_o.shape[1]
+    section, first = lax.axis_index("section"), lax.axis_index("dp") * share
+    first = first - jnp.minimum(first // LANES, width // LANES - 2) * LANES
     norm_s[...] = jnp.transpose(norm[...])
-    rows = norm_s[pl.ds(pl.multiple_of(place[1], 8), share), :]
+    rows = norm_s[pl.ds(pl.multiple_of(first, 8), share), :]
     rows = jnp.transpose(jnp.concatenate([rows, jnp.zeros((share, LANES - 8), F32)], axis=1))
     gain_o[...] = rows[0:2, :]
     shift_o[...] = rows[2:4, :]
@@ -891,15 +896,15 @@
     start = 0
     for count, ref in ((kern, kern_o), (spd, path_o), (edges, edge_o)):
         own = count // sections
-        ref[...] = tab_s[pl.ds(pl.multiple_of(start + place[0] * own, 8), own), :]
+        ref[...] = tab_s[pl.ds(pl.multiple_of(start + section * own, 8), own), :]
         start += count
 
 
-def finish(hidden, igrad, sums, norm, tab, place, kern, spd, edges, sections):
+def finish(hidden, igrad, sums, norm, tab, kern, spd, edges, sections):
     width, heads = hidden.shape[1], tab.shape[0]
     share = sums.shape[0]
     shape = jax.ShapeDtypeStruct
-    vmem, smem = pl.BlockSpec(memory_space=pltpu.VMEM), pl.BlockSpec(memory_space=pltpu.SMEM)
+    vmem = pl.BlockSpec(memory_space=pltpu.VMEM)
     outs = (
         [shape(hidden.shape, BF16), shape(igrad.shape, BF16), shape((share, sums.shape[1] - 3 * width), F32)]
         + [shape((share, width), F32)] * 3
@@ -909,12 +914,12 @@
     return pl.pallas_call(
         functools.partial(finish_body, width, kern, spd, edges, sections),
         out_shape=outs,
-        in_specs=[smem] + [vmem] * 5,
+        in_specs=[vmem] * 5,
         out_specs=[vmem] * len(outs),
         scratch_shapes=[pltpu.VMEM((DEPTH, heads), F32), pltpu.VMEM((2 * LANES, 8), F32)],
         compiler_params=pltpu.CompilerParams(vmem_limit_bytes=60 * 2**20),
         name="finish",
-    )(place, hidden, igrad, sums, norm, tab)
+    )(hidden, igrad, sums, norm, tab)
 
 
 def on_device(
@@ -934,9 +939,7 @@
         kernel_proj, path_table, edge_table,
     )
     if chips:
-        first = jnp.minimum(place * share // LANES, width // LANES - 2) * LANES
-        where = jnp.stack([section, place * share - first]).astype(jnp.int32)
-        outs = finish(hidden, igrad, *sums, where, kern, spd, edges, sections)
+        outs = finish(hidden, igrad, *sums, kern, spd, edges, sections)
         norms = [jnp.transpose(o) for o in outs[6:8]]
         return tuple(o[None] for o in [*outs[:6], *norms]) + tuple(outs[8:])
     grads, g_norm, g_tab = sums

time: 156 us -> 153 us (0.981)
  Pallas kernels: 153 us -> 151 us
    pallas_call x1, Pallas kernels: 149 us -> 147 us  [layer_call(): pl.pallas_call(functools.partial(body, sections, chips, micro, atoms, hea...]
where the time goes in v8:
time: 153 us; the launch traced here: 151 us
  Pallas kernels  151 us (99%)
    pallas_call x1, Pallas kernels, layer_call(): pl.pallas_call(functools.partial(body, sections, chips, micro, atoms, hea...  147 us
    pallas_call x1, Pallas kernels, finish(): pl.pallas_call(functools.partial(finish_body, width, kern, spd, edges, se...  3.93 us

profile of v8, /device:TPU:0, one launch (start us, length us, event | category | flops | bytes accessed | tf_op | source)
XLA Modules:
  0.0 151.4 jit_solution(9226756932136951651)
XLA Ops:
  0.7 146.7 %sections.1 = (bf16[512,768]{1,0:T(8,128)(2,1)}, bf16[512,768]{1,0:T(8,128)(2,1)}, f32[96,4608]{1,0:T(8,128)}, f32[8,256]{1,0:T(8,128)}, f32[32,256]{1,0:T(8,128)}) custom-call(s32[4]{0:T(128)} %group.1, s32[2]{0:T(128)} %counts.1, f32[3,4,128]{2,1,0:T(4,128)} %bitcast.33, s32[2,128,128]{2,1,0:T(8,128)} %path_in.1, s32[2,128,128]{2,1,0:T(8,128)} %edge_in.1, ...), custom_call_target="tpu_custom_call" | custom-call | tf_op jit(solution)/shard_map/sections/pallas_call | solution.py:863
  147.4 3.9 %finish.1 = (bf16[512,768]{1,0:T(8,128)(2,1)}, bf16[512,768]{1,0:T(8,128)(2,1)}, f32[96,2304]{1,0:T(8,128)}, f32[96,768]{1,0:T(8,128)}, f32[96,768]{1,0:T(8,128)...) custom-call(bf16[512,768]{1,0:T(8,128)(2,1)} %get-tuple-element.27.h, ...), custom_call_target="tpu_custom_call" | custom-call | tf_op jit(solution)/shard_map/finish/pallas_call | solution.py:914

commit v9 on v8

--- a/solution.py
+++ b/solution.py
@@ -18,8 +18,9 @@
 LANES = 128
 DEPTH = 256
 LAG = 3
+STRIPS = 2
 FORWARD_UNIT = 4
-BACKWARD_UNIT = 4
+BACKWARD_UNIT = 2
 BIAS_UNIT = 2
 BLOCK = 64
 TABLE_BLOCK = 16
@@ -884,27 +885,30 @@
     for k, ref in enumerate((down_o, up_o, out_o)):
         ref[...] = sums[:, k * width : (k + 1) * width]
     in_o[...] = sums[:, 3 * width :]
-    share = gain_o.shape[1]
-    section, first = lax.axis_index("section"), lax.axis_index("dp") * share
-    first = first - jnp.minimum(first // LANES, width // LANES - 2) * LANES
-    norm_s[...] = jnp.transpose(norm[...])
-    rows = norm_s[pl.ds(pl.multiple_of(first, 8), share), :]
-    rows = jnp.transpose(jnp.concatenate([rows, jnp.zeros((share, LANES - 8), F32)], axis=1))
-    gain_o[...] = rows[0:2, :]
-    shift_o[...] = rows[2:4, :]
-    tab_s[...] = jnp.transpose(tab[...])
-    start = 0
-    for count, ref in ((kern, kern_o), (spd, path_o), (edges, edge_o)):
-        own = count // sections
-        ref[...] = tab_s[pl.ds(pl.multiple_of(start + section * own, 8), own), :]
-        start += count
+    @pl.when(pl.program_id(0) == 0)
+    def _():
+        share = gain_o.shape[1]
+        section, first = lax.axis_index("section"), lax.axis_index("dp") * share
+        first = first - jnp.minimum(first // LANES, width // LANES - 2) * LANES
+        norm_s[...] = jnp.transpose(norm[...])
+        rows = norm_s[pl.ds(pl.multiple_of(first, 8), share), :]
+        rows = jnp.transpose(jnp.concatenate([rows, jnp.zeros((share, LANES - 8), F32)], axis=1))
+        gain_o[...] = rows[0:2, :]
+        shift_o[...] = rows[2:4, :]
+        tab_s[...] = jnp.transpose(tab[...])
+        start = 0
+        for count, ref in ((kern, kern_o), (spd, path_o), (edges, edge_o)):
+            own = count // sections
+            ref[...] = tab_s[pl.ds(pl.multiple_of(start + section * own, 8), own), :]
+            start += count
 
 
 def finish(hidden, igrad, sums, norm, tab, kern, spd, edges, sections):
     width, heads = hidden.shape[1], tab.shape[0]
     share = sums.shape[0]
     shape = jax.ShapeDtypeStruct
-    vmem = pl.BlockSpec(memory_space=pltpu.VMEM)
+    strip = lambda a: pl.BlockSpec((a.shape[0] // STRIPS, a.shape[1]), lambda i: (i, 0))
+    whole = lambda a: pl.BlockSpec(a.shape, lambda i: (0, 0))
     outs = (
         [shape(hidden.shape, BF16), shape(igrad.shape, BF16), shape((share, sums.shape[1] - 3 * width), F32)]
         + [shape((share, width), F32)] * 3
@@ -914,8 +918,9 @@
     return pl.pallas_call(
         functools.partial(finish_body, width, kern, spd, edges, sections),
         out_shape=outs,
-        in_specs=[vmem] * 5,
-        out_specs=[vmem] * len(outs),
+        grid=(STRIPS,),
+        in_specs=[strip(a) for a in (hidden, igrad, sums)] + [whole(a) for a in (norm, tab)],
+        out_specs=[strip(a) for a in outs[:6]] + [whole(a) for a in outs[6:]],
         scratch_shapes=[pltpu.VMEM((DEPTH, heads), F32), pltpu.VMEM((2 * LANES, 8), F32)],
         compiler_params=pltpu.CompilerParams(vmem_limit_bytes=60 * 2**20),
         name="finish",

time: 153 us -> 153 us (level)
  no operation moved by 1% of the time
where the time goes in v9:
time: 153 us; the launch traced here: 151 us
  Pallas kernels  150 us (98%)
    pallas_call x1, Pallas kernels, layer_call(): pl.pallas_call(functools.partial(body, sections, chips, micro, atoms, hea...  146 us
    pallas_call x1, Pallas kernels, finish(): pl.pallas_call(functools.partial(finish_body, width, kern, spd, edges, se...  3.56 us

profile of v9, /device:TPU:0, one launch (start us, length us, event | category | flops | bytes accessed | tf_op | source)
XLA Modules:
  0.0 150.8 jit_solution(16606551072298669587)
XLA Ops:
  0.7 146.4 %sections.1 = (bf16[512,768]{1,0:T(8,128)(2,1)}, bf16[512,768]{1,0:T(8,128)(2,1)}, f32[96,4608]{1,0:T(8,128)}, f32[8,256]{1,0:T(8,128)}, f32[32,256]{1,0:T(8,128)}) custom-call(s32[4]{0:T(128)} %group.1, s32[2]{0:T(128)} %counts.1, f32[3,4,128]{2,1,0:T(4,128)} %bitcast.33, s32[2,128,128]{2,1,0:T(8,128)} %path_in.1, s32[2,128,128]{2,1,0:T(8,128)} %edge_in.1, ...), custom_call_target="tpu_custom_call" | custom-call | tf_op jit(solution)/shard_map/sections/pallas_call | solution.py:864
  147.1 3.6 %finish.1 = (bf16[512,768]{1,0:T(8,128)(2,1)}, bf16[512,768]{1,0:T(8,128)(2,1)}, f32[96,2304]{1,0:T(8,128)}, f32[96,768]{1,0:T(8,128)}, f32[96,768]{1,0:T(8,128)...) custom-call(bf16[512,768]{1,0:T(8,128)(2,1)} %get-tuple-element.27.h, ...), custom_call_target="tpu_custom_call" | custom-call | tf_op jit(solution)/shard_map/finish/pallas_call | solution.py:918
